TPU v7x, 32 devices: a whole 2x2x4 slice. The times are simulated.
32 devices in a mesh: ctx: 16 (over z, y, x), tp: 2 (over core).
Axes of the slice: x: 2, y: 2, z: 4, core: 2. Of those that a mesh axis runs over, the one named last changes fastest.
Arguments:
- projected: bfloat16 [4096, 3, 4096], P('ctx', None, 'tp'), may hold values from -6 to 6
- short_filter: float32 [3, 3, 4096], P(None, None, 'tp'), may hold values from -3 to 3
- residues: float32 [4096, 16], P('tp'), may hold values from -3 to 3
- rates: float32 [4096, 16], P('tp'), may hold values from 1.2207031e-06 to 0.05
- skip_gain: float32 [4096], P('tp'), may hold values from -3 to 3
- out_weight: bfloat16 [4096, 4096], P('tp', 'ctx'), may hold values from -0.09375 to 0.09375
Outputs:
- mixed: bfloat16 [4096, 4096], P('ctx', 'tp')
All inputs are finite; a program needn't handle non-finite values.
Results may differ from a plain program's by a relative error of at most 0.019.
Values may be sent and summed in bfloat16 or wider, within the bound.
No kernel may reach another device: no remote copies, remote signals or barrier semaphores. Data moves between devices by JAX's collectives and lax.ppermute only.
A program may use at most 128 MiB of HBM per device.

v0:
```python
import functools

import jax
import jax.numpy as jnp
from jax import lax
from jax.experimental import pallas as pl
from jax.experimental.pallas import tpu as pltpu
from jax.sharding import PartitionSpec as P

LANES = 128
SEGS = 8
TOP = 8
SPOT, MIDDLE, KEEPS, ODD = range(4)
VMEM_LIMIT = 16 * 1024 * 1024
SMALL_LIMIT = 4 * 1024 * 1024
WHOLE_LIMIT = 50 * 1024 * 1024


def split_of(count):
    inner = 1
    while (2 * inner) ** 2 <= count and count % (2 * inner) == 0:
        inner *= 2
    return inner


def send_xor(value, count, group, step):
    pairs = [(p, p - p % group + ((p % group) ^ step)) for p in range(count)]
    return lax.ppermute(value, "ctx", pairs)


def send_along(value, count, group, steps, first=0):
    outer = count // group
    pairs = []
    for z in range(outer):
        if not 0 <= z + steps < outer:
            continue
        if (steps > 0 and z < first) or (steps < 0 and z > outer - 1 - first):
            continue
        pairs += [(z * group + e, (z + steps) * group + e) for e in range(group)]
    return lax.ppermute(value, "ctx", pairs)


def estimate(flops, bytes_accessed, transcendentals=0):
    return pl.CostEstimate(flops=flops, bytes_accessed=bytes_accessed, transcendentals=transcendentals)


def row(ref, r, lanes):
    return jnp.broadcast_to(ref[r : r + 1, lanes], (SEGS, LANES))


def lay_segments(dst, stream, halo, seg_len, lanes, group):
    pitch = seg_len + 1
    for s in range(SEGS):
        part = stream[0, s * seg_len : (s + 1) * seg_len, lanes].astype(jnp.float32)
        dst[group, TOP + s * pitch : TOP + s * pitch + seg_len, :] = part
    dst[group, TOP - 3 : TOP - 1, :] = jnp.zeros((2, LANES), jnp.float32) if halo is None else halo


def taps(short, stream, lanes):
    return [jnp.broadcast_to(short[i, stream : stream + 1, lanes], (SEGS, LANES)) for i in range(3)]


def strided(ref, group, start, pitch):
    return ref[group, pl.ds(start, SEGS, stride=pitch), :]


LAST, FIRST = 6, 4


def first_gated(short, first, last):
    products = []
    for b, stream in enumerate((1, 2)):
        tap = [short[i, stream : stream + 1, :] for i in range(3)]
        now_0, now_1 = first[2 * b : 2 * b + 1], first[2 * b + 1 : 2 * b + 2]
        old_2, old_1 = last[2 * stream : 2 * stream + 1], last[2 * stream + 1 : 2 * stream + 2]
        products.append(
            (
                tap[0] * now_0 + tap[1] * old_1 + tap[2] * old_2,
                tap[0] * now_1 + tap[1] * now_0 + tap[2] * old_1,
            )
        )
    return products[0][0] * products[1][0], products[0][1] * products[1][1]


def end_share(short, rates, first, last, rows):
    gated_0, gated_1 = first_gated(short, first, last)
    return jnp.exp(rates * (1.0 - rows)) * gated_0 + jnp.exp(rates * (2.0 - rows)) * gated_1


def local_scan_body(place, streams, short_all, rates_all, *rest, seg_len, order, share):
    ends = rest[:share]
    gated, prefix = rest[share : share + 2]
    key_pos, value_pos, end_now, held, query_held, short_held, rates_held, held_sem, small_sem = rest[share + 2 :]
    now_at = pl.program_id(0)
    wide = end_now.shape[1]
    small = [
        pltpu.make_async_copy(short_all, short_held, small_sem.at[0]),
        pltpu.make_async_copy(rates_all, rates_held, small_sem.at[1]),
        pltpu.make_async_copy(
            streams.at[0, pl.ds(seg_len * SEGS - 16, 16), :], query_held, small_sem.at[2]
        ),
    ]

    def stream_copy(at):
        columns = pl.ds(at * wide, wide)
        return pltpu.make_async_copy(
            streams.at[pl.ds(1, 2), :, columns], held.at[:, :, columns], held_sem.at[at]
        )

    @pl.when(now_at == 0)
    def _():
        stream_copy(0).start()
        for copy in small:
            copy.start()
        for at in range(1, share):
            stream_copy(at).start()
        for copy in small:
            copy.wait()

    for at in range(share):

        @pl.when(now_at == at)
        def _(at=at):
            stream_copy(at).wait()

    columns = pl.ds(pl.multiple_of(now_at * wide, LANES), wide)
    key = held.at[pl.ds(0, 1), :, columns]
    value = held.at[pl.ds(1, 1), :, columns]
    short = short_held.at[:, :, columns]
    rates = rates_held.at[:, columns]
    pitch = seg_len + 1
    groups = gated.shape[0]
    segment = lax.broadcasted_iota(jnp.int32, (SEGS, LANES), 0)
    for group in range(groups):
        lanes = slice(group * LANES, (group + 1) * LANES)
        lay_segments(key_pos, key, None, seg_len, lanes, group)
        lay_segments(value_pos, value, None, seg_len, lanes, group)
    bottom = seg_len * SEGS - 2
    end_now[order : order + 2, :] = query_held[14:16, columns].astype(jnp.float32)
    for b, stream in enumerate((key, value)):
        at = order + 2 + 2 * b
        end_now[at : at + 2, :] = stream[0, bottom : bottom + 2, :].astype(jnp.float32)
        at = order + LAST + 2 * b
        end_now[at : at + 2, :] = stream[0, 0:2, :].astype(jnp.float32)

    for group in range(groups):
        lanes = slice(group * LANES, (group + 1) * LANES)
        key_taps = taps(short, 1, lanes)
        value_taps = taps(short, 2, lanes)
        decay = [jnp.exp(-row(rates, r, lanes)) for r in range(order)]

        def step(i, carry, early=False, group=group, key_taps=key_taps, value_taps=value_taps, decay=decay):
            k1, k2, v1, v2, *states = carry
            k0 = strided(key_pos, group, TOP + i, pitch)
            v0 = strided(value_pos, group, TOP + i, pitch)
            key_now = key_taps[0] * k0 + key_taps[1] * k1 + key_taps[2] * k2
            value_now = value_taps[0] * v0 + value_taps[1] * v1 + value_taps[2] * v2
            now = key_now * value_now
            if early:
                now = jnp.where(segment >= 1, now, 0.0)
            gated[group, pl.ds(pl.multiple_of(i * SEGS, SEGS), SEGS), :] = now
            states = [d * h + now for d, h in zip(decay, states)]
            return (k0, k1, v0, v1, *states)

        zero = jnp.zeros((SEGS, LANES), jnp.float32)
        start = (
            strided(key_pos, group, TOP - 2, pitch),
            strided(key_pos, group, TOP - 3, pitch),
            strided(value_pos, group, TOP - 2, pitch),
            strided(value_pos, group, TOP - 3, pitch),
        ) + (zero,) * order
        start = step(1, step(0, start, True), True)
        states = lax.fori_loop(2, seg_len, step, start, unroll=6)[4:]
        for r in range(order):
            rate = row(rates, r, lanes)
            scan = states[r]
            for d in (1, 2, 4):
                moved = jnp.where(segment >= d, pltpu.roll(scan, d, 0), 0.0)
                scan = scan + jnp.exp(rate * (-1.0 * d * seg_len)) * moved
            prefix[group, r] = jnp.where(segment >= 1, pltpu.roll(scan, 1, 0), 0.0)
            end_now[r : r + 1, lanes] = scan[SEGS - 1 :, :]

    for j in range(share):

        @pl.when((pl.program_id(0) ^ place[SPOT]) == j)
        def _(j=j):
            ends[j][...] = end_now[...]


def local_scan(place, streams, short, rates, share):
    _, rows, chans = streams.shape
    order = rates.shape[0]
    wide = chans // share
    groups = wide // LANES
    seg_len = rows // SEGS
    pos_rows = TOP + SEGS * (seg_len + 1)
    end_shape = jax.ShapeDtypeStruct((order + LAST + FIRST, wide), jnp.float32)
    return pl.pallas_call(
        functools.partial(local_scan_body, seg_len=seg_len, order=order, share=share),
        grid_spec=pltpu.PrefetchScalarGridSpec(
            num_scalar_prefetch=1,
            grid=(share,),
            in_specs=[
                pl.BlockSpec(memory_space=pltpu.HBM),
                pl.BlockSpec(memory_space=pltpu.HBM),
                pl.BlockSpec(memory_space=pltpu.HBM),
            ],
            out_specs=[pl.BlockSpec((order + LAST + FIRST, wide), lambda g, place: (0, 0))] * share
            + [
                pl.BlockSpec((groups, rows, LANES), lambda g, place: (g, 0, 0)),
                pl.BlockSpec((groups, order, SEGS, LANES), lambda g, place: (g, 0, 0, 0)),
            ],
            scratch_shapes=[
                pltpu.VMEM((groups, pos_rows, LANES), jnp.float32),
                pltpu.VMEM((groups, pos_rows, LANES), jnp.float32),
                pltpu.VMEM((order + LAST + FIRST, wide), jnp.float32),
                pltpu.VMEM((2, rows, chans), streams.dtype),
                pltpu.VMEM((16, chans), streams.dtype),
                pltpu.VMEM(short.shape, jnp.float32),
                pltpu.VMEM(rates.shape, jnp.float32),
                pltpu.SemaphoreType.DMA((share,)),
                pltpu.SemaphoreType.DMA((3,)),
            ],
        ),
        out_shape=[end_shape] * share
        + [
            jax.ShapeDtypeStruct((chans // LANES, rows, LANES), jnp.float32),
            jax.ShapeDtypeStruct((chans // LANES, order, SEGS, LANES), jnp.float32),
        ],
        compiler_params=pltpu.CompilerParams(vmem_limit_bytes=WHOLE_LIMIT),
        cost_estimate=estimate(rows * chans * 50, rows * chans * 10),
        name="local_scan",
    )(place, streams, short, rates)


def plane_scan_body(place, rates, short, *rest, share, rows):
    ends = rest[:share]
    whole = rest[share]
    befores = rest[share + 1 : 2 * share + 1]
    by_place, before_place = rest[2 * share + 1 :]
    order = rates.shape[0]
    here = place[SPOT]
    for j in range(share):
        by_place[here ^ j] = ends[j][...]
    rate = rates[...]
    decay = jnp.exp(rate * (-1.0 * rows))
    state = jnp.zeros(rate.shape, jnp.float32)
    for at in range(share):
        before_place[at, :order] = state
        state = decay * state + by_place[at, :order]
        if at > 0:
            last = by_place[at - 1, order : order + LAST]
            before_place[at, order:] = last
            state += end_share(short, rate, by_place[at, order + LAST :], last, rows)
    before_place[0, order:] = jnp.zeros((LAST, rate.shape[1]), jnp.float32)
    whole[:order] = state
    whole[order : order + LAST] = by_place[share - 1, order : order + LAST]
    whole[order + LAST :] = by_place[0, order + LAST :]
    for j in range(share):
        befores[j][...] = before_place[here ^ j]


def plane_scan(place, rates, short, ends, rows):
    share = len(ends)
    order = rates.shape[0]
    wide = ends[0].shape[1]
    block = pl.BlockSpec((order + LAST, wide), lambda g, place: (0, 0))
    edged = pl.BlockSpec((order + LAST + FIRST, wide), lambda g, place: (0, 0))
    shape = jax.ShapeDtypeStruct((order + LAST, wide), jnp.float32)
    got = pl.pallas_call(
        functools.partial(plane_scan_body, share=share, rows=rows),
        grid_spec=pltpu.PrefetchScalarGridSpec(
            num_scalar_prefetch=1,
            grid=(1,),
            in_specs=[
                pl.BlockSpec((order, wide), lambda g, place: (0, place[SPOT])),
                pl.BlockSpec((3, 3, wide), lambda g, place: (0, 0, place[SPOT])),
            ]
            + [edged] * share,
            out_specs=[edged] + [block] * share,
            scratch_shapes=[
                pltpu.VMEM((share, order + LAST + FIRST, wide), jnp.float32),
                pltpu.VMEM((share, order + LAST, wide), jnp.float32),
            ],
        ),
        out_shape=[jax.ShapeDtypeStruct((order + LAST + FIRST, wide), jnp.float32)] + [shape] * share,
        compiler_params=pltpu.CompilerParams(vmem_limit_bytes=SMALL_LIMIT),
        cost_estimate=estimate(order * wide * 20, order * wide * 36),
        name="plane_scan",
    )(place, rates, short, *ends)
    return got[0], got[1:]


def line_scan_body(place, rates, short, whole, *rest, share, rows, lines):
    befores = rest[:share]
    arrived = rest[share : share + lines]
    outs = rest[share + lines :]
    order = rates.shape[0]
    here = place[SPOT]
    rate = rates[...]
    planes = (whole,) + tuple(arrived)

    def last_rows(k):
        if k < lines:
            return planes[k + 1][order : order + LAST]
        return jnp.zeros((LAST, rate.shape[1]), jnp.float32)

    def first_share(k):
        return end_share(short, rate, planes[k][order + LAST :], last_rows(k), rows)

    state = jnp.zeros(rate.shape, jnp.float32)
    decay = jnp.exp(rate * (-1.0 * rows * share))
    later = jnp.exp(rate * (-1.0 * rows * (share - 1)))
    for k in reversed(range(1, lines + 1)):
        state = decay * state + planes[k][:order] + later * first_share(k)
    own = first_share(0)
    for j in range(share):
        at = (here ^ j).astype(jnp.float32)
        inside = jnp.minimum(at, 1.0)
        past = inside * jnp.exp(rate * (jnp.maximum(at - 1.0, 0.0) * (-1.0 * rows)))
        before = befores[j][:order]
        outs[j][:order] = before + jnp.exp(rate * (at * (-1.0 * rows))) * state + past * own
        outs[j][order:] = befores[j][order:] + (1.0 - inside) * last_rows(0)


def line_scan(place, rates, short, whole, befores, arrived, rows):
    share, lines = len(befores), len(arrived)
    order, wide = rates.shape[0], whole.shape[1]
    block = pl.BlockSpec((order + LAST, wide), lambda g, place: (0, 0))
    edged = pl.BlockSpec((order + LAST + FIRST, wide), lambda g, place: (0, 0))
    return pl.pallas_call(
        functools.partial(line_scan_body, share=share, rows=rows, lines=lines),
        grid_spec=pltpu.PrefetchScalarGridSpec(
            num_scalar_prefetch=1,
            grid=(1,),
            in_specs=[
                pl.BlockSpec((order, wide), lambda g, place: (0, place[SPOT])),
                pl.BlockSpec((3, 3, wide), lambda g, place: (0, 0, place[SPOT])),
                edged,
            ]
            + [block] * share
            + [edged] * lines,
            out_specs=[block] * share,
        ),
        out_shape=[jax.ShapeDtypeStruct((order + LAST, wide), jnp.float32)] * share,
        compiler_params=pltpu.CompilerParams(vmem_limit_bytes=SMALL_LIMIT),
        cost_estimate=estimate(order * wide * 20, order * wide * 36),
        name="line_scan",
    )(place, rates, short, whole, *befores, *arrived)


def hidden_body(place, query, top, short, rates, coef, skip, gated, prefix, *rest, seg_len, order, share, first):
    starts = rest[:share]
    hidden = rest[share]
    query_pos, result_pos, start_by_place = rest[share + 1 :]
    pitch = seg_len + 1
    groups = gated.shape[0]
    now_at = pl.program_id(0) + first
    segment = lax.broadcasted_iota(jnp.int32, (SEGS, LANES), 0).astype(jnp.float32)

    @pl.when(pl.program_id(0) == 0)
    def _():
        for j in range(share):
            start_by_place[place[SPOT] ^ j] = starts[j][...]

    for group in range(groups):
        lanes = slice(group * LANES, (group + 1) * LANES)
        ending = start_by_place[now_at, order : order + 2, lanes]
        lay_segments(query_pos, query, ending, seg_len, lanes, group)

    for group in range(groups):
        lanes = slice(group * LANES, (group + 1) * LANES)
        query_taps = taps(short, 0, lanes)
        gain = jnp.broadcast_to(skip[0:1, lanes], (SEGS, LANES))
        decay = [jnp.exp(-row(rates, r, lanes)) for r in range(order)]
        scale = [row(coef, r, lanes) for r in range(order)]
        first = jnp.concatenate([top[b, 0:2, lanes] for b in (1, 2)], axis=0).astype(jnp.float32)
        last = start_by_place[now_at, order:, lanes]
        early = [
            jnp.broadcast_to(value, (SEGS, LANES))
            for value in first_gated(short.at[:, :, lanes], first, last)
        ]
        states = []
        for r in range(order):
            rate = row(rates, r, lanes)
            ahead = jnp.exp(rate * (segment * (-1.0 * seg_len)))
            before = jnp.broadcast_to(start_by_place[now_at, r : r + 1, lanes], (SEGS, LANES))
            grown = jnp.exp(rate)
            before += jnp.where(segment >= 1.0, grown * (early[0] + grown * early[1]), 0.0)
            states.append(prefix[group, r] + ahead * before)

        def step(
            i, carry, late=None, group=group, query_taps=query_taps, gain=gain, decay=decay, scale=scale
        ):
            q1, q2, *states = carry
            q0 = strided(query_pos, group, TOP + i, pitch)
            now = gated[group, pl.ds(pl.multiple_of(i * SEGS, SEGS), SEGS), :]
            if late is not None:
                now = jnp.where(segment >= 1.0, now, late)
            states = [d * h + now for d, h in zip(decay, states)]
            sums = [s * h for s, h in zip(scale, states)] + [gain * now]
            while len(sums) > 1:
                sums = [a + b for a, b in zip(sums[::2], sums[1::2])] + sums[len(sums) // 2 * 2 :]
            query_now = query_taps[0] * q0 + query_taps[1] * q1 + query_taps[2] * q2
            result_pos[group, pl.ds(TOP + i, SEGS, stride=pitch), :] = query_now * sums[0]
            return (q0, q1, *states)

        start = (
            strided(query_pos, group, TOP - 2, pitch),
            strided(query_pos, group, TOP - 3, pitch),
        ) + tuple(states)
        start = step(1, step(0, start, early[0]), early[1])
        lax.fori_loop(2, seg_len, step, start, unroll=6)
        for s in range(SEGS):
            part = result_pos[group, TOP + s * pitch : TOP + s * pitch + seg_len, :]
            hidden[s * seg_len : (s + 1) * seg_len, lanes] = part.astype(hidden.dtype)


def hidden_rows(place, streams, short, rates, coef, skip, gated, prefix, starts, part):
    _, rows, chans = streams.shape
    order = rates.shape[0]
    share = len(starts)
    wide = chans // share
    groups = wide // LANES
    seg_len = rows // SEGS
    steps = max(1, share // 2)
    first = part * steps
    pos_rows = TOP + SEGS * (seg_len + 1)
    return pl.pallas_call(
        functools.partial(hidden_body, seg_len=seg_len, order=order, share=share, first=first),
        grid_spec=pltpu.PrefetchScalarGridSpec(
            num_scalar_prefetch=1,
            grid=(steps,),
            in_specs=[
                pl.BlockSpec((1, rows, wide), lambda g, place: (0, 0, first + g)),
                pl.BlockSpec((3, 16, wide), lambda g, place: (0, 0, first + g)),
                pl.BlockSpec((3, 3, wide), lambda g, place: (0, 0, first + g)),
                pl.BlockSpec((order, wide), lambda g, place: (0, first + g)),
                pl.BlockSpec((order, wide), lambda g, place: (0, first + g)),
                pl.BlockSpec((1, wide), lambda g, place: (0, first + g)),
                pl.BlockSpec((groups, rows, LANES), lambda g, place: (first + g, 0, 0)),
                pl.BlockSpec((groups, order, SEGS, LANES), lambda g, place: (first + g, 0, 0, 0)),
            ]
            + [pl.BlockSpec((order + LAST, wide), lambda g, place: (0, 0))] * share,
            out_specs=pl.BlockSpec((rows, wide), lambda g, place: (0, g)),
            scratch_shapes=[
                pltpu.VMEM((groups, pos_rows, LANES), jnp.float32),
                pltpu.VMEM((groups, pos_rows, LANES), jnp.float32),
                pltpu.VMEM((share, order + LAST, wide), jnp.float32),
            ],
        ),
        out_shape=jax.ShapeDtypeStruct((rows, steps * wide), jnp.bfloat16),
        compiler_params=pltpu.CompilerParams(vmem_limit_bytes=VMEM_LIMIT),
        cost_estimate=estimate(rows * chans * 40, rows * chans * 5),
        name="hidden_rows",
    )(place, streams, streams, short, rates, coef, skip, gated, prefix, *starts)


def times_into(rows, columns, out, column):
    width = columns.shape[1]
    top = 0
    for part in rows:
        total = 0.0
        start = 0
        for piece in part:
            size, depth = piece.shape
            total += jnp.dot(
                piece[...], columns[start : start + depth, :], preferred_element_type=jnp.float32
            )
            start += depth
        out[top : top + size, column : column + width] = total.astype(out.dtype)
        top += size


def operands(refs, rows_in, slots):
    at = 0
    rows, blocks = [], []
    for group, counts in ((rows, rows_in), (blocks, slots)):
        for count in counts:
            group.append(refs[at : at + count])
            at += count
    return rows, blocks


def near_body(place, *refs, rows_in, slots):
    near, far_first = refs[-2:]
    rows, blocks = operands(refs, rows_in, slots)
    width = far_first.shape[1]

    def all_blocks(middle):
        for slot, given in enumerate(blocks):
            out, column = (near, slot * width) if slot < 2 else (far_first, 0)
            times_into(rows, given[0 if middle else -1], out, column)

    for middle in (0, 1):
        pl.when(place[MIDDLE] == middle)(functools.partial(all_blocks, middle))


def project_body(place, *refs, rows_in, slots):
    near, far_first, kept, sent = refs[-4:]
    rows, blocks = operands(refs, rows_in, slots)
    made, width = far_first.shape

    def all_blocks(keeps, middle):
        outs = (kept, sent) if keeps else (sent, kept)
        outs[0][:made] = near[...]
        outs[1][:made, :width] = far_first[...]
        columns = [given[0 if middle else -1] for given in blocks]
        for slot, block in enumerate(columns):
            far, at = divmod(slot, 2)
            times_into(rows[-1:], block, outs[far].at[pl.ds(made, outs[far].shape[0] - made)], at * width)
        times_into(rows[:-1], columns[3], outs[1], width)

    for keeps in (0, 1):
        for middle in (0, 1):
            here = (place[KEEPS] == keeps) & (place[MIDDLE] == middle)
            pl.when(here)(functools.partial(all_blocks, keeps, middle))


def project(place, rows, slots, made=None):
    flat = [piece for part in rows for piece in part] + [block for slot in slots for block in slot]
    flat += [] if made is None else list(made)
    count = sum(part[0].shape[0] for part in rows)
    depth, width = slots[0][0].shape
    widths = (2 * width, width) if len(slots) == 3 else (2 * width, 2 * width)
    held = pl.BlockSpec(memory_space=pltpu.VMEM)
    return pl.pallas_call(
        functools.partial(
            near_body if len(slots) == 3 else project_body,
            rows_in=tuple(map(len, rows)),
            slots=tuple(map(len, slots)),
        ),
        in_specs=[pl.BlockSpec(memory_space=pltpu.SMEM)] + [held] * len(flat),
        out_specs=[held] * 2,
        out_shape=[jax.ShapeDtypeStruct((count, wide), jnp.bfloat16) for wide in widths],
        compiler_params=pltpu.CompilerParams(vmem_limit_bytes=VMEM_LIMIT),
        cost_estimate=estimate(
            2 * count * depth * len(slots) * width,
            2 * (count * depth + len(slots) * width * (depth + count)),
        ),
        name="project",
    )(place, *flat)


def assemble_body(place, *refs):
    parts, out = refs[:-1], refs[-1]
    width = parts[0].shape[1]
    for j, part in enumerate(parts):
        column = pl.multiple_of((place[SPOT] ^ j) * width, LANES)
        out[:, pl.ds(column, width)] = part[...]


def assemble(place, parts, blocks, width):
    share = len(parts)
    rows = parts[0].shape[0]
    return pl.pallas_call(
        assemble_body,
        grid_spec=pltpu.PrefetchScalarGridSpec(
            num_scalar_prefetch=1,
            grid=(blocks,),
            in_specs=[pl.BlockSpec((rows, width), lambda b, place: (0, b ^ place[ODD]))] * share,
            out_specs=pl.BlockSpec((rows, share * width), lambda b, place: (0, b)),
        ),
        out_shape=jax.ShapeDtypeStruct((rows, share * blocks * width), jnp.bfloat16),
        compiler_params=pltpu.CompilerParams(vmem_limit_bytes=VMEM_LIMIT),
        cost_estimate=estimate(0, 4 * rows * share * blocks * width),
        name="assemble",
    )(place, *parts)


def after(value, *others):
    return lax.optimization_barrier((value, *others))[0]


def send_planes(value, group, moves):
    pairs = [(a * group + e, b * group + e) for a, b in moves for e in range(group)]
    return lax.ppermute(value, "ctx", pairs)


def plane_rows(hidden, count, group):
    if group != 4:
        return [hidden] + [[send_xor(part, count, group, j) for part in hidden] for j in range(1, group)]
    first, second = hidden
    first_1 = send_xor(first, count, group, 1)
    first_2 = send_xor(first, count, group, 2)
    second_2 = send_xor(second, count, group, 2)
    second_1 = send_xor(second, count, group, 1)
    first_3 = send_xor(first_1, count, group, 2)
    second_3 = send_xor(second_2, count, group, 1)
    return [[first, second], [first_1, second_1], [first_2, second_2], [first_3, second_3]]


def add_up_body(a, b, *outs):
    size = outs[0].shape[0]
    for j, out in enumerate(outs):
        rows = slice(j * size, (j + 1) * size)
        out[...] = (a[rows].astype(jnp.float32) + b[rows].astype(jnp.float32)).astype(out.dtype)


def add_up(a, b, parts):
    size, width = a.shape[0] // parts, a.shape[1]
    held = pl.BlockSpec(memory_space=pltpu.VMEM)
    return pl.pallas_call(
        add_up_body,
        in_specs=[held, held],
        out_specs=[held] * parts,
        out_shape=[jax.ShapeDtypeStruct((size, width), a.dtype)] * parts,
        compiler_params=pltpu.CompilerParams(vmem_limit_bytes=VMEM_LIMIT),
        cost_estimate=estimate(parts * size * width, 6 * parts * size * width),
        name="add_up",
    )(a, b)


def project_4x4(place, out_weight, states, hidden, count):
    group = 4
    swap = [(0, 1), (1, 0), (2, 3), (3, 2)]
    inner = [(1, 2), (2, 1)]
    outward = [(1, 0), (2, 3)]
    rows = plane_rows(hidden, count, group)
    own = out_weight
    by_1 = send_planes(own, group, swap)
    by_3_inner = send_planes(own, group, inner)
    by_2_inner = send_planes(after(by_1, states, by_3_inner), group, inner)
    by_2_outer = send_planes(after(by_3_inner, states), group, outward)
    by_3_outer = send_planes(after(by_2_inner, by_2_outer, rows[1][0], rows[2][0], hidden[1]), group, outward)
    blocks = [[own], [by_1], [by_2_inner, by_2_outer], [by_3_inner, by_3_outer]]

    made = project(place, rows[:3], blocks[:3])
    kept, sent = project(place, rows, blocks, made)
    mixed = add_up(kept, lax.ppermute(sent, "tp", [(0, 1), (1, 0)]), group)
    mixed = [mixed[0]] + [send_xor(mixed[j], count, group, j) for j in range(1, group)]
    return assemble(place, mixed, 2, out_weight.shape[1])


def project_any(out_weight, states, hidden, count):
    halves = lax.axis_size("tp")
    group = split_of(count)
    outer = count // group
    plane = lax.axis_index("ctx") // group
    size = hidden[0].shape[0]
    depth, width = out_weight.shape
    below, above = [out_weight], [out_weight]
    for k in range(1, outer):
        down, up = below[-1], above[-1]
        if k == 2:
            down, up = after(down, states), after(up, states)
        below.append(send_along(down, count, group, 1, k - 1))
        above.append(send_along(up, count, group, -1, k - 1))
    line = below[:0:-1] + above
    cols = lax.dynamic_slice_in_dim(jnp.stack(line), outer - 1 - plane, outer, 0)
    cols = jnp.moveaxis(cols, 0, 1).reshape(depth, outer * width)
    rows = plane_rows(hidden, count, group)
    held = jnp.concatenate([jnp.concatenate(part, axis=1) for part in rows], axis=0)
    partial = jnp.dot(held, cols, preferred_element_type=jnp.float32).astype(jnp.bfloat16)
    mixed = lax.psum_scatter(partial, "tp", scatter_dimension=1, tiled=True)
    mixed = jnp.split(mixed, group)
    mixed = [mixed[0]] + [send_xor(mixed[j], count, group, j) for j in range(1, group)]
    blocks = outer // halves
    stacked = jnp.stack(mixed).reshape(group, size, blocks, width)
    by_place = jnp.take(stacked, jnp.arange(group) ^ (lax.axis_index("ctx") % group), axis=0)
    return jnp.moveaxis(by_place, 0, 2).reshape(size, blocks * group * width)


def per_device(projected, short_filter, residues, rates, skip_gain, out_weight):
    count = lax.axis_size("ctx")
    halves = lax.axis_size("tp")
    here = lax.axis_index("ctx")
    rows, _, chans = projected.shape

    streams = jnp.transpose(projected, (1, 0, 2))
    rates_t = rates.T
    coef_t = (residues * jnp.sqrt(-jnp.expm1(-2.0 * rates))).T

    share = min(split_of(count), chans // LANES, 4)
    lines = count // share
    plane = here // share
    keeps = lax.axis_index("tp") == plane // 2
    place = jnp.stack([here % share, (plane == 1) | (plane == 2), keeps, plane % 2]).astype(jnp.int32)
    *ends, gated, prefix = local_scan(place, streams, short_filter, rates_t, share)
    ends = [ends[0]] + [send_xor(ends[j], count, share, j) for j in range(1, share)]
    whole, befores = plane_scan(place, rates_t, short_filter, ends, rows)
    arrived = [send_along(whole, count, share, k) for k in range(1, lines)]
    starts = line_scan(place, rates_t, short_filter, whole, befores, arrived, rows)
    states = starts[0]
    starts = [starts[0]] + [send_xor(starts[j], count, share, j) for j in range(1, share)]
    hidden = [
        hidden_rows(
            place, streams, short_filter, rates_t, coef_t, skip_gain[None], gated, prefix, starts, part
        )
        for part in range(2)
    ]
    if count == 16 and halves == 2 and out_weight.shape[1] % LANES == 0:
        return project_4x4(place, out_weight, states, hidden, count)
    return project_any(out_weight, states, hidden, count)


def solution(mesh):
    return jax.shard_map(
        per_device,
        mesh=mesh,
        in_specs=(
            P("ctx", None, "tp"),
            P(None, None, "tp"),
            P("tp", None),
            P("tp", None),
            P("tp"),
            P("tp", "ctx"),
        ),
        out_specs=P("ctx", "tp"),
        check_vma=False,
    )
```

profile of v0, /device:TPU:0, one launch (start us, length us, event | category | flops | bytes accessed | tf_op | source)
XLA Modules:
  0.0 109.7 jit_solution(9727257576092299342)
XLA Ops:
  0.0 1.8 %collective-permute-start.16 = (bf16[2048,256]{1,0:T(8,128)(2,1)}, bf16[2048,256]{1,0:T(8,128)(2,1)}, u32[]{:S(2)}, u32[]{:S(2)}) collective-permute-start(bf16[2048,256]{1,0:T(8,128)(2,1)} %refs_8_.1), channel_id=1, source_target_pairs={{8,16},{10,18},{12,20},{14,22},{16,8},{18,10},{20,12},{22,14},{9,1... | collective-permute-start | bytes 3145736 | tf_op jit(solution)/shard_map/ppermute | solution.py:577
  1.8 5.1 %collective-permute-start.15 = (bf16[2048,256]{1,0:T(8,128)(2,1)}, bf16[2048,256]{1,0:T(8,128)(2,1)}, u32[]{:S(2)}, u32[]{:S(2)}) collective-permute-start(bf16[2048,256]{1,0:T(8,128)(2,1)} %refs_8_.1), channel_id=1, source_target_pairs={{0,8},{2,10},{4,12},{6,14},{8,0},{10,2},{12,4},{14,6},{16,24},{18,... | collective-permute-start | bytes 3145736 | tf_op jit(solution)/shard_map/ppermute | solution.py:577
  8.7 6.9 %local_scan.1 = (f32[26,512]{1,0:T(8,128)S(1)}, f32[26,512]{1,0:T(8,128)S(1)}, f32[26,512]{1,0:T(8,128)S(1)}, f32[26,512]{1,0:T(8,128)S(1)}, f32[16,256,128]{2,1...) custom-call(s32[4]{0:T(128)S(1)} %pad_add_fusion.place, bf16[3,256,2048]{2,1,0:T(8,128)(2,1)} %bitcast.9, ...), custom_call_target="tpu_custom_call" | custom-call | flops 26214400 | bytes 5242880 | tf_op jit(solution)/shard_map/local_scan/pallas_call | solution.py:198
  15.6 1.6 %collective-permute-start = (f32[26,512]{1,0:T(8,128)S(1)}, f32[26,512]{1,0:T(8,128)S(1)}, u32[]{:S(2)}, u32[]{:S(2)}) collective-permute-start(f32[26,512]{1,0:T(8,128)S(1)} %get-tuple-element.34), channel_id=1, source_target_pairs={{0,2},{2,0},{4,6},{6,4},{8,10},{10,8},{12,14},{14,12},{16,18},{18,... | collective-permute-start | bytes 159752 | tf_op jit(solution)/shard_map/ppermute | solution.py:28
  19.9 2.2 %collective-permute-done.1.rest_2_ = f32[26,512]{1,0:T(8,128)S(1)} collective-permute-done((f32[26,512]{1,0:T(8,128)S(1)}, f32[26,512]{1,0:T(8,128)S(1)}, u32[]{:S(2)}, u32[]{:S(2)}) %collective-permute-start.1) | collective-permute-done | bytes 53280 | tf_op jit(solution)/shard_map/ppermute | solution.py:28
  22.1 1.7 %collective-permute-done.2.rest_3_ = f32[26,512]{1,0:T(8,128)S(1)} collective-permute-done((f32[26,512]{1,0:T(8,128)S(1)}, f32[26,512]{1,0:T(8,128)S(1)}, u32[]{:S(2)}, u32[]{:S(2)}) %collective-permute-start.2) | collective-permute-done | bytes 53280 | tf_op jit(solution)/shard_map/ppermute | solution.py:28
  24.5 3.3 %collective-permute-start.5 = (f32[26,512]{1,0:T(8,128)S(1)}, f32[26,512]{1,0:T(8,128)S(1)}, u32[]{:S(2)}, u32[]{:S(2)}) collective-permute-start(f32[26,512]{1,0:T(8,128)S(1)} %get-tuple-element.37.whole), channel_id=1, source_target_pairs={{0,24},{2,26},{4,28},{6,30},{1,25},{3,27},{5,29},{7,31}} | collective-permute-start | bytes 159752 | tf_op jit(solution)/shard_map/ppermute | solution.py:40
  29.0 2.5 %collective-permute-start.3 = (f32[26,512]{1,0:T(8,128)S(1)}, f32[26,512]{1,0:T(8,128)S(1)}, u32[]{:S(2)}, u32[]{:S(2)}) collective-permute-start(f32[26,512]{1,0:T(8,128)S(1)} %get-tuple-element.37.whole), channel_id=1, source_target_pairs={{0,8},{2,10},{4,12},{6,14},{8,16},{10,18},{12,20},{14,22},{16,24},... | collective-permute-start | bytes 159752 | tf_op jit(solution)/shard_map/ppermute | solution.py:40
  36.1 1.6 %collective-permute-start.6 = (f32[22,512]{1,0:T(8,128)S(1)}, f32[22,512]{1,0:T(8,128)S(1)}, u32[]{:S(2)}, u32[]{:S(2)}) collective-permute-start(f32[22,512]{1,0:T(8,128)S(1)} %get-tuple-element.43), channel_id=1, source_target_pairs={{0,2},{2,0},{4,6},{6,4},{8,10},{10,8},{12,14},{14,12},{16,18},{18,... | collective-permute-start | bytes 135176 | tf_op jit(solution)/shard_map/ppermute | solution.py:28
  42.1 2.1 %collective-permute-done.8.rest_3_ = f32[22,512]{1,0:T(8,128)S(1)} collective-permute-done((f32[22,512]{1,0:T(8,128)S(1)}, f32[22,512]{1,0:T(8,128)S(1)}, u32[]{:S(2)}, u32[]{:S(2)}) %collective-permute-start.8) | collective-permute-done | bytes 45088 | tf_op jit(solution)/shard_map/ppermute | solution.py:28
  44.2 4.3 %hidden_rows.2.refs_0_ = bf16[256,1024]{1,0:T(8,128)(2,1)S(1)} custom-call(s32[4]{0:T(128)S(1)} %pad_add_fusion.place, bf16[3,256,2048]{2,1,0:T(8,128)(2,1)S(1)} %bitcast.10, bf16[3,256,2048]{2,1,0:T(8,128)(2,1)S(1)} %bitcast.11, f32[3,3,2048]{2,1,0:T(4,128)S(1)} %copy-done.2, f32[16,2048]{1,0:T(8,128)S(1)} %bitcast.17, ...), custom_call_target="tpu_custom_call" | custom-call | flops 20971520 | bytes 2621440 | tf_op jit(solution)/shard_map/hidden_rows/pallas_call | solution.py:429
  49.6 4.3 %hidden_rows.3.refs_1_ = bf16[256,1024]{1,0:T(8,128)(2,1)S(1)} custom-call(s32[4]{0:T(128)S(1)} %pad_add_fusion.place, bf16[3,256,2048]{2,1,0:T(8,128)(2,1)S(1)} %bitcast.12, bf16[3,256,2048]{2,1,0:T(8,128)(2,1)S(1)} %bitcast.13, f32[3,3,2048]{2,1,0:T(4,128)S(1)} %copy-done.2, f32[16,2048]{1,0:T(8,128)S(1)} %bitcast.18, ...), custom_call_target="tpu_custom_call" | custom-call | flops 20971520 | bytes 2621440 | tf_op jit(solution)/shard_map/hidden_rows/pallas_call | solution.py:429
  53.9 1.6 %collective-permute-start.12 = (bf16[256,1024]{1,0:T(8,128)(2,1)S(1)}, bf16[256,1024]{1,0:T(8,128)(2,1)S(1)}, u32[]{:S(2)}, u32[]{:S(2)}) collective-permute-start(bf16[256,1024]{1,0:T(8,128)(2,1)S(1)} %hidden_rows.3.refs_1_), channel_id=1, source_target_pairs={{0,4},{2,6},{4,0},{6,2},{8,12},{10,14},{12,8},{14,10},{16,20},{18,... | collective-permute-start | bytes 1572872 | tf_op jit(solution)/shard_map/ppermute | solution.py:28
  55.5 7.9 %collective-permute-done.11.refs_4_ = bf16[256,1024]{1,0:T(8,128)(2,1)S(1)} collective-permute-done((bf16[256,1024]{1,0:T(8,128)(2,1)S(1)}, bf16[256,1024]{1,0:T(8,128)(2,1)S(1)}, u32[]{:S(2)}, u32[]{:S(2)}) %collective-permute-start.11) | collective-permute-done | bytes 524320 | tf_op jit(solution)/shard_map/ppermute | solution.py:28
  66.6 8.1 %collective-permute-done.12.refs_5_ = bf16[256,1024]{1,0:T(8,128)(2,1)S(1)} collective-permute-done((bf16[256,1024]{1,0:T(8,128)(2,1)S(1)}, bf16[256,1024]{1,0:T(8,128)(2,1)S(1)}, u32[]{:S(2)}, u32[]{:S(2)}) %collective-permute-start.12) | collective-permute-done | bytes 524320 | tf_op jit(solution)/shard_map/ppermute | solution.py:28
  75.2 2.5 %collective-permute-done.10.refs_3_ = bf16[256,1024]{1,0:T(8,128)(2,1)S(1)} collective-permute-done((bf16[256,1024]{1,0:T(8,128)(2,1)S(1)}, bf16[256,1024]{1,0:T(8,128)(2,1)S(1)}, u32[]{:S(2)}, u32[]{:S(2)}) %collective-permute-start.10) | collective-permute-done | bytes 524320 | tf_op jit(solution)/shard_map/ppermute | solution.py:28
  77.7 3.9 %project.2 = (bf16[768,512]{1,0:T(8,128)(2,1)S(1)}, bf16[768,256]{1,0:T(8,128)(2,1)S(1)}) custom-call(s32[4]{0:T(128)S(1)} %pad_add_fusion.place, bf16[256,1024]{1,0:T(8,128)(2,1)S(1)} %hidden_rows.2.refs_0_, bf16[256,1024]{1,0:T(8,128)(2,1)S(1)} %hidden_rows.3.refs_1_, bf16[256,1024]{1,0:T(8,128)(2,1)S(1)} %collective-permute-done.9.refs_2_, ...), custom_call_target="tpu_custom_call" | custom-call | flops 2415919104 | bytes 7471104 | tf_op jit(solution)/shard_map/project/pallas_call | solution.py:527
  82.4 2.9 %collective-permute-done.14.refs_7_ = bf16[256,1024]{1,0:T(8,128)(2,1)S(1)} collective-permute-done((bf16[256,1024]{1,0:T(8,128)(2,1)S(1)}, bf16[256,1024]{1,0:T(8,128)(2,1)S(1)}, u32[]{:S(2)}, u32[]{:S(2)}) %collective-permute-start.14) | collective-permute-done | bytes 524320 | tf_op jit(solution)/shard_map/ppermute | solution.py:28
  85.8 3.9 %project.3 = (bf16[1024,512]{1,0:T(8,128)(2,1)S(1)}, bf16[1024,512]{1,0:T(8,128)(2,1)S(1)}) custom-call(s32[4]{0:T(128)S(1)} %pad_add_fusion.place, bf16[256,1024]{1,0:T(8,128)(2,1)S(1)} %hidden_rows.2.refs_0_, bf16[256,1024]{1,0:T(8,128)(2,1)S(1)} %hidden_rows.3.refs_1_, bf16[256,1024]{1,0:T(8,128)(2,1)S(1)} %collective-permute-done.9.refs_2_, ...), custom_call_target="tpu_custom_call" | custom-call | flops 4294967296 | bytes 10485760 | tf_op jit(solution)/shard_map/project/pallas_call | solution.py:527
  89.8 2.6 %collective-permute-done.20.b = bf16[1024,512]{1,0:T(8,128)(2,1)S(1)} collective-permute-done((bf16[1024,512]{1,0:T(8,128)(2,1)S(1)}, bf16[1024,512]{1,0:T(8,128)(2,1)S(1)}, u32[]{:S(2)}, u32[]{:S(2)}) %collective-permute-start.20) | collective-permute-done | bytes 1048608 | tf_op jit(solution)/shard_map/ppermute | solution.py:630
  92.7 1.6 %collective-permute-start.21 = (bf16[256,512]{1,0:T(8,128)(2,1)S(1)}, bf16[256,512]{1,0:T(8,128)(2,1)S(1)}, u32[]{:S(2)}, u32[]{:S(2)}) collective-permute-start(bf16[256,512]{1,0:T(8,128)(2,1)S(1)} %get-tuple-element.54), channel_id=1, source_target_pairs={{0,2},{2,0},{4,6},{6,4},{8,10},{10,8},{12,14},{14,12},{16,18},{18,... | collective-permute-start | bytes 786440 | tf_op jit(solution)/shard_map/ppermute | solution.py:28
  96.3 5.7 %collective-permute-done.21.refs_1_ = bf16[256,512]{1,0:T(8,128)(2,1)S(1)} collective-permute-done((bf16[256,512]{1,0:T(8,128)(2,1)S(1)}, bf16[256,512]{1,0:T(8,128)(2,1)S(1)}, u32[]{:S(2)}, u32[]{:S(2)}) %collective-permute-start.21) | collective-permute-done | bytes 262176 | tf_op jit(solution)/shard_map/ppermute | solution.py:28
  101.9 6.0 %collective-permute-done.22.refs_2_ = bf16[256,512]{1,0:T(8,128)(2,1)S(1)} collective-permute-done((bf16[256,512]{1,0:T(8,128)(2,1)S(1)}, bf16[256,512]{1,0:T(8,128)(2,1)S(1)}, u32[]{:S(2)}, u32[]{:S(2)}) %collective-permute-start.22) | collective-permute-done | bytes 262176 | tf_op jit(solution)/shard_map/ppermute | solution.py:28
  108.0 1.7 %assemble.1 = bf16[256,2048]{1,0:T(8,128)(2,1)} custom-call(s32[4]{0:T(128)S(1)} %pad_add_fusion.place, bf16[256,512]{1,0:T(8,128)(2,1)S(1)} %get-tuple-element.53.refs_0_, bf16[256,512]{1,0:T(8,128)(2,1)S(1)} %collective-permute-done.21.refs_1_, bf16[256,512]{1,0:T(8,128)(2,1)S(1)} %collective-permute-done.22.refs_2_, ...), custom_call_target="tpu_custom_call" | custom-call | bytes 2097152 | tf_op jit(solution)/shard_map/assemble/pallas_call | solution.py:556
  (47 shorter events, 23.9 us)
Async XLA Ops:
  0.0 34.1 %collective-permute-start.16 = (bf16[2048,256]{1,0:T(8,128)(2,1)}, bf16[2048,256]{1,0:T(8,128)(2,1)}, u32[]{:S(2)}, u32[]{:S(2)}) collective-permute-start(bf16[2048,256]{1,0:T(8,128)(2,1)} %refs_8_.1), channel_id=1, source_target_pairs={{8,16},{10,18},{12,20},{14,22},{16,8},{18,10},{20,12},{22,14},{9,1... | collective-permute-start | bytes 3145736 | tf_op jit(solution)/shard_map/ppermute | solution.py:577
  1.8 32.3 %collective-permute-start.15 = (bf16[2048,256]{1,0:T(8,128)(2,1)}, bf16[2048,256]{1,0:T(8,128)(2,1)}, u32[]{:S(2)}, u32[]{:S(2)}) collective-permute-start(bf16[2048,256]{1,0:T(8,128)(2,1)} %refs_8_.1), channel_id=1, source_target_pairs={{0,8},{2,10},{4,12},{6,14},{8,0},{10,2},{12,4},{14,6},{16,24},{18,... | collective-permute-start | bytes 3145736 | tf_op jit(solution)/shard_map/ppermute | solution.py:577
  15.6 4.3 %collective-permute-start = (f32[26,512]{1,0:T(8,128)S(1)}, f32[26,512]{1,0:T(8,128)S(1)}, u32[]{:S(2)}, u32[]{:S(2)}) collective-permute-start(f32[26,512]{1,0:T(8,128)S(1)} %get-tuple-element.34), channel_id=1, source_target_pairs={{0,2},{2,0},{4,6},{6,4},{8,10},{10,8},{12,14},{14,12},{16,18},{18,... | collective-permute-start | bytes 159752 | tf_op jit(solution)/shard_map/ppermute | solution.py:28
  17.2 5.0 %collective-permute-start.1 = (f32[26,512]{1,0:T(8,128)S(1)}, f32[26,512]{1,0:T(8,128)S(1)}, u32[]{:S(2)}, u32[]{:S(2)}) collective-permute-start(f32[26,512]{1,0:T(8,128)S(1)} %get-tuple-element.35), channel_id=1, source_target_pairs={{0,4},{2,6},{4,0},{6,2},{8,12},{10,14},{12,8},{14,10},{16,20},{18,... | collective-permute-start | bytes 159752 | tf_op jit(solution)/shard_map/ppermute | solution.py:28
  18.7 5.2 %collective-permute-start.2 = (f32[26,512]{1,0:T(8,128)S(1)}, f32[26,512]{1,0:T(8,128)S(1)}, u32[]{:S(2)}, u32[]{:S(2)}) collective-permute-start(f32[26,512]{1,0:T(8,128)S(1)} %get-tuple-element.36), channel_id=1, source_target_pairs={{0,6},{2,4},{4,2},{6,0},{8,14},{10,12},{12,10},{14,8},{16,22},{18,... | collective-permute-start | bytes 159752 | tf_op jit(solution)/shard_map/ppermute | solution.py:28
  24.5 7.5 %collective-permute-start.5 = (f32[26,512]{1,0:T(8,128)S(1)}, f32[26,512]{1,0:T(8,128)S(1)}, u32[]{:S(2)}, u32[]{:S(2)}) collective-permute-start(f32[26,512]{1,0:T(8,128)S(1)} %get-tuple-element.37.whole), channel_id=1, source_target_pairs={{0,24},{2,26},{4,28},{6,30},{1,25},{3,27},{5,29},{7,31}} | collective-permute-start | bytes 159752 | tf_op jit(solution)/shard_map/ppermute | solution.py:40
  27.7 5.0 %collective-permute-start.4 = (f32[26,512]{1,0:T(8,128)S(1)}, f32[26,512]{1,0:T(8,128)S(1)}, u32[]{:S(2)}, u32[]{:S(2)}) collective-permute-start(f32[26,512]{1,0:T(8,128)S(1)} %get-tuple-element.37.whole), channel_id=1, source_target_pairs={{0,16},{2,18},{4,20},{6,22},{8,24},{10,26},{12,28},{14,30},{1,17},... | collective-permute-start | bytes 159752 | tf_op jit(solution)/shard_map/ppermute | solution.py:40
  29.0 4.4 %collective-permute-start.3 = (f32[26,512]{1,0:T(8,128)S(1)}, f32[26,512]{1,0:T(8,128)S(1)}, u32[]{:S(2)}, u32[]{:S(2)}) collective-permute-start(f32[26,512]{1,0:T(8,128)S(1)} %get-tuple-element.37.whole), channel_id=1, source_target_pairs={{0,8},{2,10},{4,12},{6,14},{8,16},{10,18},{12,20},{14,22},{16,24},... | collective-permute-start | bytes 159752 | tf_op jit(solution)/shard_map/ppermute | solution.py:40
  34.1 29.3 %collective-permute-start.17 = (bf16[2048,256]{1,0:T(8,128)(2,1)}, bf16[2048,256]{1,0:T(8,128)(2,1)S(1)}, u32[]{:S(2)}, u32[]{:S(2)}) collective-permute-start(bf16[2048,256]{1,0:T(8,128)(2,1)} %collective-permute-done.15.refs_7_.refs_9_), channel_id=1, source_target_pairs={{8,16},{10,18},{12,20},{14,22},{16,8},{18,10},{20,12},{22,14},{9,1... | collective-permute-start | bytes 3145736 | tf_op jit(solution)/shard_map/ppermute | solution.py:577
  34.8 28.6 %collective-permute-start.18 = (bf16[2048,256]{1,0:T(8,128)(2,1)}, bf16[2048,256]{1,0:T(8,128)(2,1)S(1)}, u32[]{:S(2)}, u32[]{:S(2)}) collective-permute-start(bf16[2048,256]{1,0:T(8,128)(2,1)} %collective-permute-done.16.refs_12_), channel_id=1, source_target_pairs={{8,0},{10,2},{12,4},{14,6},{16,24},{18,26},{20,28},{22,30},{9,1},{... | collective-permute-start | bytes 3145736 | tf_op jit(solution)/shard_map/ppermute | solution.py:577
  36.1 4.6 %collective-permute-start.6 = (f32[22,512]{1,0:T(8,128)S(1)}, f32[22,512]{1,0:T(8,128)S(1)}, u32[]{:S(2)}, u32[]{:S(2)}) collective-permute-start(f32[22,512]{1,0:T(8,128)S(1)} %get-tuple-element.43), channel_id=1, source_target_pairs={{0,2},{2,0},{4,6},{6,4},{8,10},{10,8},{12,14},{14,12},{16,18},{18,... | collective-permute-start | bytes 135176 | tf_op jit(solution)/shard_map/ppermute | solution.py:28
  37.7 4.4 %collective-permute-start.7 = (f32[22,512]{1,0:T(8,128)S(1)}, f32[22,512]{1,0:T(8,128)S(1)}, u32[]{:S(2)}, u32[]{:S(2)}) collective-permute-start(f32[22,512]{1,0:T(8,128)S(1)} %get-tuple-element.44), channel_id=1, source_target_pairs={{0,4},{2,6},{4,0},{6,2},{8,12},{10,14},{12,8},{14,10},{16,20},{18,... | collective-permute-start | bytes 135176 | tf_op jit(solution)/shard_map/ppermute | solution.py:28
  39.2 5.0 %collective-permute-start.8 = (f32[22,512]{1,0:T(8,128)S(1)}, f32[22,512]{1,0:T(8,128)S(1)}, u32[]{:S(2)}, u32[]{:S(2)}) collective-permute-start(f32[22,512]{1,0:T(8,128)S(1)} %get-tuple-element.45), channel_id=1, source_target_pairs={{0,6},{2,4},{4,2},{6,0},{8,14},{10,12},{12,10},{14,8},{16,22},{18,... | collective-permute-start | bytes 135176 | tf_op jit(solution)/shard_map/ppermute | solution.py:28
  48.5 14.9 %collective-permute-start.11 = (bf16[256,1024]{1,0:T(8,128)(2,1)S(1)}, bf16[256,1024]{1,0:T(8,128)(2,1)S(1)}, u32[]{:S(2)}, u32[]{:S(2)}) collective-permute-start(bf16[256,1024]{1,0:T(8,128)(2,1)S(1)} %hidden_rows.2.refs_0_), channel_id=1, source_target_pairs={{0,4},{2,6},{4,0},{6,2},{8,12},{10,14},{12,8},{14,10},{16,20},{18,... | collective-permute-start | bytes 1572872 | tf_op jit(solution)/shard_map/ppermute | solution.py:28
  49.1 14.4 %collective-permute-start.9 = (bf16[256,1024]{1,0:T(8,128)(2,1)S(1)}, bf16[256,1024]{1,0:T(8,128)(2,1)S(1)}, u32[]{:S(2)}, u32[]{:S(2)}) collective-permute-start(bf16[256,1024]{1,0:T(8,128)(2,1)S(1)} %hidden_rows.2.refs_0_), channel_id=1, source_target_pairs={{0,2},{2,0},{4,6},{6,4},{8,10},{10,8},{12,14},{14,12},{16,18},{18,... | collective-permute-start | bytes 1572872 | tf_op jit(solution)/shard_map/ppermute | solution.py:28
  53.9 20.8 %collective-permute-start.12 = (bf16[256,1024]{1,0:T(8,128)(2,1)S(1)}, bf16[256,1024]{1,0:T(8,128)(2,1)S(1)}, u32[]{:S(2)}, u32[]{:S(2)}) collective-permute-start(bf16[256,1024]{1,0:T(8,128)(2,1)S(1)} %hidden_rows.3.refs_1_), channel_id=1, source_target_pairs={{0,4},{2,6},{4,0},{6,2},{8,12},{10,14},{12,8},{14,10},{16,20},{18,... | collective-permute-start | bytes 1572872 | tf_op jit(solution)/shard_map/ppermute | solution.py:28
  63.4 22.4 %collective-permute-start.19 = (bf16[2048,256]{1,0:T(8,128)(2,1)S(1)}, bf16[2048,256]{1,0:T(8,128)(2,1)S(1)}, u32[]{:S(2)}, u32[]{:S(2)}) collective-permute-start(bf16[2048,256]{1,0:T(8,128)(2,1)S(1)} %collective-permute-done.17.refs_8_.refs_10_), channel_id=1, source_target_pairs={{8,0},{10,2},{12,4},{14,6},{16,24},{18,26},{20,28},{22,30},{9,1},{... | collective-permute-start | bytes 3145736 | tf_op jit(solution)/shard_map/ppermute | solution.py:577
  64.7 13.0 %collective-permute-start.10 = (bf16[256,1024]{1,0:T(8,128)(2,1)S(1)}, bf16[256,1024]{1,0:T(8,128)(2,1)S(1)}, u32[]{:S(2)}, u32[]{:S(2)}) collective-permute-start(bf16[256,1024]{1,0:T(8,128)(2,1)S(1)} %hidden_rows.3.refs_1_), channel_id=1, source_target_pairs={{0,2},{2,0},{4,6},{6,4},{8,10},{10,8},{12,14},{14,12},{16,18},{18,... | collective-permute-start | bytes 1572872 | tf_op jit(solution)/shard_map/ppermute | solution.py:28
  65.3 17.0 %collective-permute-start.13 = (bf16[256,1024]{1,0:T(8,128)(2,1)S(1)}, bf16[256,1024]{1,0:T(8,128)(2,1)S(1)}, u32[]{:S(2)}, u32[]{:S(2)}) collective-permute-start(bf16[256,1024]{1,0:T(8,128)(2,1)S(1)} %collective-permute-done.9.refs_2_), channel_id=1, source_target_pairs={{0,4},{2,6},{4,0},{6,2},{8,12},{10,14},{12,8},{14,10},{16,20},{18,... | collective-permute-start | bytes 1572872 | tf_op jit(solution)/shard_map/ppermute | solution.py:28
  74.7 10.6 %collective-permute-start.14 = (bf16[256,1024]{1,0:T(8,128)(2,1)S(1)}, bf16[256,1024]{1,0:T(8,128)(2,1)S(1)}, u32[]{:S(2)}, u32[]{:S(2)}) collective-permute-start(bf16[256,1024]{1,0:T(8,128)(2,1)S(1)} %collective-permute-done.12.refs_5_), channel_id=1, source_target_pairs={{0,2},{2,0},{4,6},{6,4},{8,10},{10,8},{12,14},{14,12},{16,18},{18,... | collective-permute-start | bytes 1572872 | tf_op jit(solution)/shard_map/ppermute | solution.py:28
  89.7 2.7 %collective-permute-start.20 = (bf16[1024,512]{1,0:T(8,128)(2,1)S(1)}, bf16[1024,512]{1,0:T(8,128)(2,1)S(1)}, u32[]{:S(2)}, u32[]{:S(2)}) collective-permute-start(bf16[1024,512]{1,0:T(8,128)(2,1)S(1)} %get-tuple-element.52), channel_id=1, source_target_pairs={{0,1},{1,0},{2,3},{3,2},{4,5},{5,4},{6,7},{7,6},{8,9},{9,8},{10,11... | collective-permute-start | bytes 3145736 | tf_op jit(solution)/shard_map/ppermute | solution.py:630
  92.7 9.2 %collective-permute-start.21 = (bf16[256,512]{1,0:T(8,128)(2,1)S(1)}, bf16[256,512]{1,0:T(8,128)(2,1)S(1)}, u32[]{:S(2)}, u32[]{:S(2)}) collective-permute-start(bf16[256,512]{1,0:T(8,128)(2,1)S(1)} %get-tuple-element.54), channel_id=1, source_target_pairs={{0,2},{2,0},{4,6},{6,4},{8,10},{10,8},{12,14},{14,12},{16,18},{18,... | collective-permute-start | bytes 786440 | tf_op jit(solution)/shard_map/ppermute | solution.py:28
  94.3 13.7 %collective-permute-start.22 = (bf16[256,512]{1,0:T(8,128)(2,1)S(1)}, bf16[256,512]{1,0:T(8,128)(2,1)S(1)}, u32[]{:S(2)}, u32[]{:S(2)}) collective-permute-start(bf16[256,512]{1,0:T(8,128)(2,1)S(1)} %get-tuple-element.55), channel_id=1, source_target_pairs={{0,4},{2,6},{4,0},{6,2},{8,12},{10,14},{12,8},{14,10},{16,20},{18,... | collective-permute-start | bytes 786440 | tf_op jit(solution)/shard_map/ppermute | solution.py:28
  95.8 12.2 %collective-permute-start.23 = (bf16[256,512]{1,0:T(8,128)(2,1)S(1)}, bf16[256,512]{1,0:T(8,128)(2,1)S(1)}, u32[]{:S(2)}, u32[]{:S(2)}) collective-permute-start(bf16[256,512]{1,0:T(8,128)(2,1)S(1)} %get-tuple-element.56), channel_id=1, source_target_pairs={{0,6},{2,4},{4,2},{6,0},{8,14},{10,12},{12,10},{14,8},{16,22},{18,... | collective-permute-start | bytes 786440 | tf_op jit(solution)/shard_map/ppermute | solution.py:28
  (6 other events, 141.7 us)
where the time goes:
time: 110 us
  waiting for transfers between devices  48.1 us (44%)
  starting transfers between devices  33 us (30%)
  Pallas kernels  26.5 us (24%)
  local copies, waits for them, and re-layouts  1.81 us (2%)
    ppermute x15, waiting for transfers between devices, send_xor(): return lax.ppermute(value, 'ctx', pairs)  43 us
    ppermute x15, starting transfers between devices, send_xor(): return lax.ppermute(value, 'ctx', pairs)  15.7 us
    ppermute x5, starting transfers between devices, send_planes(): return lax.ppermute(value, 'ctx', pairs)  10.1 us
    pallas_call x2, Pallas kernels, hidden_rows(): pl.pallas_call(functools.partial(hidden_body, seg_len=seg_len, order=orde...  8.55 us
    pallas_call x2, Pallas kernels, project(): pl.pallas_call(functools.partial(near_body if len(slots) == 3 else projec...  7.84 us
    ppermute x3, starting transfers between devices, send_along(): return lax.ppermute(value, 'ctx', pairs)  7.02 us
    pallas_call x1, Pallas kernels, local_scan(): pl.pallas_call(functools.partial(local_scan_body, seg_len=seg_len, order=...  6.87 us
    ppermute x1, waiting for transfers between devices, project_4x4(): mixed = add_up(kept, lax.ppermute(sent, 'tp', [(0, 1), (1, 0)]), group)  2.65 us
  transfers between devices with their start and end apart: 24, of which 18 were waited for; matrix products, arithmetic and copies ran while one was open for 0% of the time, Pallas kernels for 19%

commit v1 on v0

--- a/solution.py
+++ b/solution.py
@@ -170,7 +170,7 @@
             strided(value_pos, group, TOP - 3, pitch),
         ) + (zero,) * order
         start = step(1, step(0, start, True), True)
-        states = lax.fori_loop(2, seg_len, step, start, unroll=6)[4:]
+        states = lax.fori_loop(2, seg_len, step, start, unroll=seg_len - 2)[4:]
         for r in range(order):
             rate = row(rates, r, lanes)
             scan = states[r]
@@ -410,7 +410,7 @@
             strided(query_pos, group, TOP - 3, pitch),
         ) + tuple(states)
         start = step(1, step(0, start, early[0]), early[1])
-        lax.fori_loop(2, seg_len, step, start, unroll=6)
+        lax.fori_loop(2, seg_len, step, start, unroll=seg_len - 2)
         for s in range(SEGS):
             part = result_pos[group, TOP + s * pitch : TOP + s * pitch + seg_len, :]
             hidden[s * seg_len : (s + 1) * seg_len, lanes] = part.astype(hidden.dtype)
@@ -544,23 +544,22 @@
 
 def assemble_body(place, *refs):
     parts, out = refs[:-1], refs[-1]
-    width = parts[0].shape[1]
+    blocks = 2
+    width = parts[0].shape[1] // blocks
     for j, part in enumerate(parts):
-        column = pl.multiple_of((place[SPOT] ^ j) * width, LANES)
-        out[:, pl.ds(column, width)] = part[...]
+        for b in range(blocks):
+            column = ((b ^ place[ODD]) * len(parts) + (place[SPOT] ^ j)) * width
+            out[:, pl.ds(pl.multiple_of(column, LANES), width)] = part[:, b * width : (b + 1) * width]
 
 
 def assemble(place, parts, blocks, width):
     share = len(parts)
     rows = parts[0].shape[0]
+    held = pl.BlockSpec(memory_space=pltpu.VMEM)
     return pl.pallas_call(
         assemble_body,
-        grid_spec=pltpu.PrefetchScalarGridSpec(
-            num_scalar_prefetch=1,
-            grid=(blocks,),
-            in_specs=[pl.BlockSpec((rows, width), lambda b, place: (0, b ^ place[ODD]))] * share,
-            out_specs=pl.BlockSpec((rows, share * width), lambda b, place: (0, b)),
-        ),
+        in_specs=[pl.BlockSpec(memory_space=pltpu.SMEM)] + [held] * share,
+        out_specs=held,
         out_shape=jax.ShapeDtypeStruct((rows, share * blocks * width), jnp.bfloat16),
         compiler_params=pltpu.CompilerParams(vmem_limit_bytes=VMEM_LIMIT),
         cost_estimate=estimate(0, 4 * rows * share * blocks * width),

time: 110 us -> 110 us (level)
  transfers between devices with their start and end apart: 24 -> 24, of which waited for: 18 -> 18; matrix products, arithmetic and copies ran while one was open for 0% -> 0% of each run, Pallas kernels for 19% -> 18%
where the time goes in v1:
time: 110 us
  waiting for transfers between devices  48.7 us (44%)
  starting transfers between devices  33.2 us (30%)
  Pallas kernels  25.6 us (23%)
  local copies, waits for them, and re-layouts  1.81 us (2%)
    ppermute x15, waiting for transfers between devices, send_xor(): return lax.ppermute(value, 'ctx', pairs)  43.2 us
    ppermute x15, starting transfers between devices, send_xor(): return lax.ppermute(value, 'ctx', pairs)  16 us
    ppermute x5, starting transfers between devices, send_planes(): return lax.ppermute(value, 'ctx', pairs)  10.1 us
    pallas_call x2, Pallas kernels, hidden_rows(): pl.pallas_call(functools.partial(hidden_body, seg_len=seg_len, order=orde...  8.06 us
    pallas_call x2, Pallas kernels, project(): pl.pallas_call(functools.partial(near_body if len(slots) == 3 else projec...  7.83 us
    ppermute x3, starting transfers between devices, send_along(): return lax.ppermute(value, 'ctx', pairs)  7.02 us
    pallas_call x1, Pallas kernels, local_scan(): pl.pallas_call(functools.partial(local_scan_body, seg_len=seg_len, order=...  6.47 us
    ppermute x1, waiting for transfers between devices, project_4x4(): mixed = add_up(kept, lax.ppermute(sent, 'tp', [(0, 1), (1, 0)]), group)  2.65 us
  transfers between devices with their start and end apart: 24, of which 18 were waited for; matrix products, arithmetic and copies ran while one was open for 0% of the time, Pallas kernels for 18%

profile of v1, /device:TPU:0, one launch (start us, length us, event | category | flops | bytes accessed | tf_op | source)
XLA Modules:
  0.0 109.6 jit_solution(18115671926375692517)
XLA Ops:
  0.0 1.8 %collective-permute-start.16 = (bf16[2048,256]{1,0:T(8,128)(2,1)}, bf16[2048,256]{1,0:T(8,128)(2,1)}, u32[]{:S(2)}, u32[]{:S(2)}) collective-permute-start(bf16[2048,256]{1,0:T(8,128)(2,1)} %refs_8_.1), channel_id=1, source_target_pairs={{8,16},{10,18},{12,20},{14,22},{16,8},{18,10},{20,12},{22,14},{9,1... | collective-permute-start | bytes 3145736 | tf_op jit(solution)/shard_map/ppermute | solution.py:576
  1.8 5.1 %collective-permute-start.15 = (bf16[2048,256]{1,0:T(8,128)(2,1)}, bf16[2048,256]{1,0:T(8,128)(2,1)}, u32[]{:S(2)}, u32[]{:S(2)}) collective-permute-start(bf16[2048,256]{1,0:T(8,128)(2,1)} %refs_8_.1), channel_id=1, source_target_pairs={{0,8},{2,10},{4,12},{6,14},{8,0},{10,2},{12,4},{14,6},{16,24},{18,... | collective-permute-start | bytes 3145736 | tf_op jit(solution)/shard_map/ppermute | solution.py:576
  8.7 6.5 %local_scan.1 = (f32[26,512]{1,0:T(8,128)S(1)}, f32[26,512]{1,0:T(8,128)S(1)}, f32[26,512]{1,0:T(8,128)S(1)}, f32[26,512]{1,0:T(8,128)S(1)}, f32[16,256,128]{2,1...) custom-call(s32[4]{0:T(128)S(1)} %pad_add_fusion.place, bf16[3,256,2048]{2,1,0:T(8,128)(2,1)} %bitcast.9, ...), custom_call_target="tpu_custom_call" | custom-call | flops 26214400 | bytes 5242880 | tf_op jit(solution)/shard_map/local_scan/pallas_call | solution.py:198
  15.2 1.6 %collective-permute-start = (f32[26,512]{1,0:T(8,128)S(1)}, f32[26,512]{1,0:T(8,128)S(1)}, u32[]{:S(2)}, u32[]{:S(2)}) collective-permute-start(f32[26,512]{1,0:T(8,128)S(1)} %get-tuple-element.34), channel_id=1, source_target_pairs={{0,2},{2,0},{4,6},{6,4},{8,10},{10,8},{12,14},{14,12},{16,18},{18,... | collective-permute-start | bytes 159752 | tf_op jit(solution)/shard_map/ppermute | solution.py:28
  19.5 2.2 %collective-permute-done.1.rest_2_ = f32[26,512]{1,0:T(8,128)S(1)} collective-permute-done((f32[26,512]{1,0:T(8,128)S(1)}, f32[26,512]{1,0:T(8,128)S(1)}, u32[]{:S(2)}, u32[]{:S(2)}) %collective-permute-start.1) | collective-permute-done | bytes 53280 | tf_op jit(solution)/shard_map/ppermute | solution.py:28
  21.7 1.7 %collective-permute-done.2.rest_3_ = f32[26,512]{1,0:T(8,128)S(1)} collective-permute-done((f32[26,512]{1,0:T(8,128)S(1)}, f32[26,512]{1,0:T(8,128)S(1)}, u32[]{:S(2)}, u32[]{:S(2)}) %collective-permute-start.2) | collective-permute-done | bytes 53280 | tf_op jit(solution)/shard_map/ppermute | solution.py:28
  24.1 3.3 %collective-permute-start.5 = (f32[26,512]{1,0:T(8,128)S(1)}, f32[26,512]{1,0:T(8,128)S(1)}, u32[]{:S(2)}, u32[]{:S(2)}) collective-permute-start(f32[26,512]{1,0:T(8,128)S(1)} %get-tuple-element.37.whole), channel_id=1, source_target_pairs={{0,24},{2,26},{4,28},{6,30},{1,25},{3,27},{5,29},{7,31}} | collective-permute-start | bytes 159752 | tf_op jit(solution)/shard_map/ppermute | solution.py:40
  28.6 2.5 %collective-permute-start.3 = (f32[26,512]{1,0:T(8,128)S(1)}, f32[26,512]{1,0:T(8,128)S(1)}, u32[]{:S(2)}, u32[]{:S(2)}) collective-permute-start(f32[26,512]{1,0:T(8,128)S(1)} %get-tuple-element.37.whole), channel_id=1, source_target_pairs={{0,8},{2,10},{4,12},{6,14},{8,16},{10,18},{12,20},{14,22},{16,24},... | collective-permute-start | bytes 159752 | tf_op jit(solution)/shard_map/ppermute | solution.py:40
  36.1 1.6 %collective-permute-start.6 = (f32[22,512]{1,0:T(8,128)S(1)}, f32[22,512]{1,0:T(8,128)S(1)}, u32[]{:S(2)}, u32[]{:S(2)}) collective-permute-start(f32[22,512]{1,0:T(8,128)S(1)} %get-tuple-element.43), channel_id=1, source_target_pairs={{0,2},{2,0},{4,6},{6,4},{8,10},{10,8},{12,14},{14,12},{16,18},{18,... | collective-permute-start | bytes 135176 | tf_op jit(solution)/shard_map/ppermute | solution.py:28
  42.1 2.1 %collective-permute-done.8.rest_3_ = f32[22,512]{1,0:T(8,128)S(1)} collective-permute-done((f32[22,512]{1,0:T(8,128)S(1)}, f32[22,512]{1,0:T(8,128)S(1)}, u32[]{:S(2)}, u32[]{:S(2)}) %collective-permute-start.8) | collective-permute-done | bytes 45088 | tf_op jit(solution)/shard_map/ppermute | solution.py:28
  44.2 4.0 %hidden_rows.2.refs_0_ = bf16[256,1024]{1,0:T(8,128)(2,1)S(1)} custom-call(s32[4]{0:T(128)S(1)} %pad_add_fusion.place, bf16[3,256,2048]{2,1,0:T(8,128)(2,1)S(1)} %bitcast.10, bf16[3,256,2048]{2,1,0:T(8,128)(2,1)S(1)} %bitcast.11, f32[3,3,2048]{2,1,0:T(4,128)S(1)} %copy-done.2, f32[16,2048]{1,0:T(8,128)S(1)} %bitcast.17, ...), custom_call_target="tpu_custom_call" | custom-call | flops 20971520 | bytes 2621440 | tf_op jit(solution)/shard_map/hidden_rows/pallas_call | solution.py:429
  49.4 4.0 %hidden_rows.3.refs_1_ = bf16[256,1024]{1,0:T(8,128)(2,1)S(1)} custom-call(s32[4]{0:T(128)S(1)} %pad_add_fusion.place, bf16[3,256,2048]{2,1,0:T(8,128)(2,1)S(1)} %bitcast.12, bf16[3,256,2048]{2,1,0:T(8,128)(2,1)S(1)} %bitcast.13, f32[3,3,2048]{2,1,0:T(4,128)S(1)} %copy-done.2, f32[16,2048]{1,0:T(8,128)S(1)} %bitcast.18, ...), custom_call_target="tpu_custom_call" | custom-call | flops 20971520 | bytes 2621440 | tf_op jit(solution)/shard_map/hidden_rows/pallas_call | solution.py:429
  53.4 1.6 %collective-permute-start.12 = (bf16[256,1024]{1,0:T(8,128)(2,1)S(1)}, bf16[256,1024]{1,0:T(8,128)(2,1)S(1)}, u32[]{:S(2)}, u32[]{:S(2)}) collective-permute-start(bf16[256,1024]{1,0:T(8,128)(2,1)S(1)} %hidden_rows.3.refs_1_), channel_id=1, source_target_pairs={{0,4},{2,6},{4,0},{6,2},{8,12},{10,14},{12,8},{14,10},{16,20},{18,... | collective-permute-start | bytes 1572872 | tf_op jit(solution)/shard_map/ppermute | solution.py:28
  55.0 8.2 %collective-permute-done.11.refs_4_ = bf16[256,1024]{1,0:T(8,128)(2,1)S(1)} collective-permute-done((bf16[256,1024]{1,0:T(8,128)(2,1)S(1)}, bf16[256,1024]{1,0:T(8,128)(2,1)S(1)}, u32[]{:S(2)}, u32[]{:S(2)}) %collective-permute-start.11) | collective-permute-done | bytes 524320 | tf_op jit(solution)/shard_map/ppermute | solution.py:28
  66.6 7.8 %collective-permute-done.12.refs_5_ = bf16[256,1024]{1,0:T(8,128)(2,1)S(1)} collective-permute-done((bf16[256,1024]{1,0:T(8,128)(2,1)S(1)}, bf16[256,1024]{1,0:T(8,128)(2,1)S(1)}, u32[]{:S(2)}, u32[]{:S(2)}) %collective-permute-start.12) | collective-permute-done | bytes 524320 | tf_op jit(solution)/shard_map/ppermute | solution.py:28
  75.0 3.0 %collective-permute-done.10.refs_3_ = bf16[256,1024]{1,0:T(8,128)(2,1)S(1)} collective-permute-done((bf16[256,1024]{1,0:T(8,128)(2,1)S(1)}, bf16[256,1024]{1,0:T(8,128)(2,1)S(1)}, u32[]{:S(2)}, u32[]{:S(2)}) %collective-permute-start.10) | collective-permute-done | bytes 524320 | tf_op jit(solution)/shard_map/ppermute | solution.py:28
  78.0 3.9 %project.2 = (bf16[768,512]{1,0:T(8,128)(2,1)S(1)}, bf16[768,256]{1,0:T(8,128)(2,1)S(1)}) custom-call(s32[4]{0:T(128)S(1)} %pad_add_fusion.place, bf16[256,1024]{1,0:T(8,128)(2,1)S(1)} %hidden_rows.2.refs_0_, bf16[256,1024]{1,0:T(8,128)(2,1)S(1)} %hidden_rows.3.refs_1_, bf16[256,1024]{1,0:T(8,128)(2,1)S(1)} %collective-permute-done.9.refs_2_, ...), custom_call_target="tpu_custom_call" | custom-call | flops 2415919104 | bytes 7471104 | tf_op jit(solution)/shard_map/project/pallas_call | solution.py:527
  82.1 3.2 %collective-permute-done.14.refs_7_ = bf16[256,1024]{1,0:T(8,128)(2,1)S(1)} collective-permute-done((bf16[256,1024]{1,0:T(8,128)(2,1)S(1)}, bf16[256,1024]{1,0:T(8,128)(2,1)S(1)}, u32[]{:S(2)}, u32[]{:S(2)}) %collective-permute-start.14) | collective-permute-done | bytes 524320 | tf_op jit(solution)/shard_map/ppermute | solution.py:28
  85.8 3.9 %project.3 = (bf16[1024,512]{1,0:T(8,128)(2,1)S(1)}, bf16[1024,512]{1,0:T(8,128)(2,1)S(1)}) custom-call(s32[4]{0:T(128)S(1)} %pad_add_fusion.place, bf16[256,1024]{1,0:T(8,128)(2,1)S(1)} %hidden_rows.2.refs_0_, bf16[256,1024]{1,0:T(8,128)(2,1)S(1)} %hidden_rows.3.refs_1_, bf16[256,1024]{1,0:T(8,128)(2,1)S(1)} %collective-permute-done.9.refs_2_, ...), custom_call_target="tpu_custom_call" | custom-call | flops 4294967296 | bytes 10485760 | tf_op jit(solution)/shard_map/project/pallas_call | solution.py:527
  89.8 2.6 %collective-permute-done.20.b = bf16[1024,512]{1,0:T(8,128)(2,1)S(1)} collective-permute-done((bf16[1024,512]{1,0:T(8,128)(2,1)S(1)}, bf16[1024,512]{1,0:T(8,128)(2,1)S(1)}, u32[]{:S(2)}, u32[]{:S(2)}) %collective-permute-start.20) | collective-permute-done | bytes 1048608 | tf_op jit(solution)/shard_map/ppermute | solution.py:629
  92.7 1.6 %collective-permute-start.21 = (bf16[256,512]{1,0:T(8,128)(2,1)S(1)}, bf16[256,512]{1,0:T(8,128)(2,1)S(1)}, u32[]{:S(2)}, u32[]{:S(2)}) collective-permute-start(bf16[256,512]{1,0:T(8,128)(2,1)S(1)} %get-tuple-element.54), channel_id=1, source_target_pairs={{0,2},{2,0},{4,6},{6,4},{8,10},{10,8},{12,14},{14,12},{16,18},{18,... | collective-permute-start | bytes 786440 | tf_op jit(solution)/shard_map/ppermute | solution.py:28
  96.3 5.7 %collective-permute-done.21.refs_1_ = bf16[256,512]{1,0:T(8,128)(2,1)S(1)} collective-permute-done((bf16[256,512]{1,0:T(8,128)(2,1)S(1)}, bf16[256,512]{1,0:T(8,128)(2,1)S(1)}, u32[]{:S(2)}, u32[]{:S(2)}) %collective-permute-start.21) | collective-permute-done | bytes 262176 | tf_op jit(solution)/shard_map/ppermute | solution.py:28
  101.9 6.0 %collective-permute-done.22.refs_2_ = bf16[256,512]{1,0:T(8,128)(2,1)S(1)} collective-permute-done((bf16[256,512]{1,0:T(8,128)(2,1)S(1)}, bf16[256,512]{1,0:T(8,128)(2,1)S(1)}, u32[]{:S(2)}, u32[]{:S(2)}) %collective-permute-start.22) | collective-permute-done | bytes 262176 | tf_op jit(solution)/shard_map/ppermute | solution.py:28
  108.0 1.7 %assemble.1 = bf16[256,2048]{1,0:T(8,128)(2,1)} custom-call(s32[4]{0:T(128)S(1)} %pad_add_fusion.place, bf16[256,512]{1,0:T(8,128)(2,1)S(1)} %get-tuple-element.53.refs_0_, bf16[256,512]{1,0:T(8,128)(2,1)S(1)} %collective-permute-done.21.refs_1_, bf16[256,512]{1,0:T(8,128)(2,1)S(1)} %collective-permute-done.22.refs_2_, ...), custom_call_target="tpu_custom_call" | custom-call | bytes 2097152 | tf_op jit(solution)/shard_map/assemble/pallas_call | solution.py:559
  (47 shorter events, 24.0 us)
Async XLA Ops:
  0.0 34.1 %collective-permute-start.16 = (bf16[2048,256]{1,0:T(8,128)(2,1)}, bf16[2048,256]{1,0:T(8,128)(2,1)}, u32[]{:S(2)}, u32[]{:S(2)}) collective-permute-start(bf16[2048,256]{1,0:T(8,128)(2,1)} %refs_8_.1), channel_id=1, source_target_pairs={{8,16},{10,18},{12,20},{14,22},{16,8},{18,10},{20,12},{22,14},{9,1... | collective-permute-start | bytes 3145736 | tf_op jit(solution)/shard_map/ppermute | solution.py:576
  1.8 32.3 %collective-permute-start.15 = (bf16[2048,256]{1,0:T(8,128)(2,1)}, bf16[2048,256]{1,0:T(8,128)(2,1)}, u32[]{:S(2)}, u32[]{:S(2)}) collective-permute-start(bf16[2048,256]{1,0:T(8,128)(2,1)} %refs_8_.1), channel_id=1, source_target_pairs={{0,8},{2,10},{4,12},{6,14},{8,0},{10,2},{12,4},{14,6},{16,24},{18,... | collective-permute-start | bytes 3145736 | tf_op jit(solution)/shard_map/ppermute | solution.py:576
  15.2 4.3 %collective-permute-start = (f32[26,512]{1,0:T(8,128)S(1)}, f32[26,512]{1,0:T(8,128)S(1)}, u32[]{:S(2)}, u32[]{:S(2)}) collective-permute-start(f32[26,512]{1,0:T(8,128)S(1)} %get-tuple-element.34), channel_id=1, source_target_pairs={{0,2},{2,0},{4,6},{6,4},{8,10},{10,8},{12,14},{14,12},{16,18},{18,... | collective-permute-start | bytes 159752 | tf_op jit(solution)/shard_map/ppermute | solution.py:28
  16.8 5.0 %collective-permute-start.1 = (f32[26,512]{1,0:T(8,128)S(1)}, f32[26,512]{1,0:T(8,128)S(1)}, u32[]{:S(2)}, u32[]{:S(2)}) collective-permute-start(f32[26,512]{1,0:T(8,128)S(1)} %get-tuple-element.35), channel_id=1, source_target_pairs={{0,4},{2,6},{4,0},{6,2},{8,12},{10,14},{12,8},{14,10},{16,20},{18,... | collective-permute-start | bytes 159752 | tf_op jit(solution)/shard_map/ppermute | solution.py:28
  18.3 5.2 %collective-permute-start.2 = (f32[26,512]{1,0:T(8,128)S(1)}, f32[26,512]{1,0:T(8,128)S(1)}, u32[]{:S(2)}, u32[]{:S(2)}) collective-permute-start(f32[26,512]{1,0:T(8,128)S(1)} %get-tuple-element.36), channel_id=1, source_target_pairs={{0,6},{2,4},{4,2},{6,0},{8,14},{10,12},{12,10},{14,8},{16,22},{18,... | collective-permute-start | bytes 159752 | tf_op jit(solution)/shard_map/ppermute | solution.py:28
  24.1 7.9 %collective-permute-start.5 = (f32[26,512]{1,0:T(8,128)S(1)}, f32[26,512]{1,0:T(8,128)S(1)}, u32[]{:S(2)}, u32[]{:S(2)}) collective-permute-start(f32[26,512]{1,0:T(8,128)S(1)} %get-tuple-element.37.whole), channel_id=1, source_target_pairs={{0,24},{2,26},{4,28},{6,30},{1,25},{3,27},{5,29},{7,31}} | collective-permute-start | bytes 159752 | tf_op jit(solution)/shard_map/ppermute | solution.py:40
  27.3 5.4 %collective-permute-start.4 = (f32[26,512]{1,0:T(8,128)S(1)}, f32[26,512]{1,0:T(8,128)S(1)}, u32[]{:S(2)}, u32[]{:S(2)}) collective-permute-start(f32[26,512]{1,0:T(8,128)S(1)} %get-tuple-element.37.whole), channel_id=1, source_target_pairs={{0,16},{2,18},{4,20},{6,22},{8,24},{10,26},{12,28},{14,30},{1,17},... | collective-permute-start | bytes 159752 | tf_op jit(solution)/shard_map/ppermute | solution.py:40
  28.6 4.8 %collective-permute-start.3 = (f32[26,512]{1,0:T(8,128)S(1)}, f32[26,512]{1,0:T(8,128)S(1)}, u32[]{:S(2)}, u32[]{:S(2)}) collective-permute-start(f32[26,512]{1,0:T(8,128)S(1)} %get-tuple-element.37.whole), channel_id=1, source_target_pairs={{0,8},{2,10},{4,12},{6,14},{8,16},{10,18},{12,20},{14,22},{16,24},... | collective-permute-start | bytes 159752 | tf_op jit(solution)/shard_map/ppermute | solution.py:40
  34.1 29.1 %collective-permute-start.17 = (bf16[2048,256]{1,0:T(8,128)(2,1)}, bf16[2048,256]{1,0:T(8,128)(2,1)S(1)}, u32[]{:S(2)}, u32[]{:S(2)}) collective-permute-start(bf16[2048,256]{1,0:T(8,128)(2,1)} %collective-permute-done.15.refs_7_.refs_9_), channel_id=1, source_target_pairs={{8,16},{10,18},{12,20},{14,22},{16,8},{18,10},{20,12},{22,14},{9,1... | collective-permute-start | bytes 3145736 | tf_op jit(solution)/shard_map/ppermute | solution.py:576
  34.8 28.4 %collective-permute-start.18 = (bf16[2048,256]{1,0:T(8,128)(2,1)}, bf16[2048,256]{1,0:T(8,128)(2,1)S(1)}, u32[]{:S(2)}, u32[]{:S(2)}) collective-permute-start(bf16[2048,256]{1,0:T(8,128)(2,1)} %collective-permute-done.16.refs_12_), channel_id=1, source_target_pairs={{8,0},{10,2},{12,4},{14,6},{16,24},{18,26},{20,28},{22,30},{9,1},{... | collective-permute-start | bytes 3145736 | tf_op jit(solution)/shard_map/ppermute | solution.py:576
  36.1 4.6 %collective-permute-start.6 = (f32[22,512]{1,0:T(8,128)S(1)}, f32[22,512]{1,0:T(8,128)S(1)}, u32[]{:S(2)}, u32[]{:S(2)}) collective-permute-start(f32[22,512]{1,0:T(8,128)S(1)} %get-tuple-element.43), channel_id=1, source_target_pairs={{0,2},{2,0},{4,6},{6,4},{8,10},{10,8},{12,14},{14,12},{16,18},{18,... | collective-permute-start | bytes 135176 | tf_op jit(solution)/shard_map/ppermute | solution.py:28
  37.7 4.4 %collective-permute-start.7 = (f32[22,512]{1,0:T(8,128)S(1)}, f32[22,512]{1,0:T(8,128)S(1)}, u32[]{:S(2)}, u32[]{:S(2)}) collective-permute-start(f32[22,512]{1,0:T(8,128)S(1)} %get-tuple-element.44), channel_id=1, source_target_pairs={{0,4},{2,6},{4,0},{6,2},{8,12},{10,14},{12,8},{14,10},{16,20},{18,... | collective-permute-start | bytes 135176 | tf_op jit(solution)/shard_map/ppermute | solution.py:28
  39.2 5.0 %collective-permute-start.8 = (f32[22,512]{1,0:T(8,128)S(1)}, f32[22,512]{1,0:T(8,128)S(1)}, u32[]{:S(2)}, u32[]{:S(2)}) collective-permute-start(f32[22,512]{1,0:T(8,128)S(1)} %get-tuple-element.45), channel_id=1, source_target_pairs={{0,6},{2,4},{4,2},{6,0},{8,14},{10,12},{12,10},{14,8},{16,22},{18,... | collective-permute-start | bytes 135176 | tf_op jit(solution)/shard_map/ppermute | solution.py:28
  48.2 14.9 %collective-permute-start.11 = (bf16[256,1024]{1,0:T(8,128)(2,1)S(1)}, bf16[256,1024]{1,0:T(8,128)(2,1)S(1)}, u32[]{:S(2)}, u32[]{:S(2)}) collective-permute-start(bf16[256,1024]{1,0:T(8,128)(2,1)S(1)} %hidden_rows.2.refs_0_), channel_id=1, source_target_pairs={{0,4},{2,6},{4,0},{6,2},{8,12},{10,14},{12,8},{14,10},{16,20},{18,... | collective-permute-start | bytes 1572872 | tf_op jit(solution)/shard_map/ppermute | solution.py:28
  48.8 14.4 %collective-permute-start.9 = (bf16[256,1024]{1,0:T(8,128)(2,1)S(1)}, bf16[256,1024]{1,0:T(8,128)(2,1)S(1)}, u32[]{:S(2)}, u32[]{:S(2)}) collective-permute-start(bf16[256,1024]{1,0:T(8,128)(2,1)S(1)} %hidden_rows.2.refs_0_), channel_id=1, source_target_pairs={{0,2},{2,0},{4,6},{6,4},{8,10},{10,8},{12,14},{14,12},{16,18},{18,... | collective-permute-start | bytes 1572872 | tf_op jit(solution)/shard_map/ppermute | solution.py:28
  53.4 21.0 %collective-permute-start.12 = (bf16[256,1024]{1,0:T(8,128)(2,1)S(1)}, bf16[256,1024]{1,0:T(8,128)(2,1)S(1)}, u32[]{:S(2)}, u32[]{:S(2)}) collective-permute-start(bf16[256,1024]{1,0:T(8,128)(2,1)S(1)} %hidden_rows.3.refs_1_), channel_id=1, source_target_pairs={{0,4},{2,6},{4,0},{6,2},{8,12},{10,14},{12,8},{14,10},{16,20},{18,... | collective-permute-start | bytes 1572872 | tf_op jit(solution)/shard_map/ppermute | solution.py:28
  63.2 22.6 %collective-permute-start.19 = (bf16[2048,256]{1,0:T(8,128)(2,1)S(1)}, bf16[2048,256]{1,0:T(8,128)(2,1)S(1)}, u32[]{:S(2)}, u32[]{:S(2)}) collective-permute-start(bf16[2048,256]{1,0:T(8,128)(2,1)S(1)} %collective-permute-done.17.refs_8_.refs_10_), channel_id=1, source_target_pairs={{8,0},{10,2},{12,4},{14,6},{16,24},{18,26},{20,28},{22,30},{9,1},{... | collective-permute-start | bytes 3145736 | tf_op jit(solution)/shard_map/ppermute | solution.py:576
  64.5 13.5 %collective-permute-start.10 = (bf16[256,1024]{1,0:T(8,128)(2,1)S(1)}, bf16[256,1024]{1,0:T(8,128)(2,1)S(1)}, u32[]{:S(2)}, u32[]{:S(2)}) collective-permute-start(bf16[256,1024]{1,0:T(8,128)(2,1)S(1)} %hidden_rows.3.refs_1_), channel_id=1, source_target_pairs={{0,2},{2,0},{4,6},{6,4},{8,10},{10,8},{12,14},{14,12},{16,18},{18,... | collective-permute-start | bytes 1572872 | tf_op jit(solution)/shard_map/ppermute | solution.py:28
  65.1 17.0 %collective-permute-start.13 = (bf16[256,1024]{1,0:T(8,128)(2,1)S(1)}, bf16[256,1024]{1,0:T(8,128)(2,1)S(1)}, u32[]{:S(2)}, u32[]{:S(2)}) collective-permute-start(bf16[256,1024]{1,0:T(8,128)(2,1)S(1)} %collective-permute-done.9.refs_2_), channel_id=1, source_target_pairs={{0,4},{2,6},{4,0},{6,2},{8,12},{10,14},{12,8},{14,10},{16,20},{18,... | collective-permute-start | bytes 1572872 | tf_op jit(solution)/shard_map/ppermute | solution.py:28
  74.4 10.9 %collective-permute-start.14 = (bf16[256,1024]{1,0:T(8,128)(2,1)S(1)}, bf16[256,1024]{1,0:T(8,128)(2,1)S(1)}, u32[]{:S(2)}, u32[]{:S(2)}) collective-permute-start(bf16[256,1024]{1,0:T(8,128)(2,1)S(1)} %collective-permute-done.12.refs_5_), channel_id=1, source_target_pairs={{0,2},{2,0},{4,6},{6,4},{8,10},{10,8},{12,14},{14,12},{16,18},{18,... | collective-permute-start | bytes 1572872 | tf_op jit(solution)/shard_map/ppermute | solution.py:28
  89.7 2.7 %collective-permute-start.20 = (bf16[1024,512]{1,0:T(8,128)(2,1)S(1)}, bf16[1024,512]{1,0:T(8,128)(2,1)S(1)}, u32[]{:S(2)}, u32[]{:S(2)}) collective-permute-start(bf16[1024,512]{1,0:T(8,128)(2,1)S(1)} %get-tuple-element.52), channel_id=1, source_target_pairs={{0,1},{1,0},{2,3},{3,2},{4,5},{5,4},{6,7},{7,6},{8,9},{9,8},{10,11... | collective-permute-start | bytes 3145736 | tf_op jit(solution)/shard_map/ppermute | solution.py:629
  92.7 9.2 %collective-permute-start.21 = (bf16[256,512]{1,0:T(8,128)(2,1)S(1)}, bf16[256,512]{1,0:T(8,128)(2,1)S(1)}, u32[]{:S(2)}, u32[]{:S(2)}) collective-permute-start(bf16[256,512]{1,0:T(8,128)(2,1)S(1)} %get-tuple-element.54), channel_id=1, source_target_pairs={{0,2},{2,0},{4,6},{6,4},{8,10},{10,8},{12,14},{14,12},{16,18},{18,... | collective-permute-start | bytes 786440 | tf_op jit(solution)/shard_map/ppermute | solution.py:28
  94.3 13.7 %collective-permute-start.22 = (bf16[256,512]{1,0:T(8,128)(2,1)S(1)}, bf16[256,512]{1,0:T(8,128)(2,1)S(1)}, u32[]{:S(2)}, u32[]{:S(2)}) collective-permute-start(bf16[256,512]{1,0:T(8,128)(2,1)S(1)} %get-tuple-element.55), channel_id=1, source_target_pairs={{0,4},{2,6},{4,0},{6,2},{8,12},{10,14},{12,8},{14,10},{16,20},{18,... | collective-permute-start | bytes 786440 | tf_op jit(solution)/shard_map/ppermute | solution.py:28
  95.8 12.2 %collective-permute-start.23 = (bf16[256,512]{1,0:T(8,128)(2,1)S(1)}, bf16[256,512]{1,0:T(8,128)(2,1)S(1)}, u32[]{:S(2)}, u32[]{:S(2)}) collective-permute-start(bf16[256,512]{1,0:T(8,128)(2,1)S(1)} %get-tuple-element.56), channel_id=1, source_target_pairs={{0,6},{2,4},{4,2},{6,0},{8,14},{10,12},{12,10},{14,8},{16,22},{18,... | collective-permute-start | bytes 786440 | tf_op jit(solution)/shard_map/ppermute | solution.py:28
  (6 other events, 142.2 us)

commit v2 on v1

--- a/solution.py
+++ b/solution.py
@@ -90,7 +90,7 @@
 def local_scan_body(place, streams, short_all, rates_all, *rest, seg_len, order, share):
     ends = rest[:share]
     gated, prefix = rest[share : share + 2]
-    key_pos, value_pos, end_now, held, query_held, short_held, rates_held, held_sem, small_sem = rest[share + 2 :]
+    key_pos, value_pos, end_now, table, held, query_held, short_held, rates_held, held_sem, small_sem = rest[share + 2 :]
     now_at = pl.program_id(0)
     wide = end_now.shape[1]
     small = [
@@ -127,7 +127,10 @@
     key = held.at[pl.ds(0, 1), :, columns]
     value = held.at[pl.ds(1, 1), :, columns]
     short = short_held.at[:, :, columns]
-    rates = rates_held.at[:, columns]
+    rates = rates_held[:, columns]
+    table[0] = jnp.exp(-rates)
+    for e, d in enumerate((1, 2, 4)):
+        table[1 + e] = jnp.exp(rates * (-1.0 * d * seg_len))
     pitch = seg_len + 1
     groups = gated.shape[0]
     segment = lax.broadcasted_iota(jnp.int32, (SEGS, LANES), 0)
@@ -147,7 +150,7 @@
         lanes = slice(group * LANES, (group + 1) * LANES)
         key_taps = taps(short, 1, lanes)
         value_taps = taps(short, 2, lanes)
-        decay = [jnp.exp(-row(rates, r, lanes)) for r in range(order)]
+        decay = [row(table.at[0], r, lanes) for r in range(order)]
 
         def step(i, carry, early=False, group=group, key_taps=key_taps, value_taps=value_taps, decay=decay):
             k1, k2, v1, v2, *states = carry
@@ -172,11 +175,10 @@
         start = step(1, step(0, start, True), True)
         states = lax.fori_loop(2, seg_len, step, start, unroll=seg_len - 2)[4:]
         for r in range(order):
-            rate = row(rates, r, lanes)
             scan = states[r]
-            for d in (1, 2, 4):
+            for e, d in enumerate((1, 2, 4)):
                 moved = jnp.where(segment >= d, pltpu.roll(scan, d, 0), 0.0)
-                scan = scan + jnp.exp(rate * (-1.0 * d * seg_len)) * moved
+                scan = scan + row(table.at[1 + e], r, lanes) * moved
             prefix[group, r] = jnp.where(segment >= 1, pltpu.roll(scan, 1, 0), 0.0)
             end_now[r : r + 1, lanes] = scan[SEGS - 1 :, :]
 
@@ -214,6 +216,7 @@
                 pltpu.VMEM((groups, pos_rows, LANES), jnp.float32),
                 pltpu.VMEM((groups, pos_rows, LANES), jnp.float32),
                 pltpu.VMEM((order + LAST + FIRST, wide), jnp.float32),
+                pltpu.VMEM((4, order, wide), jnp.float32),
                 pltpu.VMEM((2, rows, chans), streams.dtype),
                 pltpu.VMEM((16, chans), streams.dtype),
                 pltpu.VMEM(short.shape, jnp.float32),
@@ -352,10 +355,12 @@
 def hidden_body(place, query, top, short, rates, coef, skip, gated, prefix, *rest, seg_len, order, share, first):
     starts = rest[:share]
     hidden = rest[share]
-    query_pos, result_pos, start_by_place = rest[share + 1 :]
+    query_pos, result_pos, start_by_place, table = rest[share + 1 :]
     pitch = seg_len + 1
     groups = gated.shape[0]
     now_at = pl.program_id(0) + first
+    table[0] = jnp.exp(-rates[...])
+    table[1] = jnp.exp(rates[...])
     segment = lax.broadcasted_iota(jnp.int32, (SEGS, LANES), 0).astype(jnp.float32)
 
     @pl.when(pl.program_id(0) == 0)
@@ -372,7 +377,7 @@
         lanes = slice(group * LANES, (group + 1) * LANES)
         query_taps = taps(short, 0, lanes)
         gain = jnp.broadcast_to(skip[0:1, lanes], (SEGS, LANES))
-        decay = [jnp.exp(-row(rates, r, lanes)) for r in range(order)]
+        decay = [row(table.at[0], r, lanes) for r in range(order)]
         scale = [row(coef, r, lanes) for r in range(order)]
         first = jnp.concatenate([top[b, 0:2, lanes] for b in (1, 2)], axis=0).astype(jnp.float32)
         last = start_by_place[now_at, order:, lanes]
@@ -385,7 +390,7 @@
             rate = row(rates, r, lanes)
             ahead = jnp.exp(rate * (segment * (-1.0 * seg_len)))
             before = jnp.broadcast_to(start_by_place[now_at, r : r + 1, lanes], (SEGS, LANES))
-            grown = jnp.exp(rate)
+            grown = row(table.at[1], r, lanes)
             before += jnp.where(segment >= 1.0, grown * (early[0] + grown * early[1]), 0.0)
             states.append(prefix[group, r] + ahead * before)
 
@@ -447,6 +452,7 @@
                 pltpu.VMEM((groups, pos_rows, LANES), jnp.float32),
                 pltpu.VMEM((groups, pos_rows, LANES), jnp.float32),
                 pltpu.VMEM((share, order + LAST, wide), jnp.float32),
+                pltpu.VMEM((2, order, wide), jnp.float32),
             ],
         ),
         out_shape=jax.ShapeDtypeStruct((rows, steps * wide), jnp.bfloat16),

time: 110 us -> 110 us (level)
  Pallas kernels: 25.6 us -> 24.4 us
  transfers between devices with their start and end apart: 24 -> 24, of which waited for: 18 -> 17; matrix products, arithmetic and copies ran while one was open for 0% -> 0% of each run, Pallas kernels for 18% -> 17%
where the time goes in v2:
time: 110 us
  waiting for transfers between devices  49.5 us (45%)
  starting transfers between devices  33.6 us (31%)
  Pallas kernels  24.4 us (22%)
  local copies, waits for them, and re-layouts  1.81 us (2%)
    ppermute x15, waiting for transfers between devices, send_xor(): return lax.ppermute(value, 'ctx', pairs)  43.6 us
    ppermute x15, starting transfers between devices, send_xor(): return lax.ppermute(value, 'ctx', pairs)  16.4 us
    ppermute x5, starting transfers between devices, send_planes(): return lax.ppermute(value, 'ctx', pairs)  10.1 us
    pallas_call x2, Pallas kernels, project(): pl.pallas_call(functools.partial(near_body if len(slots) == 3 else projec...  7.83 us
    pallas_call x2, Pallas kernels, hidden_rows(): pl.pallas_call(functools.partial(hidden_body, seg_len=seg_len, order=orde...  7.21 us
    ppermute x3, starting transfers between devices, send_along(): return lax.ppermute(value, 'ctx', pairs)  7.02 us
    pallas_call x1, Pallas kernels, local_scan(): pl.pallas_call(functools.partial(local_scan_body, seg_len=seg_len, order=...  6.12 us
    ppermute x1, waiting for transfers between devices, project_4x4(): mixed = add_up(kept, lax.ppermute(sent, 'tp', [(0, 1), (1, 0)]), group)  2.65 us
  transfers between devices with their start and end apart: 24, of which 17 were waited for; matrix products, arithmetic and copies ran while one was open for 0% of the time, Pallas kernels for 17%

profile of v2, /device:TPU:0, one launch (start us, length us, event | category | flops | bytes accessed | tf_op | source)
XLA Modules:
  0.0 109.6 jit_solution(2928802531916202386)
XLA Ops:
  0.0 1.8 %collective-permute-start.16 = (bf16[2048,256]{1,0:T(8,128)(2,1)}, bf16[2048,256]{1,0:T(8,128)(2,1)}, u32[]{:S(2)}, u32[]{:S(2)}) collective-permute-start(bf16[2048,256]{1,0:T(8,128)(2,1)} %refs_8_.1), channel_id=1, source_target_pairs={{8,16},{10,18},{12,20},{14,22},{16,8},{18,10},{20,12},{22,14},{9,1... | collective-permute-start | bytes 3145736 | tf_op jit(solution)/shard_map/ppermute | solution.py:582
  1.8 5.1 %collective-permute-start.15 = (bf16[2048,256]{1,0:T(8,128)(2,1)}, bf16[2048,256]{1,0:T(8,128)(2,1)}, u32[]{:S(2)}, u32[]{:S(2)}) collective-permute-start(bf16[2048,256]{1,0:T(8,128)(2,1)} %refs_8_.1), channel_id=1, source_target_pairs={{0,8},{2,10},{4,12},{6,14},{8,0},{10,2},{12,4},{14,6},{16,24},{18,... | collective-permute-start | bytes 3145736 | tf_op jit(solution)/shard_map/ppermute | solution.py:582
  8.7 6.1 %local_scan.1 = (f32[26,512]{1,0:T(8,128)S(1)}, f32[26,512]{1,0:T(8,128)S(1)}, f32[26,512]{1,0:T(8,128)S(1)}, f32[26,512]{1,0:T(8,128)S(1)}, f32[16,256,128]{2,1...) custom-call(s32[4]{0:T(128)S(1)} %pad_add_fusion.place, bf16[3,256,2048]{2,1,0:T(8,128)(2,1)} %bitcast.9, ...), custom_call_target="tpu_custom_call" | custom-call | flops 26214400 | bytes 5242880 | tf_op jit(solution)/shard_map/local_scan/pallas_call | solution.py:200
  14.8 1.6 %collective-permute-start = (f32[26,512]{1,0:T(8,128)S(1)}, f32[26,512]{1,0:T(8,128)S(1)}, u32[]{:S(2)}, u32[]{:S(2)}) collective-permute-start(f32[26,512]{1,0:T(8,128)S(1)} %get-tuple-element.34), channel_id=1, source_target_pairs={{0,2},{2,0},{4,6},{6,4},{8,10},{10,8},{12,14},{14,12},{16,18},{18,... | collective-permute-start | bytes 159752 | tf_op jit(solution)/shard_map/ppermute | solution.py:28
  19.2 2.2 %collective-permute-done.1.rest_2_ = f32[26,512]{1,0:T(8,128)S(1)} collective-permute-done((f32[26,512]{1,0:T(8,128)S(1)}, f32[26,512]{1,0:T(8,128)S(1)}, u32[]{:S(2)}, u32[]{:S(2)}) %collective-permute-start.1) | collective-permute-done | bytes 53280 | tf_op jit(solution)/shard_map/ppermute | solution.py:28
  21.4 1.7 %collective-permute-done.2.rest_3_ = f32[26,512]{1,0:T(8,128)S(1)} collective-permute-done((f32[26,512]{1,0:T(8,128)S(1)}, f32[26,512]{1,0:T(8,128)S(1)}, u32[]{:S(2)}, u32[]{:S(2)}) %collective-permute-start.2) | collective-permute-done | bytes 53280 | tf_op jit(solution)/shard_map/ppermute | solution.py:28
  23.7 3.3 %collective-permute-start.5 = (f32[26,512]{1,0:T(8,128)S(1)}, f32[26,512]{1,0:T(8,128)S(1)}, u32[]{:S(2)}, u32[]{:S(2)}) collective-permute-start(f32[26,512]{1,0:T(8,128)S(1)} %get-tuple-element.37.whole), channel_id=1, source_target_pairs={{0,24},{2,26},{4,28},{6,30},{1,25},{3,27},{5,29},{7,31}} | collective-permute-start | bytes 159752 | tf_op jit(solution)/shard_map/ppermute | solution.py:40
  28.3 2.5 %collective-permute-start.3 = (f32[26,512]{1,0:T(8,128)S(1)}, f32[26,512]{1,0:T(8,128)S(1)}, u32[]{:S(2)}, u32[]{:S(2)}) collective-permute-start(f32[26,512]{1,0:T(8,128)S(1)} %get-tuple-element.37.whole), channel_id=1, source_target_pairs={{0,8},{2,10},{4,12},{6,14},{8,16},{10,18},{12,20},{14,22},{16,24},... | collective-permute-start | bytes 159752 | tf_op jit(solution)/shard_map/ppermute | solution.py:40
  36.1 1.6 %collective-permute-start.6 = (f32[22,512]{1,0:T(8,128)S(1)}, f32[22,512]{1,0:T(8,128)S(1)}, u32[]{:S(2)}, u32[]{:S(2)}) collective-permute-start(f32[22,512]{1,0:T(8,128)S(1)} %get-tuple-element.43), channel_id=1, source_target_pairs={{0,2},{2,0},{4,6},{6,4},{8,10},{10,8},{12,14},{14,12},{16,18},{18,... | collective-permute-start | bytes 135176 | tf_op jit(solution)/shard_map/ppermute | solution.py:28
  42.1 2.1 %collective-permute-done.8.rest_3_ = f32[22,512]{1,0:T(8,128)S(1)} collective-permute-done((f32[22,512]{1,0:T(8,128)S(1)}, f32[22,512]{1,0:T(8,128)S(1)}, u32[]{:S(2)}, u32[]{:S(2)}) %collective-permute-start.8) | collective-permute-done | bytes 45088 | tf_op jit(solution)/shard_map/ppermute | solution.py:28
  44.2 3.6 %hidden_rows.2.refs_0_ = bf16[256,1024]{1,0:T(8,128)(2,1)S(1)} custom-call(s32[4]{0:T(128)S(1)} %pad_add_fusion.place, bf16[3,256,2048]{2,1,0:T(8,128)(2,1)S(1)} %bitcast.10, bf16[3,256,2048]{2,1,0:T(8,128)(2,1)S(1)} %bitcast.11, f32[3,3,2048]{2,1,0:T(4,128)S(1)} %copy-done.2, f32[16,2048]{1,0:T(8,128)S(1)} %bitcast.17, ...), custom_call_target="tpu_custom_call" | custom-call | flops 20971520 | bytes 2621440 | tf_op jit(solution)/shard_map/hidden_rows/pallas_call | solution.py:434
  48.9 3.6 %hidden_rows.3.refs_1_ = bf16[256,1024]{1,0:T(8,128)(2,1)S(1)} custom-call(s32[4]{0:T(128)S(1)} %pad_add_fusion.place, bf16[3,256,2048]{2,1,0:T(8,128)(2,1)S(1)} %bitcast.12, bf16[3,256,2048]{2,1,0:T(8,128)(2,1)S(1)} %bitcast.13, f32[3,3,2048]{2,1,0:T(4,128)S(1)} %copy-done.2, f32[16,2048]{1,0:T(8,128)S(1)} %bitcast.18, ...), custom_call_target="tpu_custom_call" | custom-call | flops 20971520 | bytes 2621440 | tf_op jit(solution)/shard_map/hidden_rows/pallas_call | solution.py:434
  52.6 1.6 %collective-permute-start.12 = (bf16[256,1024]{1,0:T(8,128)(2,1)S(1)}, bf16[256,1024]{1,0:T(8,128)(2,1)S(1)}, u32[]{:S(2)}, u32[]{:S(2)}) collective-permute-start(bf16[256,1024]{1,0:T(8,128)(2,1)S(1)} %hidden_rows.3.refs_1_), channel_id=1, source_target_pairs={{0,4},{2,6},{4,0},{6,2},{8,12},{10,14},{12,8},{14,10},{16,20},{18,... | collective-permute-start | bytes 1572872 | tf_op jit(solution)/shard_map/ppermute | solution.py:28
  54.1 8.6 %collective-permute-done.11.refs_4_ = bf16[256,1024]{1,0:T(8,128)(2,1)S(1)} collective-permute-done((bf16[256,1024]{1,0:T(8,128)(2,1)S(1)}, bf16[256,1024]{1,0:T(8,128)(2,1)S(1)}, u32[]{:S(2)}, u32[]{:S(2)}) %collective-permute-start.11) | collective-permute-done | bytes 524320 | tf_op jit(solution)/shard_map/ppermute | solution.py:28
  66.6 7.4 %collective-permute-done.12.refs_5_ = bf16[256,1024]{1,0:T(8,128)(2,1)S(1)} collective-permute-done((bf16[256,1024]{1,0:T(8,128)(2,1)S(1)}, bf16[256,1024]{1,0:T(8,128)(2,1)S(1)}, u32[]{:S(2)}, u32[]{:S(2)}) %collective-permute-start.12) | collective-permute-done | bytes 524320 | tf_op jit(solution)/shard_map/ppermute | solution.py:28
  74.5 3.9 %collective-permute-done.10.refs_3_ = bf16[256,1024]{1,0:T(8,128)(2,1)S(1)} collective-permute-done((bf16[256,1024]{1,0:T(8,128)(2,1)S(1)}, bf16[256,1024]{1,0:T(8,128)(2,1)S(1)}, u32[]{:S(2)}, u32[]{:S(2)}) %collective-permute-start.10) | collective-permute-done | bytes 524320 | tf_op jit(solution)/shard_map/ppermute | solution.py:28
  78.4 3.9 %project.2 = (bf16[768,512]{1,0:T(8,128)(2,1)S(1)}, bf16[768,256]{1,0:T(8,128)(2,1)S(1)}) custom-call(s32[4]{0:T(128)S(1)} %pad_add_fusion.place, bf16[256,1024]{1,0:T(8,128)(2,1)S(1)} %hidden_rows.2.refs_0_, bf16[256,1024]{1,0:T(8,128)(2,1)S(1)} %hidden_rows.3.refs_1_, bf16[256,1024]{1,0:T(8,128)(2,1)S(1)} %collective-permute-done.9.refs_2_, ...), custom_call_target="tpu_custom_call" | custom-call | flops 2415919104 | bytes 7471104 | tf_op jit(solution)/shard_map/project/pallas_call | solution.py:533
  82.3 3.0 %collective-permute-done.14.refs_7_ = bf16[256,1024]{1,0:T(8,128)(2,1)S(1)} collective-permute-done((bf16[256,1024]{1,0:T(8,128)(2,1)S(1)}, bf16[256,1024]{1,0:T(8,128)(2,1)S(1)}, u32[]{:S(2)}, u32[]{:S(2)}) %collective-permute-start.14) | collective-permute-done | bytes 524320 | tf_op jit(solution)/shard_map/ppermute | solution.py:28
  85.8 3.9 %project.3 = (bf16[1024,512]{1,0:T(8,128)(2,1)S(1)}, bf16[1024,512]{1,0:T(8,128)(2,1)S(1)}) custom-call(s32[4]{0:T(128)S(1)} %pad_add_fusion.place, bf16[256,1024]{1,0:T(8,128)(2,1)S(1)} %hidden_rows.2.refs_0_, bf16[256,1024]{1,0:T(8,128)(2,1)S(1)} %hidden_rows.3.refs_1_, bf16[256,1024]{1,0:T(8,128)(2,1)S(1)} %collective-permute-done.9.refs_2_, ...), custom_call_target="tpu_custom_call" | custom-call | flops 4294967296 | bytes 10485760 | tf_op jit(solution)/shard_map/project/pallas_call | solution.py:533
  89.8 2.6 %collective-permute-done.20.b = bf16[1024,512]{1,0:T(8,128)(2,1)S(1)} collective-permute-done((bf16[1024,512]{1,0:T(8,128)(2,1)S(1)}, bf16[1024,512]{1,0:T(8,128)(2,1)S(1)}, u32[]{:S(2)}, u32[]{:S(2)}) %collective-permute-start.20) | collective-permute-done | bytes 1048608 | tf_op jit(solution)/shard_map/ppermute | solution.py:635
  92.7 1.6 %collective-permute-start.21 = (bf16[256,512]{1,0:T(8,128)(2,1)S(1)}, bf16[256,512]{1,0:T(8,128)(2,1)S(1)}, u32[]{:S(2)}, u32[]{:S(2)}) collective-permute-start(bf16[256,512]{1,0:T(8,128)(2,1)S(1)} %get-tuple-element.54), channel_id=1, source_target_pairs={{0,2},{2,0},{4,6},{6,4},{8,10},{10,8},{12,14},{14,12},{16,18},{18,... | collective-permute-start | bytes 786440 | tf_op jit(solution)/shard_map/ppermute | solution.py:28
  96.3 5.7 %collective-permute-done.21.refs_1_ = bf16[256,512]{1,0:T(8,128)(2,1)S(1)} collective-permute-done((bf16[256,512]{1,0:T(8,128)(2,1)S(1)}, bf16[256,512]{1,0:T(8,128)(2,1)S(1)}, u32[]{:S(2)}, u32[]{:S(2)}) %collective-permute-start.21) | collective-permute-done | bytes 262176 | tf_op jit(solution)/shard_map/ppermute | solution.py:28
  101.9 6.0 %collective-permute-done.22.refs_2_ = bf16[256,512]{1,0:T(8,128)(2,1)S(1)} collective-permute-done((bf16[256,512]{1,0:T(8,128)(2,1)S(1)}, bf16[256,512]{1,0:T(8,128)(2,1)S(1)}, u32[]{:S(2)}, u32[]{:S(2)}) %collective-permute-start.22) | collective-permute-done | bytes 262176 | tf_op jit(solution)/shard_map/ppermute | solution.py:28
  108.0 1.7 %assemble.1 = bf16[256,2048]{1,0:T(8,128)(2,1)} custom-call(s32[4]{0:T(128)S(1)} %pad_add_fusion.place, bf16[256,512]{1,0:T(8,128)(2,1)S(1)} %get-tuple-element.53.refs_0_, bf16[256,512]{1,0:T(8,128)(2,1)S(1)} %collective-permute-done.21.refs_1_, bf16[256,512]{1,0:T(8,128)(2,1)S(1)} %collective-permute-done.22.refs_2_, ...), custom_call_target="tpu_custom_call" | custom-call | bytes 2097152 | tf_op jit(solution)/shard_map/assemble/pallas_call | solution.py:565
  (47 shorter events, 24.6 us)
Async XLA Ops:
  0.0 34.1 %collective-permute-start.16 = (bf16[2048,256]{1,0:T(8,128)(2,1)}, bf16[2048,256]{1,0:T(8,128)(2,1)}, u32[]{:S(2)}, u32[]{:S(2)}) collective-permute-start(bf16[2048,256]{1,0:T(8,128)(2,1)} %refs_8_.1), channel_id=1, source_target_pairs={{8,16},{10,18},{12,20},{14,22},{16,8},{18,10},{20,12},{22,14},{9,1... | collective-permute-start | bytes 3145736 | tf_op jit(solution)/shard_map/ppermute | solution.py:582
  1.8 32.3 %collective-permute-start.15 = (bf16[2048,256]{1,0:T(8,128)(2,1)}, bf16[2048,256]{1,0:T(8,128)(2,1)}, u32[]{:S(2)}, u32[]{:S(2)}) collective-permute-start(bf16[2048,256]{1,0:T(8,128)(2,1)} %refs_8_.1), channel_id=1, source_target_pairs={{0,8},{2,10},{4,12},{6,14},{8,0},{10,2},{12,4},{14,6},{16,24},{18,... | collective-permute-start | bytes 3145736 | tf_op jit(solution)/shard_map/ppermute | solution.py:582
  14.8 4.3 %collective-permute-start = (f32[26,512]{1,0:T(8,128)S(1)}, f32[26,512]{1,0:T(8,128)S(1)}, u32[]{:S(2)}, u32[]{:S(2)}) collective-permute-start(f32[26,512]{1,0:T(8,128)S(1)} %get-tuple-element.34), channel_id=1, source_target_pairs={{0,2},{2,0},{4,6},{6,4},{8,10},{10,8},{12,14},{14,12},{16,18},{18,... | collective-permute-start | bytes 159752 | tf_op jit(solution)/shard_map/ppermute | solution.py:28
  16.4 5.0 %collective-permute-start.1 = (f32[26,512]{1,0:T(8,128)S(1)}, f32[26,512]{1,0:T(8,128)S(1)}, u32[]{:S(2)}, u32[]{:S(2)}) collective-permute-start(f32[26,512]{1,0:T(8,128)S(1)} %get-tuple-element.35), channel_id=1, source_target_pairs={{0,4},{2,6},{4,0},{6,2},{8,12},{10,14},{12,8},{14,10},{16,20},{18,... | collective-permute-start | bytes 159752 | tf_op jit(solution)/shard_map/ppermute | solution.py:28
  17.9 5.2 %collective-permute-start.2 = (f32[26,512]{1,0:T(8,128)S(1)}, f32[26,512]{1,0:T(8,128)S(1)}, u32[]{:S(2)}, u32[]{:S(2)}) collective-permute-start(f32[26,512]{1,0:T(8,128)S(1)} %get-tuple-element.36), channel_id=1, source_target_pairs={{0,6},{2,4},{4,2},{6,0},{8,14},{10,12},{12,10},{14,8},{16,22},{18,... | collective-permute-start | bytes 159752 | tf_op jit(solution)/shard_map/ppermute | solution.py:28
  23.7 8.3 %collective-permute-start.5 = (f32[26,512]{1,0:T(8,128)S(1)}, f32[26,512]{1,0:T(8,128)S(1)}, u32[]{:S(2)}, u32[]{:S(2)}) collective-permute-start(f32[26,512]{1,0:T(8,128)S(1)} %get-tuple-element.37.whole), channel_id=1, source_target_pairs={{0,24},{2,26},{4,28},{6,30},{1,25},{3,27},{5,29},{7,31}} | collective-permute-start | bytes 159752 | tf_op jit(solution)/shard_map/ppermute | solution.py:40
  27.0 5.7 %collective-permute-start.4 = (f32[26,512]{1,0:T(8,128)S(1)}, f32[26,512]{1,0:T(8,128)S(1)}, u32[]{:S(2)}, u32[]{:S(2)}) collective-permute-start(f32[26,512]{1,0:T(8,128)S(1)} %get-tuple-element.37.whole), channel_id=1, source_target_pairs={{0,16},{2,18},{4,20},{6,22},{8,24},{10,26},{12,28},{14,30},{1,17},... | collective-permute-start | bytes 159752 | tf_op jit(solution)/shard_map/ppermute | solution.py:40
  28.3 5.1 %collective-permute-start.3 = (f32[26,512]{1,0:T(8,128)S(1)}, f32[26,512]{1,0:T(8,128)S(1)}, u32[]{:S(2)}, u32[]{:S(2)}) collective-permute-start(f32[26,512]{1,0:T(8,128)S(1)} %get-tuple-element.37.whole), channel_id=1, source_target_pairs={{0,8},{2,10},{4,12},{6,14},{8,16},{10,18},{12,20},{14,22},{16,24},... | collective-permute-start | bytes 159752 | tf_op jit(solution)/shard_map/ppermute | solution.py:40
  34.1 28.7 %collective-permute-start.17 = (bf16[2048,256]{1,0:T(8,128)(2,1)}, bf16[2048,256]{1,0:T(8,128)(2,1)S(1)}, u32[]{:S(2)}, u32[]{:S(2)}) collective-permute-start(bf16[2048,256]{1,0:T(8,128)(2,1)} %collective-permute-done.15.refs_7_.refs_9_), channel_id=1, source_target_pairs={{8,16},{10,18},{12,20},{14,22},{16,8},{18,10},{20,12},{22,14},{9,1... | collective-permute-start | bytes 3145736 | tf_op jit(solution)/shard_map/ppermute | solution.py:582
  34.8 27.9 %collective-permute-start.18 = (bf16[2048,256]{1,0:T(8,128)(2,1)}, bf16[2048,256]{1,0:T(8,128)(2,1)S(1)}, u32[]{:S(2)}, u32[]{:S(2)}) collective-permute-start(bf16[2048,256]{1,0:T(8,128)(2,1)} %collective-permute-done.16.refs_12_), channel_id=1, source_target_pairs={{8,0},{10,2},{12,4},{14,6},{16,24},{18,26},{20,28},{22,30},{9,1},{... | collective-permute-start | bytes 3145736 | tf_op jit(solution)/shard_map/ppermute | solution.py:582
  36.1 4.6 %collective-permute-start.6 = (f32[22,512]{1,0:T(8,128)S(1)}, f32[22,512]{1,0:T(8,128)S(1)}, u32[]{:S(2)}, u32[]{:S(2)}) collective-permute-start(f32[22,512]{1,0:T(8,128)S(1)} %get-tuple-element.43), channel_id=1, source_target_pairs={{0,2},{2,0},{4,6},{6,4},{8,10},{10,8},{12,14},{14,12},{16,18},{18,... | collective-permute-start | bytes 135176 | tf_op jit(solution)/shard_map/ppermute | solution.py:28
  37.7 4.4 %collective-permute-start.7 = (f32[22,512]{1,0:T(8,128)S(1)}, f32[22,512]{1,0:T(8,128)S(1)}, u32[]{:S(2)}, u32[]{:S(2)}) collective-permute-start(f32[22,512]{1,0:T(8,128)S(1)} %get-tuple-element.44), channel_id=1, source_target_pairs={{0,4},{2,6},{4,0},{6,2},{8,12},{10,14},{12,8},{14,10},{16,20},{18,... | collective-permute-start | bytes 135176 | tf_op jit(solution)/shard_map/ppermute | solution.py:28
  39.2 5.0 %collective-permute-start.8 = (f32[22,512]{1,0:T(8,128)S(1)}, f32[22,512]{1,0:T(8,128)S(1)}, u32[]{:S(2)}, u32[]{:S(2)}) collective-permute-start(f32[22,512]{1,0:T(8,128)S(1)} %get-tuple-element.45), channel_id=1, source_target_pairs={{0,6},{2,4},{4,2},{6,0},{8,14},{10,12},{12,10},{14,8},{16,22},{18,... | collective-permute-start | bytes 135176 | tf_op jit(solution)/shard_map/ppermute | solution.py:28
  47.8 14.9 %collective-permute-start.11 = (bf16[256,1024]{1,0:T(8,128)(2,1)S(1)}, bf16[256,1024]{1,0:T(8,128)(2,1)S(1)}, u32[]{:S(2)}, u32[]{:S(2)}) collective-permute-start(bf16[256,1024]{1,0:T(8,128)(2,1)S(1)} %hidden_rows.2.refs_0_), channel_id=1, source_target_pairs={{0,4},{2,6},{4,0},{6,2},{8,12},{10,14},{12,8},{14,10},{16,20},{18,... | collective-permute-start | bytes 1572872 | tf_op jit(solution)/shard_map/ppermute | solution.py:28
  48.4 14.4 %collective-permute-start.9 = (bf16[256,1024]{1,0:T(8,128)(2,1)S(1)}, bf16[256,1024]{1,0:T(8,128)(2,1)S(1)}, u32[]{:S(2)}, u32[]{:S(2)}) collective-permute-start(bf16[256,1024]{1,0:T(8,128)(2,1)S(1)} %hidden_rows.2.refs_0_), channel_id=1, source_target_pairs={{0,2},{2,0},{4,6},{6,4},{8,10},{10,8},{12,14},{14,12},{16,18},{18,... | collective-permute-start | bytes 1572872 | tf_op jit(solution)/shard_map/ppermute | solution.py:28
  52.6 21.4 %collective-permute-start.12 = (bf16[256,1024]{1,0:T(8,128)(2,1)S(1)}, bf16[256,1024]{1,0:T(8,128)(2,1)S(1)}, u32[]{:S(2)}, u32[]{:S(2)}) collective-permute-start(bf16[256,1024]{1,0:T(8,128)(2,1)S(1)} %hidden_rows.3.refs_1_), channel_id=1, source_target_pairs={{0,4},{2,6},{4,0},{6,2},{8,12},{10,14},{12,8},{14,10},{16,20},{18,... | collective-permute-start | bytes 1572872 | tf_op jit(solution)/shard_map/ppermute | solution.py:28
  62.8 23.0 %collective-permute-start.19 = (bf16[2048,256]{1,0:T(8,128)(2,1)S(1)}, bf16[2048,256]{1,0:T(8,128)(2,1)S(1)}, u32[]{:S(2)}, u32[]{:S(2)}) collective-permute-start(bf16[2048,256]{1,0:T(8,128)(2,1)S(1)} %collective-permute-done.17.refs_8_.refs_10_), channel_id=1, source_target_pairs={{8,0},{10,2},{12,4},{14,6},{16,24},{18,26},{20,28},{22,30},{9,1},{... | collective-permute-start | bytes 3145736 | tf_op jit(solution)/shard_map/ppermute | solution.py:582
  64.1 14.3 %collective-permute-start.10 = (bf16[256,1024]{1,0:T(8,128)(2,1)S(1)}, bf16[256,1024]{1,0:T(8,128)(2,1)S(1)}, u32[]{:S(2)}, u32[]{:S(2)}) collective-permute-start(bf16[256,1024]{1,0:T(8,128)(2,1)S(1)} %hidden_rows.3.refs_1_), channel_id=1, source_target_pairs={{0,2},{2,0},{4,6},{6,4},{8,10},{10,8},{12,14},{14,12},{16,18},{18,... | collective-permute-start | bytes 1572872 | tf_op jit(solution)/shard_map/ppermute | solution.py:28
  65.0 17.3 %collective-permute-start.13 = (bf16[256,1024]{1,0:T(8,128)(2,1)S(1)}, bf16[256,1024]{1,0:T(8,128)(2,1)S(1)}, u32[]{:S(2)}, u32[]{:S(2)}) collective-permute-start(bf16[256,1024]{1,0:T(8,128)(2,1)S(1)} %collective-permute-done.9.refs_2_), channel_id=1, source_target_pairs={{0,4},{2,6},{4,0},{6,2},{8,12},{10,14},{12,8},{14,10},{16,20},{18,... | collective-permute-start | bytes 1572872 | tf_op jit(solution)/shard_map/ppermute | solution.py:28
  74.0 11.3 %collective-permute-start.14 = (bf16[256,1024]{1,0:T(8,128)(2,1)S(1)}, bf16[256,1024]{1,0:T(8,128)(2,1)S(1)}, u32[]{:S(2)}, u32[]{:S(2)}) collective-permute-start(bf16[256,1024]{1,0:T(8,128)(2,1)S(1)} %collective-permute-done.12.refs_5_), channel_id=1, source_target_pairs={{0,2},{2,0},{4,6},{6,4},{8,10},{10,8},{12,14},{14,12},{16,18},{18,... | collective-permute-start | bytes 1572872 | tf_op jit(solution)/shard_map/ppermute | solution.py:28
  89.7 2.7 %collective-permute-start.20 = (bf16[1024,512]{1,0:T(8,128)(2,1)S(1)}, bf16[1024,512]{1,0:T(8,128)(2,1)S(1)}, u32[]{:S(2)}, u32[]{:S(2)}) collective-permute-start(bf16[1024,512]{1,0:T(8,128)(2,1)S(1)} %get-tuple-element.52), channel_id=1, source_target_pairs={{0,1},{1,0},{2,3},{3,2},{4,5},{5,4},{6,7},{7,6},{8,9},{9,8},{10,11... | collective-permute-start | bytes 3145736 | tf_op jit(solution)/shard_map/ppermute | solution.py:635
  92.7 9.2 %collective-permute-start.21 = (bf16[256,512]{1,0:T(8,128)(2,1)S(1)}, bf16[256,512]{1,0:T(8,128)(2,1)S(1)}, u32[]{:S(2)}, u32[]{:S(2)}) collective-permute-start(bf16[256,512]{1,0:T(8,128)(2,1)S(1)} %get-tuple-element.54), channel_id=1, source_target_pairs={{0,2},{2,0},{4,6},{6,4},{8,10},{10,8},{12,14},{14,12},{16,18},{18,... | collective-permute-start | bytes 786440 | tf_op jit(solution)/shard_map/ppermute | solution.py:28
  94.3 13.7 %collective-permute-start.22 = (bf16[256,512]{1,0:T(8,128)(2,1)S(1)}, bf16[256,512]{1,0:T(8,128)(2,1)S(1)}, u32[]{:S(2)}, u32[]{:S(2)}) collective-permute-start(bf16[256,512]{1,0:T(8,128)(2,1)S(1)} %get-tuple-element.55), channel_id=1, source_target_pairs={{0,4},{2,6},{4,0},{6,2},{8,12},{10,14},{12,8},{14,10},{16,20},{18,... | collective-permute-start | bytes 786440 | tf_op jit(solution)/shard_map/ppermute | solution.py:28
  95.8 12.2 %collective-permute-start.23 = (bf16[256,512]{1,0:T(8,128)(2,1)S(1)}, bf16[256,512]{1,0:T(8,128)(2,1)S(1)}, u32[]{:S(2)}, u32[]{:S(2)}) collective-permute-start(bf16[256,512]{1,0:T(8,128)(2,1)S(1)} %get-tuple-element.56), channel_id=1, source_target_pairs={{0,6},{2,4},{4,2},{6,0},{8,14},{10,12},{12,10},{14,8},{16,22},{18,... | collective-permute-start | bytes 786440 | tf_op jit(solution)/shard_map/ppermute | solution.py:28
  (6 other events, 143.1 us)

commit v3 on v2

--- a/solution.py
+++ b/solution.py
@@ -466,14 +466,9 @@
     width = columns.shape[1]
     top = 0
     for part in rows:
-        total = 0.0
-        start = 0
-        for piece in part:
-            size, depth = piece.shape
-            total += jnp.dot(
-                piece[...], columns[start : start + depth, :], preferred_element_type=jnp.float32
-            )
-            start += depth
+        size = part[0].shape[0]
+        joined = jnp.concatenate([piece[...] for piece in part], axis=1)
+        total = jnp.dot(joined, columns[...], preferred_element_type=jnp.float32)
         out[top : top + size, column : column + width] = total.astype(out.dtype)
         top += size
 

time: 110 us -> 110 us (level)
  no operation moved by 1% of the time
where the time goes in v3:
time: 110 us
  waiting for transfers between devices  49.5 us (45%)
  starting transfers between devices  33.6 us (31%)
  Pallas kernels  24.4 us (22%)
  local copies, waits for them, and re-layouts  1.81 us (2%)
    ppermute x15, waiting for transfers between devices, send_xor(): return lax.ppermute(value, 'ctx', pairs)  43.6 us
    ppermute x15, starting transfers between devices, send_xor(): return lax.ppermute(value, 'ctx', pairs)  16.4 us
    ppermute x5, starting transfers between devices, send_planes(): return lax.ppermute(value, 'ctx', pairs)  10.1 us
    pallas_call x2, Pallas kernels, project(): pl.pallas_call(functools.partial(near_body if len(slots) == 3 else projec...  7.83 us
    pallas_call x2, Pallas kernels, hidden_rows(): pl.pallas_call(functools.partial(hidden_body, seg_len=seg_len, order=orde...  7.21 us
    ppermute x3, starting transfers between devices, send_along(): return lax.ppermute(value, 'ctx', pairs)  7.02 us
    pallas_call x1, Pallas kernels, local_scan(): pl.pallas_call(functools.partial(local_scan_body, seg_len=seg_len, order=...  6.12 us
    ppermute x1, waiting for transfers between devices, project_4x4(): mixed = add_up(kept, lax.ppermute(sent, 'tp', [(0, 1), (1, 0)]), group)  2.65 us
  transfers between devices with their start and end apart: 24, of which 17 were waited for; matrix products, arithmetic and copies ran while one was open for 0% of the time, Pallas kernels for 17%

profile of v3, /device:TPU:0, one launch (start us, length us, event | category | flops | bytes accessed | tf_op | source)
XLA Modules:
  0.0 109.6 jit_solution(18295768765120287191)
XLA Ops:
  0.0 1.8 %collective-permute-start.16 = (bf16[2048,256]{1,0:T(8,128)(2,1)}, bf16[2048,256]{1,0:T(8,128)(2,1)}, u32[]{:S(2)}, u32[]{:S(2)}) collective-permute-start(bf16[2048,256]{1,0:T(8,128)(2,1)} %refs_8_.1), channel_id=1, source_target_pairs={{8,16},{10,18},{12,20},{14,22},{16,8},{18,10},{20,12},{22,14},{9,1... | collective-permute-start | bytes 3145736 | tf_op jit(solution)/shard_map/ppermute | solution.py:577
  1.8 5.1 %collective-permute-start.15 = (bf16[2048,256]{1,0:T(8,128)(2,1)}, bf16[2048,256]{1,0:T(8,128)(2,1)}, u32[]{:S(2)}, u32[]{:S(2)}) collective-permute-start(bf16[2048,256]{1,0:T(8,128)(2,1)} %refs_8_.1), channel_id=1, source_target_pairs={{0,8},{2,10},{4,12},{6,14},{8,0},{10,2},{12,4},{14,6},{16,24},{18,... | collective-permute-start | bytes 3145736 | tf_op jit(solution)/shard_map/ppermute | solution.py:577
  8.7 6.1 %local_scan.1 = (f32[26,512]{1,0:T(8,128)S(1)}, f32[26,512]{1,0:T(8,128)S(1)}, f32[26,512]{1,0:T(8,128)S(1)}, f32[26,512]{1,0:T(8,128)S(1)}, f32[16,256,128]{2,1...) custom-call(s32[4]{0:T(128)S(1)} %pad_add_fusion.place, bf16[3,256,2048]{2,1,0:T(8,128)(2,1)} %bitcast.9, ...), custom_call_target="tpu_custom_call" | custom-call | flops 26214400 | bytes 5242880 | tf_op jit(solution)/shard_map/local_scan/pallas_call | solution.py:200
  14.8 1.6 %collective-permute-start = (f32[26,512]{1,0:T(8,128)S(1)}, f32[26,512]{1,0:T(8,128)S(1)}, u32[]{:S(2)}, u32[]{:S(2)}) collective-permute-start(f32[26,512]{1,0:T(8,128)S(1)} %get-tuple-element.34), channel_id=1, source_target_pairs={{0,2},{2,0},{4,6},{6,4},{8,10},{10,8},{12,14},{14,12},{16,18},{18,... | collective-permute-start | bytes 159752 | tf_op jit(solution)/shard_map/ppermute | solution.py:28
  19.2 2.2 %collective-permute-done.1.rest_2_ = f32[26,512]{1,0:T(8,128)S(1)} collective-permute-done((f32[26,512]{1,0:T(8,128)S(1)}, f32[26,512]{1,0:T(8,128)S(1)}, u32[]{:S(2)}, u32[]{:S(2)}) %collective-permute-start.1) | collective-permute-done | bytes 53280 | tf_op jit(solution)/shard_map/ppermute | solution.py:28
  21.4 1.7 %collective-permute-done.2.rest_3_ = f32[26,512]{1,0:T(8,128)S(1)} collective-permute-done((f32[26,512]{1,0:T(8,128)S(1)}, f32[26,512]{1,0:T(8,128)S(1)}, u32[]{:S(2)}, u32[]{:S(2)}) %collective-permute-start.2) | collective-permute-done | bytes 53280 | tf_op jit(solution)/shard_map/ppermute | solution.py:28
  23.7 3.3 %collective-permute-start.5 = (f32[26,512]{1,0:T(8,128)S(1)}, f32[26,512]{1,0:T(8,128)S(1)}, u32[]{:S(2)}, u32[]{:S(2)}) collective-permute-start(f32[26,512]{1,0:T(8,128)S(1)} %get-tuple-element.37.whole), channel_id=1, source_target_pairs={{0,24},{2,26},{4,28},{6,30},{1,25},{3,27},{5,29},{7,31}} | collective-permute-start | bytes 159752 | tf_op jit(solution)/shard_map/ppermute | solution.py:40
  28.3 2.5 %collective-permute-start.3 = (f32[26,512]{1,0:T(8,128)S(1)}, f32[26,512]{1,0:T(8,128)S(1)}, u32[]{:S(2)}, u32[]{:S(2)}) collective-permute-start(f32[26,512]{1,0:T(8,128)S(1)} %get-tuple-element.37.whole), channel_id=1, source_target_pairs={{0,8},{2,10},{4,12},{6,14},{8,16},{10,18},{12,20},{14,22},{16,24},... | collective-permute-start | bytes 159752 | tf_op jit(solution)/shard_map/ppermute | solution.py:40
  36.1 1.6 %collective-permute-start.6 = (f32[22,512]{1,0:T(8,128)S(1)}, f32[22,512]{1,0:T(8,128)S(1)}, u32[]{:S(2)}, u32[]{:S(2)}) collective-permute-start(f32[22,512]{1,0:T(8,128)S(1)} %get-tuple-element.43), channel_id=1, source_target_pairs={{0,2},{2,0},{4,6},{6,4},{8,10},{10,8},{12,14},{14,12},{16,18},{18,... | collective-permute-start | bytes 135176 | tf_op jit(solution)/shard_map/ppermute | solution.py:28
  42.1 2.1 %collective-permute-done.8.rest_3_ = f32[22,512]{1,0:T(8,128)S(1)} collective-permute-done((f32[22,512]{1,0:T(8,128)S(1)}, f32[22,512]{1,0:T(8,128)S(1)}, u32[]{:S(2)}, u32[]{:S(2)}) %collective-permute-start.8) | collective-permute-done | bytes 45088 | tf_op jit(solution)/shard_map/ppermute | solution.py:28
  44.2 3.6 %hidden_rows.2.refs_0_ = bf16[256,1024]{1,0:T(8,128)(2,1)S(1)} custom-call(s32[4]{0:T(128)S(1)} %pad_add_fusion.place, bf16[3,256,2048]{2,1,0:T(8,128)(2,1)S(1)} %bitcast.10, bf16[3,256,2048]{2,1,0:T(8,128)(2,1)S(1)} %bitcast.11, f32[3,3,2048]{2,1,0:T(4,128)S(1)} %copy-done.2, f32[16,2048]{1,0:T(8,128)S(1)} %bitcast.17, ...), custom_call_target="tpu_custom_call" | custom-call | flops 20971520 | bytes 2621440 | tf_op jit(solution)/shard_map/hidden_rows/pallas_call | solution.py:434
  48.9 3.6 %hidden_rows.3.refs_1_ = bf16[256,1024]{1,0:T(8,128)(2,1)S(1)} custom-call(s32[4]{0:T(128)S(1)} %pad_add_fusion.place, bf16[3,256,2048]{2,1,0:T(8,128)(2,1)S(1)} %bitcast.12, bf16[3,256,2048]{2,1,0:T(8,128)(2,1)S(1)} %bitcast.13, f32[3,3,2048]{2,1,0:T(4,128)S(1)} %copy-done.2, f32[16,2048]{1,0:T(8,128)S(1)} %bitcast.18, ...), custom_call_target="tpu_custom_call" | custom-call | flops 20971520 | bytes 2621440 | tf_op jit(solution)/shard_map/hidden_rows/pallas_call | solution.py:434
  52.6 1.6 %collective-permute-start.12 = (bf16[256,1024]{1,0:T(8,128)(2,1)S(1)}, bf16[256,1024]{1,0:T(8,128)(2,1)S(1)}, u32[]{:S(2)}, u32[]{:S(2)}) collective-permute-start(bf16[256,1024]{1,0:T(8,128)(2,1)S(1)} %hidden_rows.3.refs_1_), channel_id=1, source_target_pairs={{0,4},{2,6},{4,0},{6,2},{8,12},{10,14},{12,8},{14,10},{16,20},{18,... | collective-permute-start | bytes 1572872 | tf_op jit(solution)/shard_map/ppermute | solution.py:28
  54.1 8.6 %collective-permute-done.11.refs_4_ = bf16[256,1024]{1,0:T(8,128)(2,1)S(1)} collective-permute-done((bf16[256,1024]{1,0:T(8,128)(2,1)S(1)}, bf16[256,1024]{1,0:T(8,128)(2,1)S(1)}, u32[]{:S(2)}, u32[]{:S(2)}) %collective-permute-start.11) | collective-permute-done | bytes 524320 | tf_op jit(solution)/shard_map/ppermute | solution.py:28
  66.6 7.4 %collective-permute-done.12.refs_5_ = bf16[256,1024]{1,0:T(8,128)(2,1)S(1)} collective-permute-done((bf16[256,1024]{1,0:T(8,128)(2,1)S(1)}, bf16[256,1024]{1,0:T(8,128)(2,1)S(1)}, u32[]{:S(2)}, u32[]{:S(2)}) %collective-permute-start.12) | collective-permute-done | bytes 524320 | tf_op jit(solution)/shard_map/ppermute | solution.py:28
  74.5 3.9 %collective-permute-done.10.refs_3_ = bf16[256,1024]{1,0:T(8,128)(2,1)S(1)} collective-permute-done((bf16[256,1024]{1,0:T(8,128)(2,1)S(1)}, bf16[256,1024]{1,0:T(8,128)(2,1)S(1)}, u32[]{:S(2)}, u32[]{:S(2)}) %collective-permute-start.10) | collective-permute-done | bytes 524320 | tf_op jit(solution)/shard_map/ppermute | solution.py:28
  78.4 3.9 %project.2 = (bf16[768,512]{1,0:T(8,128)(2,1)S(1)}, bf16[768,256]{1,0:T(8,128)(2,1)S(1)}) custom-call(s32[4]{0:T(128)S(1)} %pad_add_fusion.place, bf16[256,1024]{1,0:T(8,128)(2,1)S(1)} %hidden_rows.2.refs_0_, bf16[256,1024]{1,0:T(8,128)(2,1)S(1)} %hidden_rows.3.refs_1_, bf16[256,1024]{1,0:T(8,128)(2,1)S(1)} %collective-permute-done.9.refs_2_, ...), custom_call_target="tpu_custom_call" | custom-call | flops 2415919104 | bytes 7471104 | tf_op jit(solution)/shard_map/project/pallas_call | solution.py:528
  82.3 3.0 %collective-permute-done.14.refs_7_ = bf16[256,1024]{1,0:T(8,128)(2,1)S(1)} collective-permute-done((bf16[256,1024]{1,0:T(8,128)(2,1)S(1)}, bf16[256,1024]{1,0:T(8,128)(2,1)S(1)}, u32[]{:S(2)}, u32[]{:S(2)}) %collective-permute-start.14) | collective-permute-done | bytes 524320 | tf_op jit(solution)/shard_map/ppermute | solution.py:28
  85.8 3.9 %project.3 = (bf16[1024,512]{1,0:T(8,128)(2,1)S(1)}, bf16[1024,512]{1,0:T(8,128)(2,1)S(1)}) custom-call(s32[4]{0:T(128)S(1)} %pad_add_fusion.place, bf16[256,1024]{1,0:T(8,128)(2,1)S(1)} %hidden_rows.2.refs_0_, bf16[256,1024]{1,0:T(8,128)(2,1)S(1)} %hidden_rows.3.refs_1_, bf16[256,1024]{1,0:T(8,128)(2,1)S(1)} %collective-permute-done.9.refs_2_, ...), custom_call_target="tpu_custom_call" | custom-call | flops 4294967296 | bytes 10485760 | tf_op jit(solution)/shard_map/project/pallas_call | solution.py:528
  89.8 2.6 %collective-permute-done.20.b = bf16[1024,512]{1,0:T(8,128)(2,1)S(1)} collective-permute-done((bf16[1024,512]{1,0:T(8,128)(2,1)S(1)}, bf16[1024,512]{1,0:T(8,128)(2,1)S(1)}, u32[]{:S(2)}, u32[]{:S(2)}) %collective-permute-start.20) | collective-permute-done | bytes 1048608 | tf_op jit(solution)/shard_map/ppermute | solution.py:630
  92.7 1.6 %collective-permute-start.21 = (bf16[256,512]{1,0:T(8,128)(2,1)S(1)}, bf16[256,512]{1,0:T(8,128)(2,1)S(1)}, u32[]{:S(2)}, u32[]{:S(2)}) collective-permute-start(bf16[256,512]{1,0:T(8,128)(2,1)S(1)} %get-tuple-element.54), channel_id=1, source_target_pairs={{0,2},{2,0},{4,6},{6,4},{8,10},{10,8},{12,14},{14,12},{16,18},{18,... | collective-permute-start | bytes 786440 | tf_op jit(solution)/shard_map/ppermute | solution.py:28
  96.3 5.7 %collective-permute-done.21.refs_1_ = bf16[256,512]{1,0:T(8,128)(2,1)S(1)} collective-permute-done((bf16[256,512]{1,0:T(8,128)(2,1)S(1)}, bf16[256,512]{1,0:T(8,128)(2,1)S(1)}, u32[]{:S(2)}, u32[]{:S(2)}) %collective-permute-start.21) | collective-permute-done | bytes 262176 | tf_op jit(solution)/shard_map/ppermute | solution.py:28
  101.9 6.0 %collective-permute-done.22.refs_2_ = bf16[256,512]{1,0:T(8,128)(2,1)S(1)} collective-permute-done((bf16[256,512]{1,0:T(8,128)(2,1)S(1)}, bf16[256,512]{1,0:T(8,128)(2,1)S(1)}, u32[]{:S(2)}, u32[]{:S(2)}) %collective-permute-start.22) | collective-permute-done | bytes 262176 | tf_op jit(solution)/shard_map/ppermute | solution.py:28
  108.0 1.7 %assemble.1 = bf16[256,2048]{1,0:T(8,128)(2,1)} custom-call(s32[4]{0:T(128)S(1)} %pad_add_fusion.place, bf16[256,512]{1,0:T(8,128)(2,1)S(1)} %get-tuple-element.53.refs_0_, bf16[256,512]{1,0:T(8,128)(2,1)S(1)} %collective-permute-done.21.refs_1_, bf16[256,512]{1,0:T(8,128)(2,1)S(1)} %collective-permute-done.22.refs_2_, ...), custom_call_target="tpu_custom_call" | custom-call | bytes 2097152 | tf_op jit(solution)/shard_map/assemble/pallas_call | solution.py:560
  (47 shorter events, 24.6 us)
Async XLA Ops:
  0.0 34.1 %collective-permute-start.16 = (bf16[2048,256]{1,0:T(8,128)(2,1)}, bf16[2048,256]{1,0:T(8,128)(2,1)}, u32[]{:S(2)}, u32[]{:S(2)}) collective-permute-start(bf16[2048,256]{1,0:T(8,128)(2,1)} %refs_8_.1), channel_id=1, source_target_pairs={{8,16},{10,18},{12,20},{14,22},{16,8},{18,10},{20,12},{22,14},{9,1... | collective-permute-start | bytes 3145736 | tf_op jit(solution)/shard_map/ppermute | solution.py:577
  1.8 32.3 %collective-permute-start.15 = (bf16[2048,256]{1,0:T(8,128)(2,1)}, bf16[2048,256]{1,0:T(8,128)(2,1)}, u32[]{:S(2)}, u32[]{:S(2)}) collective-permute-start(bf16[2048,256]{1,0:T(8,128)(2,1)} %refs_8_.1), channel_id=1, source_target_pairs={{0,8},{2,10},{4,12},{6,14},{8,0},{10,2},{12,4},{14,6},{16,24},{18,... | collective-permute-start | bytes 3145736 | tf_op jit(solution)/shard_map/ppermute | solution.py:577
  14.8 4.3 %collective-permute-start = (f32[26,512]{1,0:T(8,128)S(1)}, f32[26,512]{1,0:T(8,128)S(1)}, u32[]{:S(2)}, u32[]{:S(2)}) collective-permute-start(f32[26,512]{1,0:T(8,128)S(1)} %get-tuple-element.34), channel_id=1, source_target_pairs={{0,2},{2,0},{4,6},{6,4},{8,10},{10,8},{12,14},{14,12},{16,18},{18,... | collective-permute-start | bytes 159752 | tf_op jit(solution)/shard_map/ppermute | solution.py:28
  16.4 5.0 %collective-permute-start.1 = (f32[26,512]{1,0:T(8,128)S(1)}, f32[26,512]{1,0:T(8,128)S(1)}, u32[]{:S(2)}, u32[]{:S(2)}) collective-permute-start(f32[26,512]{1,0:T(8,128)S(1)} %get-tuple-element.35), channel_id=1, source_target_pairs={{0,4},{2,6},{4,0},{6,2},{8,12},{10,14},{12,8},{14,10},{16,20},{18,... | collective-permute-start | bytes 159752 | tf_op jit(solution)/shard_map/ppermute | solution.py:28
  17.9 5.2 %collective-permute-start.2 = (f32[26,512]{1,0:T(8,128)S(1)}, f32[26,512]{1,0:T(8,128)S(1)}, u32[]{:S(2)}, u32[]{:S(2)}) collective-permute-start(f32[26,512]{1,0:T(8,128)S(1)} %get-tuple-element.36), channel_id=1, source_target_pairs={{0,6},{2,4},{4,2},{6,0},{8,14},{10,12},{12,10},{14,8},{16,22},{18,... | collective-permute-start | bytes 159752 | tf_op jit(solution)/shard_map/ppermute | solution.py:28
  23.7 8.3 %collective-permute-start.5 = (f32[26,512]{1,0:T(8,128)S(1)}, f32[26,512]{1,0:T(8,128)S(1)}, u32[]{:S(2)}, u32[]{:S(2)}) collective-permute-start(f32[26,512]{1,0:T(8,128)S(1)} %get-tuple-element.37.whole), channel_id=1, source_target_pairs={{0,24},{2,26},{4,28},{6,30},{1,25},{3,27},{5,29},{7,31}} | collective-permute-start | bytes 159752 | tf_op jit(solution)/shard_map/ppermute | solution.py:40
  27.0 5.7 %collective-permute-start.4 = (f32[26,512]{1,0:T(8,128)S(1)}, f32[26,512]{1,0:T(8,128)S(1)}, u32[]{:S(2)}, u32[]{:S(2)}) collective-permute-start(f32[26,512]{1,0:T(8,128)S(1)} %get-tuple-element.37.whole), channel_id=1, source_target_pairs={{0,16},{2,18},{4,20},{6,22},{8,24},{10,26},{12,28},{14,30},{1,17},... | collective-permute-start | bytes 159752 | tf_op jit(solution)/shard_map/ppermute | solution.py:40
  28.3 5.1 %collective-permute-start.3 = (f32[26,512]{1,0:T(8,128)S(1)}, f32[26,512]{1,0:T(8,128)S(1)}, u32[]{:S(2)}, u32[]{:S(2)}) collective-permute-start(f32[26,512]{1,0:T(8,128)S(1)} %get-tuple-element.37.whole), channel_id=1, source_target_pairs={{0,8},{2,10},{4,12},{6,14},{8,16},{10,18},{12,20},{14,22},{16,24},... | collective-permute-start | bytes 159752 | tf_op jit(solution)/shard_map/ppermute | solution.py:40
  34.1 28.7 %collective-permute-start.17 = (bf16[2048,256]{1,0:T(8,128)(2,1)}, bf16[2048,256]{1,0:T(8,128)(2,1)S(1)}, u32[]{:S(2)}, u32[]{:S(2)}) collective-permute-start(bf16[2048,256]{1,0:T(8,128)(2,1)} %collective-permute-done.15.refs_7_.refs_9_), channel_id=1, source_target_pairs={{8,16},{10,18},{12,20},{14,22},{16,8},{18,10},{20,12},{22,14},{9,1... | collective-permute-start | bytes 3145736 | tf_op jit(solution)/shard_map/ppermute | solution.py:577
  34.8 27.9 %collective-permute-start.18 = (bf16[2048,256]{1,0:T(8,128)(2,1)}, bf16[2048,256]{1,0:T(8,128)(2,1)S(1)}, u32[]{:S(2)}, u32[]{:S(2)}) collective-permute-start(bf16[2048,256]{1,0:T(8,128)(2,1)} %collective-permute-done.16.refs_12_), channel_id=1, source_target_pairs={{8,0},{10,2},{12,4},{14,6},{16,24},{18,26},{20,28},{22,30},{9,1},{... | collective-permute-start | bytes 3145736 | tf_op jit(solution)/shard_map/ppermute | solution.py:577
  36.1 4.6 %collective-permute-start.6 = (f32[22,512]{1,0:T(8,128)S(1)}, f32[22,512]{1,0:T(8,128)S(1)}, u32[]{:S(2)}, u32[]{:S(2)}) collective-permute-start(f32[22,512]{1,0:T(8,128)S(1)} %get-tuple-element.43), channel_id=1, source_target_pairs={{0,2},{2,0},{4,6},{6,4},{8,10},{10,8},{12,14},{14,12},{16,18},{18,... | collective-permute-start | bytes 135176 | tf_op jit(solution)/shard_map/ppermute | solution.py:28
  37.7 4.4 %collective-permute-start.7 = (f32[22,512]{1,0:T(8,128)S(1)}, f32[22,512]{1,0:T(8,128)S(1)}, u32[]{:S(2)}, u32[]{:S(2)}) collective-permute-start(f32[22,512]{1,0:T(8,128)S(1)} %get-tuple-element.44), channel_id=1, source_target_pairs={{0,4},{2,6},{4,0},{6,2},{8,12},{10,14},{12,8},{14,10},{16,20},{18,... | collective-permute-start | bytes 135176 | tf_op jit(solution)/shard_map/ppermute | solution.py:28
  39.2 5.0 %collective-permute-start.8 = (f32[22,512]{1,0:T(8,128)S(1)}, f32[22,512]{1,0:T(8,128)S(1)}, u32[]{:S(2)}, u32[]{:S(2)}) collective-permute-start(f32[22,512]{1,0:T(8,128)S(1)} %get-tuple-element.45), channel_id=1, source_target_pairs={{0,6},{2,4},{4,2},{6,0},{8,14},{10,12},{12,10},{14,8},{16,22},{18,... | collective-permute-start | bytes 135176 | tf_op jit(solution)/shard_map/ppermute | solution.py:28
  47.8 14.9 %collective-permute-start.11 = (bf16[256,1024]{1,0:T(8,128)(2,1)S(1)}, bf16[256,1024]{1,0:T(8,128)(2,1)S(1)}, u32[]{:S(2)}, u32[]{:S(2)}) collective-permute-start(bf16[256,1024]{1,0:T(8,128)(2,1)S(1)} %hidden_rows.2.refs_0_), channel_id=1, source_target_pairs={{0,4},{2,6},{4,0},{6,2},{8,12},{10,14},{12,8},{14,10},{16,20},{18,... | collective-permute-start | bytes 1572872 | tf_op jit(solution)/shard_map/ppermute | solution.py:28
  48.4 14.4 %collective-permute-start.9 = (bf16[256,1024]{1,0:T(8,128)(2,1)S(1)}, bf16[256,1024]{1,0:T(8,128)(2,1)S(1)}, u32[]{:S(2)}, u32[]{:S(2)}) collective-permute-start(bf16[256,1024]{1,0:T(8,128)(2,1)S(1)} %hidden_rows.2.refs_0_), channel_id=1, source_target_pairs={{0,2},{2,0},{4,6},{6,4},{8,10},{10,8},{12,14},{14,12},{16,18},{18,... | collective-permute-start | bytes 1572872 | tf_op jit(solution)/shard_map/ppermute | solution.py:28
  52.6 21.4 %collective-permute-start.12 = (bf16[256,1024]{1,0:T(8,128)(2,1)S(1)}, bf16[256,1024]{1,0:T(8,128)(2,1)S(1)}, u32[]{:S(2)}, u32[]{:S(2)}) collective-permute-start(bf16[256,1024]{1,0:T(8,128)(2,1)S(1)} %hidden_rows.3.refs_1_), channel_id=1, source_target_pairs={{0,4},{2,6},{4,0},{6,2},{8,12},{10,14},{12,8},{14,10},{16,20},{18,... | collective-permute-start | bytes 1572872 | tf_op jit(solution)/shard_map/ppermute | solution.py:28
  62.8 23.0 %collective-permute-start.19 = (bf16[2048,256]{1,0:T(8,128)(2,1)S(1)}, bf16[2048,256]{1,0:T(8,128)(2,1)S(1)}, u32[]{:S(2)}, u32[]{:S(2)}) collective-permute-start(bf16[2048,256]{1,0:T(8,128)(2,1)S(1)} %collective-permute-done.17.refs_8_.refs_10_), channel_id=1, source_target_pairs={{8,0},{10,2},{12,4},{14,6},{16,24},{18,26},{20,28},{22,30},{9,1},{... | collective-permute-start | bytes 3145736 | tf_op jit(solution)/shard_map/ppermute | solution.py:577
  64.1 14.3 %collective-permute-start.10 = (bf16[256,1024]{1,0:T(8,128)(2,1)S(1)}, bf16[256,1024]{1,0:T(8,128)(2,1)S(1)}, u32[]{:S(2)}, u32[]{:S(2)}) collective-permute-start(bf16[256,1024]{1,0:T(8,128)(2,1)S(1)} %hidden_rows.3.refs_1_), channel_id=1, source_target_pairs={{0,2},{2,0},{4,6},{6,4},{8,10},{10,8},{12,14},{14,12},{16,18},{18,... | collective-permute-start | bytes 1572872 | tf_op jit(solution)/shard_map/ppermute | solution.py:28
  65.0 17.3 %collective-permute-start.13 = (bf16[256,1024]{1,0:T(8,128)(2,1)S(1)}, bf16[256,1024]{1,0:T(8,128)(2,1)S(1)}, u32[]{:S(2)}, u32[]{:S(2)}) collective-permute-start(bf16[256,1024]{1,0:T(8,128)(2,1)S(1)} %collective-permute-done.9.refs_2_), channel_id=1, source_target_pairs={{0,4},{2,6},{4,0},{6,2},{8,12},{10,14},{12,8},{14,10},{16,20},{18,... | collective-permute-start | bytes 1572872 | tf_op jit(solution)/shard_map/ppermute | solution.py:28
  74.0 11.3 %collective-permute-start.14 = (bf16[256,1024]{1,0:T(8,128)(2,1)S(1)}, bf16[256,1024]{1,0:T(8,128)(2,1)S(1)}, u32[]{:S(2)}, u32[]{:S(2)}) collective-permute-start(bf16[256,1024]{1,0:T(8,128)(2,1)S(1)} %collective-permute-done.12.refs_5_), channel_id=1, source_target_pairs={{0,2},{2,0},{4,6},{6,4},{8,10},{10,8},{12,14},{14,12},{16,18},{18,... | collective-permute-start | bytes 1572872 | tf_op jit(solution)/shard_map/ppermute | solution.py:28
  89.7 2.7 %collective-permute-start.20 = (bf16[1024,512]{1,0:T(8,128)(2,1)S(1)}, bf16[1024,512]{1,0:T(8,128)(2,1)S(1)}, u32[]{:S(2)}, u32[]{:S(2)}) collective-permute-start(bf16[1024,512]{1,0:T(8,128)(2,1)S(1)} %get-tuple-element.52), channel_id=1, source_target_pairs={{0,1},{1,0},{2,3},{3,2},{4,5},{5,4},{6,7},{7,6},{8,9},{9,8},{10,11... | collective-permute-start | bytes 3145736 | tf_op jit(solution)/shard_map/ppermute | solution.py:630
  92.7 9.2 %collective-permute-start.21 = (bf16[256,512]{1,0:T(8,128)(2,1)S(1)}, bf16[256,512]{1,0:T(8,128)(2,1)S(1)}, u32[]{:S(2)}, u32[]{:S(2)}) collective-permute-start(bf16[256,512]{1,0:T(8,128)(2,1)S(1)} %get-tuple-element.54), channel_id=1, source_target_pairs={{0,2},{2,0},{4,6},{6,4},{8,10},{10,8},{12,14},{14,12},{16,18},{18,... | collective-permute-start | bytes 786440 | tf_op jit(solution)/shard_map/ppermute | solution.py:28
  94.3 13.7 %collective-permute-start.22 = (bf16[256,512]{1,0:T(8,128)(2,1)S(1)}, bf16[256,512]{1,0:T(8,128)(2,1)S(1)}, u32[]{:S(2)}, u32[]{:S(2)}) collective-permute-start(bf16[256,512]{1,0:T(8,128)(2,1)S(1)} %get-tuple-element.55), channel_id=1, source_target_pairs={{0,4},{2,6},{4,0},{6,2},{8,12},{10,14},{12,8},{14,10},{16,20},{18,... | collective-permute-start | bytes 786440 | tf_op jit(solution)/shard_map/ppermute | solution.py:28
  95.8 12.2 %collective-permute-start.23 = (bf16[256,512]{1,0:T(8,128)(2,1)S(1)}, bf16[256,512]{1,0:T(8,128)(2,1)S(1)}, u32[]{:S(2)}, u32[]{:S(2)}) collective-permute-start(bf16[256,512]{1,0:T(8,128)(2,1)S(1)} %get-tuple-element.56), channel_id=1, source_target_pairs={{0,6},{2,4},{4,2},{6,0},{8,14},{10,12},{12,10},{14,8},{16,22},{18,... | collective-permute-start | bytes 786440 | tf_op jit(solution)/shard_map/ppermute | solution.py:28
  (6 other events, 143.1 us)

commit v4 on v3

--- a/solution.py
+++ b/solution.py
@@ -507,9 +507,11 @@
         outs[0][:made] = near[...]
         outs[1][:made, :width] = far_first[...]
         columns = [given[0 if middle else -1] for given in blocks]
-        for slot, block in enumerate(columns):
-            far, at = divmod(slot, 2)
-            times_into(rows[-1:], block, outs[far].at[pl.ds(made, outs[far].shape[0] - made)], at * width)
+        joined = jnp.concatenate([piece[...] for piece in rows[-1]], axis=1)
+        together = jnp.concatenate([block[...] for block in columns], axis=1)
+        total = jnp.dot(joined, together, preferred_element_type=jnp.float32).astype(kept.dtype)
+        outs[0][made:] = total[:, : 2 * width]
+        outs[1][made:] = total[:, 2 * width :]
         times_into(rows[:-1], columns[3], outs[1], width)
 
     for keeps in (0, 1):

time: 110 us -> 110 us (level)
  no operation moved by 1% of the time
where the time goes in v4:
time: 110 us
  waiting for transfers between devices  49.5 us (45%)
  starting transfers between devices  33.6 us (31%)
  Pallas kernels  24.4 us (22%)
  local copies, waits for them, and re-layouts  1.81 us (2%)
    ppermute x15, waiting for transfers between devices, send_xor(): return lax.ppermute(value, 'ctx', pairs)  43.6 us
    ppermute x15, starting transfers between devices, send_xor(): return lax.ppermute(value, 'ctx', pairs)  16.4 us
    ppermute x5, starting transfers between devices, send_planes(): return lax.ppermute(value, 'ctx', pairs)  10.1 us
    pallas_call x2, Pallas kernels, project(): pl.pallas_call(functools.partial(near_body if len(slots) == 3 else projec...  7.84 us
    pallas_call x2, Pallas kernels, hidden_rows(): pl.pallas_call(functools.partial(hidden_body, seg_len=seg_len, order=orde...  7.21 us
    ppermute x3, starting transfers between devices, send_along(): return lax.ppermute(value, 'ctx', pairs)  7.02 us
    pallas_call x1, Pallas kernels, local_scan(): pl.pallas_call(functools.partial(local_scan_body, seg_len=seg_len, order=...  6.12 us
    ppermute x1, waiting for transfers between devices, project_4x4(): mixed = add_up(kept, lax.ppermute(sent, 'tp', [(0, 1), (1, 0)]), group)  2.65 us
  transfers between devices with their start and end apart: 24, of which 17 were waited for; matrix products, arithmetic and copies ran while one was open for 0% of the time, Pallas kernels for 17%

profile of v4, /device:TPU:0, one launch (start us, length us, event | category | flops | bytes accessed | tf_op | source)
XLA Modules:
  0.0 109.6 jit_solution(5573053867142757689)
XLA Ops:
  0.0 1.8 %collective-permute-start.16 = (bf16[2048,256]{1,0:T(8,128)(2,1)}, bf16[2048,256]{1,0:T(8,128)(2,1)}, u32[]{:S(2)}, u32[]{:S(2)}) collective-permute-start(bf16[2048,256]{1,0:T(8,128)(2,1)} %refs_8_.1), channel_id=1, source_target_pairs={{8,16},{10,18},{12,20},{14,22},{16,8},{18,10},{20,12},{22,14},{9,1... | collective-permute-start | bytes 3145736 | tf_op jit(solution)/shard_map/ppermute | solution.py:579
  1.8 5.1 %collective-permute-start.15 = (bf16[2048,256]{1,0:T(8,128)(2,1)}, bf16[2048,256]{1,0:T(8,128)(2,1)}, u32[]{:S(2)}, u32[]{:S(2)}) collective-permute-start(bf16[2048,256]{1,0:T(8,128)(2,1)} %refs_8_.1), channel_id=1, source_target_pairs={{0,8},{2,10},{4,12},{6,14},{8,0},{10,2},{12,4},{14,6},{16,24},{18,... | collective-permute-start | bytes 3145736 | tf_op jit(solution)/shard_map/ppermute | solution.py:579
  8.7 6.1 %local_scan.1 = (f32[26,512]{1,0:T(8,128)S(1)}, f32[26,512]{1,0:T(8,128)S(1)}, f32[26,512]{1,0:T(8,128)S(1)}, f32[26,512]{1,0:T(8,128)S(1)}, f32[16,256,128]{2,1...) custom-call(s32[4]{0:T(128)S(1)} %pad_add_fusion.place, bf16[3,256,2048]{2,1,0:T(8,128)(2,1)} %bitcast.9, ...), custom_call_target="tpu_custom_call" | custom-call | flops 26214400 | bytes 5242880 | tf_op jit(solution)/shard_map/local_scan/pallas_call | solution.py:200
  14.8 1.6 %collective-permute-start = (f32[26,512]{1,0:T(8,128)S(1)}, f32[26,512]{1,0:T(8,128)S(1)}, u32[]{:S(2)}, u32[]{:S(2)}) collective-permute-start(f32[26,512]{1,0:T(8,128)S(1)} %get-tuple-element.34), channel_id=1, source_target_pairs={{0,2},{2,0},{4,6},{6,4},{8,10},{10,8},{12,14},{14,12},{16,18},{18,... | collective-permute-start | bytes 159752 | tf_op jit(solution)/shard_map/ppermute | solution.py:28
  19.2 2.2 %collective-permute-done.1.rest_2_ = f32[26,512]{1,0:T(8,128)S(1)} collective-permute-done((f32[26,512]{1,0:T(8,128)S(1)}, f32[26,512]{1,0:T(8,128)S(1)}, u32[]{:S(2)}, u32[]{:S(2)}) %collective-permute-start.1) | collective-permute-done | bytes 53280 | tf_op jit(solution)/shard_map/ppermute | solution.py:28
  21.4 1.7 %collective-permute-done.2.rest_3_ = f32[26,512]{1,0:T(8,128)S(1)} collective-permute-done((f32[26,512]{1,0:T(8,128)S(1)}, f32[26,512]{1,0:T(8,128)S(1)}, u32[]{:S(2)}, u32[]{:S(2)}) %collective-permute-start.2) | collective-permute-done | bytes 53280 | tf_op jit(solution)/shard_map/ppermute | solution.py:28
  23.7 3.3 %collective-permute-start.5 = (f32[26,512]{1,0:T(8,128)S(1)}, f32[26,512]{1,0:T(8,128)S(1)}, u32[]{:S(2)}, u32[]{:S(2)}) collective-permute-start(f32[26,512]{1,0:T(8,128)S(1)} %get-tuple-element.37.whole), channel_id=1, source_target_pairs={{0,24},{2,26},{4,28},{6,30},{1,25},{3,27},{5,29},{7,31}} | collective-permute-start | bytes 159752 | tf_op jit(solution)/shard_map/ppermute | solution.py:40
  28.3 2.5 %collective-permute-start.3 = (f32[26,512]{1,0:T(8,128)S(1)}, f32[26,512]{1,0:T(8,128)S(1)}, u32[]{:S(2)}, u32[]{:S(2)}) collective-permute-start(f32[26,512]{1,0:T(8,128)S(1)} %get-tuple-element.37.whole), channel_id=1, source_target_pairs={{0,8},{2,10},{4,12},{6,14},{8,16},{10,18},{12,20},{14,22},{16,24},... | collective-permute-start | bytes 159752 | tf_op jit(solution)/shard_map/ppermute | solution.py:40
  36.1 1.6 %collective-permute-start.6 = (f32[22,512]{1,0:T(8,128)S(1)}, f32[22,512]{1,0:T(8,128)S(1)}, u32[]{:S(2)}, u32[]{:S(2)}) collective-permute-start(f32[22,512]{1,0:T(8,128)S(1)} %get-tuple-element.43), channel_id=1, source_target_pairs={{0,2},{2,0},{4,6},{6,4},{8,10},{10,8},{12,14},{14,12},{16,18},{18,... | collective-permute-start | bytes 135176 | tf_op jit(solution)/shard_map/ppermute | solution.py:28
  42.1 2.1 %collective-permute-done.8.rest_3_ = f32[22,512]{1,0:T(8,128)S(1)} collective-permute-done((f32[22,512]{1,0:T(8,128)S(1)}, f32[22,512]{1,0:T(8,128)S(1)}, u32[]{:S(2)}, u32[]{:S(2)}) %collective-permute-start.8) | collective-permute-done | bytes 45088 | tf_op jit(solution)/shard_map/ppermute | solution.py:28
  44.2 3.6 %hidden_rows.2.refs_0_ = bf16[256,1024]{1,0:T(8,128)(2,1)S(1)} custom-call(s32[4]{0:T(128)S(1)} %pad_add_fusion.place, bf16[3,256,2048]{2,1,0:T(8,128)(2,1)S(1)} %bitcast.10, bf16[3,256,2048]{2,1,0:T(8,128)(2,1)S(1)} %bitcast.11, f32[3,3,2048]{2,1,0:T(4,128)S(1)} %copy-done.2, f32[16,2048]{1,0:T(8,128)S(1)} %bitcast.17, ...), custom_call_target="tpu_custom_call" | custom-call | flops 20971520 | bytes 2621440 | tf_op jit(solution)/shard_map/hidden_rows/pallas_call | solution.py:434
  48.9 3.6 %hidden_rows.3.refs_1_ = bf16[256,1024]{1,0:T(8,128)(2,1)S(1)} custom-call(s32[4]{0:T(128)S(1)} %pad_add_fusion.place, bf16[3,256,2048]{2,1,0:T(8,128)(2,1)S(1)} %bitcast.12, bf16[3,256,2048]{2,1,0:T(8,128)(2,1)S(1)} %bitcast.13, f32[3,3,2048]{2,1,0:T(4,128)S(1)} %copy-done.2, f32[16,2048]{1,0:T(8,128)S(1)} %bitcast.18, ...), custom_call_target="tpu_custom_call" | custom-call | flops 20971520 | bytes 2621440 | tf_op jit(solution)/shard_map/hidden_rows/pallas_call | solution.py:434
  52.6 1.6 %collective-permute-start.12 = (bf16[256,1024]{1,0:T(8,128)(2,1)S(1)}, bf16[256,1024]{1,0:T(8,128)(2,1)S(1)}, u32[]{:S(2)}, u32[]{:S(2)}) collective-permute-start(bf16[256,1024]{1,0:T(8,128)(2,1)S(1)} %hidden_rows.3.refs_1_), channel_id=1, source_target_pairs={{0,4},{2,6},{4,0},{6,2},{8,12},{10,14},{12,8},{14,10},{16,20},{18,... | collective-permute-start | bytes 1572872 | tf_op jit(solution)/shard_map/ppermute | solution.py:28
  54.1 8.6 %collective-permute-done.11.refs_4_ = bf16[256,1024]{1,0:T(8,128)(2,1)S(1)} collective-permute-done((bf16[256,1024]{1,0:T(8,128)(2,1)S(1)}, bf16[256,1024]{1,0:T(8,128)(2,1)S(1)}, u32[]{:S(2)}, u32[]{:S(2)}) %collective-permute-start.11) | collective-permute-done | bytes 524320 | tf_op jit(solution)/shard_map/ppermute | solution.py:28
  66.6 7.4 %collective-permute-done.12.refs_5_ = bf16[256,1024]{1,0:T(8,128)(2,1)S(1)} collective-permute-done((bf16[256,1024]{1,0:T(8,128)(2,1)S(1)}, bf16[256,1024]{1,0:T(8,128)(2,1)S(1)}, u32[]{:S(2)}, u32[]{:S(2)}) %collective-permute-start.12) | collective-permute-done | bytes 524320 | tf_op jit(solution)/shard_map/ppermute | solution.py:28
  74.5 3.9 %collective-permute-done.10.refs_3_ = bf16[256,1024]{1,0:T(8,128)(2,1)S(1)} collective-permute-done((bf16[256,1024]{1,0:T(8,128)(2,1)S(1)}, bf16[256,1024]{1,0:T(8,128)(2,1)S(1)}, u32[]{:S(2)}, u32[]{:S(2)}) %collective-permute-start.10) | collective-permute-done | bytes 524320 | tf_op jit(solution)/shard_map/ppermute | solution.py:28
  78.4 3.9 %project.2 = (bf16[768,512]{1,0:T(8,128)(2,1)S(1)}, bf16[768,256]{1,0:T(8,128)(2,1)S(1)}) custom-call(s32[4]{0:T(128)S(1)} %pad_add_fusion.place, bf16[256,1024]{1,0:T(8,128)(2,1)S(1)} %hidden_rows.2.refs_0_, bf16[256,1024]{1,0:T(8,128)(2,1)S(1)} %hidden_rows.3.refs_1_, bf16[256,1024]{1,0:T(8,128)(2,1)S(1)} %collective-permute-done.9.refs_2_, ...), custom_call_target="tpu_custom_call" | custom-call | flops 2415919104 | bytes 7471104 | tf_op jit(solution)/shard_map/project/pallas_call | solution.py:530
  82.3 3.0 %collective-permute-done.14.refs_7_ = bf16[256,1024]{1,0:T(8,128)(2,1)S(1)} collective-permute-done((bf16[256,1024]{1,0:T(8,128)(2,1)S(1)}, bf16[256,1024]{1,0:T(8,128)(2,1)S(1)}, u32[]{:S(2)}, u32[]{:S(2)}) %collective-permute-start.14) | collective-permute-done | bytes 524320 | tf_op jit(solution)/shard_map/ppermute | solution.py:28
  85.8 3.9 %project.3 = (bf16[1024,512]{1,0:T(8,128)(2,1)S(1)}, bf16[1024,512]{1,0:T(8,128)(2,1)S(1)}) custom-call(s32[4]{0:T(128)S(1)} %pad_add_fusion.place, bf16[256,1024]{1,0:T(8,128)(2,1)S(1)} %hidden_rows.2.refs_0_, bf16[256,1024]{1,0:T(8,128)(2,1)S(1)} %hidden_rows.3.refs_1_, bf16[256,1024]{1,0:T(8,128)(2,1)S(1)} %collective-permute-done.9.refs_2_, ...), custom_call_target="tpu_custom_call" | custom-call | flops 4294967296 | bytes 10485760 | tf_op jit(solution)/shard_map/project/pallas_call | solution.py:530
  89.8 2.6 %collective-permute-done.20.b = bf16[1024,512]{1,0:T(8,128)(2,1)S(1)} collective-permute-done((bf16[1024,512]{1,0:T(8,128)(2,1)S(1)}, bf16[1024,512]{1,0:T(8,128)(2,1)S(1)}, u32[]{:S(2)}, u32[]{:S(2)}) %collective-permute-start.20) | collective-permute-done | bytes 1048608 | tf_op jit(solution)/shard_map/ppermute | solution.py:632
  92.7 1.6 %collective-permute-start.21 = (bf16[256,512]{1,0:T(8,128)(2,1)S(1)}, bf16[256,512]{1,0:T(8,128)(2,1)S(1)}, u32[]{:S(2)}, u32[]{:S(2)}) collective-permute-start(bf16[256,512]{1,0:T(8,128)(2,1)S(1)} %get-tuple-element.54), channel_id=1, source_target_pairs={{0,2},{2,0},{4,6},{6,4},{8,10},{10,8},{12,14},{14,12},{16,18},{18,... | collective-permute-start | bytes 786440 | tf_op jit(solution)/shard_map/ppermute | solution.py:28
  96.3 5.7 %collective-permute-done.21.refs_1_ = bf16[256,512]{1,0:T(8,128)(2,1)S(1)} collective-permute-done((bf16[256,512]{1,0:T(8,128)(2,1)S(1)}, bf16[256,512]{1,0:T(8,128)(2,1)S(1)}, u32[]{:S(2)}, u32[]{:S(2)}) %collective-permute-start.21) | collective-permute-done | bytes 262176 | tf_op jit(solution)/shard_map/ppermute | solution.py:28
  101.9 6.0 %collective-permute-done.22.refs_2_ = bf16[256,512]{1,0:T(8,128)(2,1)S(1)} collective-permute-done((bf16[256,512]{1,0:T(8,128)(2,1)S(1)}, bf16[256,512]{1,0:T(8,128)(2,1)S(1)}, u32[]{:S(2)}, u32[]{:S(2)}) %collective-permute-start.22) | collective-permute-done | bytes 262176 | tf_op jit(solution)/shard_map/ppermute | solution.py:28
  108.0 1.7 %assemble.1 = bf16[256,2048]{1,0:T(8,128)(2,1)} custom-call(s32[4]{0:T(128)S(1)} %pad_add_fusion.place, bf16[256,512]{1,0:T(8,128)(2,1)S(1)} %get-tuple-element.53.refs_0_, bf16[256,512]{1,0:T(8,128)(2,1)S(1)} %collective-permute-done.21.refs_1_, bf16[256,512]{1,0:T(8,128)(2,1)S(1)} %collective-permute-done.22.refs_2_, ...), custom_call_target="tpu_custom_call" | custom-call | bytes 2097152 | tf_op jit(solution)/shard_map/assemble/pallas_call | solution.py:562
  (47 shorter events, 24.6 us)
Async XLA Ops:
  0.0 34.1 %collective-permute-start.16 = (bf16[2048,256]{1,0:T(8,128)(2,1)}, bf16[2048,256]{1,0:T(8,128)(2,1)}, u32[]{:S(2)}, u32[]{:S(2)}) collective-permute-start(bf16[2048,256]{1,0:T(8,128)(2,1)} %refs_8_.1), channel_id=1, source_target_pairs={{8,16},{10,18},{12,20},{14,22},{16,8},{18,10},{20,12},{22,14},{9,1... | collective-permute-start | bytes 3145736 | tf_op jit(solution)/shard_map/ppermute | solution.py:579
  1.8 32.3 %collective-permute-start.15 = (bf16[2048,256]{1,0:T(8,128)(2,1)}, bf16[2048,256]{1,0:T(8,128)(2,1)}, u32[]{:S(2)}, u32[]{:S(2)}) collective-permute-start(bf16[2048,256]{1,0:T(8,128)(2,1)} %refs_8_.1), channel_id=1, source_target_pairs={{0,8},{2,10},{4,12},{6,14},{8,0},{10,2},{12,4},{14,6},{16,24},{18,... | collective-permute-start | bytes 3145736 | tf_op jit(solution)/shard_map/ppermute | solution.py:579
  14.8 4.3 %collective-permute-start = (f32[26,512]{1,0:T(8,128)S(1)}, f32[26,512]{1,0:T(8,128)S(1)}, u32[]{:S(2)}, u32[]{:S(2)}) collective-permute-start(f32[26,512]{1,0:T(8,128)S(1)} %get-tuple-element.34), channel_id=1, source_target_pairs={{0,2},{2,0},{4,6},{6,4},{8,10},{10,8},{12,14},{14,12},{16,18},{18,... | collective-permute-start | bytes 159752 | tf_op jit(solution)/shard_map/ppermute | solution.py:28
  16.4 5.0 %collective-permute-start.1 = (f32[26,512]{1,0:T(8,128)S(1)}, f32[26,512]{1,0:T(8,128)S(1)}, u32[]{:S(2)}, u32[]{:S(2)}) collective-permute-start(f32[26,512]{1,0:T(8,128)S(1)} %get-tuple-element.35), channel_id=1, source_target_pairs={{0,4},{2,6},{4,0},{6,2},{8,12},{10,14},{12,8},{14,10},{16,20},{18,... | collective-permute-start | bytes 159752 | tf_op jit(solution)/shard_map/ppermute | solution.py:28
  17.9 5.2 %collective-permute-start.2 = (f32[26,512]{1,0:T(8,128)S(1)}, f32[26,512]{1,0:T(8,128)S(1)}, u32[]{:S(2)}, u32[]{:S(2)}) collective-permute-start(f32[26,512]{1,0:T(8,128)S(1)} %get-tuple-element.36), channel_id=1, source_target_pairs={{0,6},{2,4},{4,2},{6,0},{8,14},{10,12},{12,10},{14,8},{16,22},{18,... | collective-permute-start | bytes 159752 | tf_op jit(solution)/shard_map/ppermute | solution.py:28
  23.7 8.3 %collective-permute-start.5 = (f32[26,512]{1,0:T(8,128)S(1)}, f32[26,512]{1,0:T(8,128)S(1)}, u32[]{:S(2)}, u32[]{:S(2)}) collective-permute-start(f32[26,512]{1,0:T(8,128)S(1)} %get-tuple-element.37.whole), channel_id=1, source_target_pairs={{0,24},{2,26},{4,28},{6,30},{1,25},{3,27},{5,29},{7,31}} | collective-permute-start | bytes 159752 | tf_op jit(solution)/shard_map/ppermute | solution.py:40
  27.0 5.7 %collective-permute-start.4 = (f32[26,512]{1,0:T(8,128)S(1)}, f32[26,512]{1,0:T(8,128)S(1)}, u32[]{:S(2)}, u32[]{:S(2)}) collective-permute-start(f32[26,512]{1,0:T(8,128)S(1)} %get-tuple-element.37.whole), channel_id=1, source_target_pairs={{0,16},{2,18},{4,20},{6,22},{8,24},{10,26},{12,28},{14,30},{1,17},... | collective-permute-start | bytes 159752 | tf_op jit(solution)/shard_map/ppermute | solution.py:40
  28.3 5.1 %collective-permute-start.3 = (f32[26,512]{1,0:T(8,128)S(1)}, f32[26,512]{1,0:T(8,128)S(1)}, u32[]{:S(2)}, u32[]{:S(2)}) collective-permute-start(f32[26,512]{1,0:T(8,128)S(1)} %get-tuple-element.37.whole), channel_id=1, source_target_pairs={{0,8},{2,10},{4,12},{6,14},{8,16},{10,18},{12,20},{14,22},{16,24},... | collective-permute-start | bytes 159752 | tf_op jit(solution)/shard_map/ppermute | solution.py:40
  34.1 28.7 %collective-permute-start.17 = (bf16[2048,256]{1,0:T(8,128)(2,1)}, bf16[2048,256]{1,0:T(8,128)(2,1)S(1)}, u32[]{:S(2)}, u32[]{:S(2)}) collective-permute-start(bf16[2048,256]{1,0:T(8,128)(2,1)} %collective-permute-done.15.refs_7_.refs_9_), channel_id=1, source_target_pairs={{8,16},{10,18},{12,20},{14,22},{16,8},{18,10},{20,12},{22,14},{9,1... | collective-permute-start | bytes 3145736 | tf_op jit(solution)/shard_map/ppermute | solution.py:579
  34.8 27.9 %collective-permute-start.18 = (bf16[2048,256]{1,0:T(8,128)(2,1)}, bf16[2048,256]{1,0:T(8,128)(2,1)S(1)}, u32[]{:S(2)}, u32[]{:S(2)}) collective-permute-start(bf16[2048,256]{1,0:T(8,128)(2,1)} %collective-permute-done.16.refs_12_), channel_id=1, source_target_pairs={{8,0},{10,2},{12,4},{14,6},{16,24},{18,26},{20,28},{22,30},{9,1},{... | collective-permute-start | bytes 3145736 | tf_op jit(solution)/shard_map/ppermute | solution.py:579
  36.1 4.6 %collective-permute-start.6 = (f32[22,512]{1,0:T(8,128)S(1)}, f32[22,512]{1,0:T(8,128)S(1)}, u32[]{:S(2)}, u32[]{:S(2)}) collective-permute-start(f32[22,512]{1,0:T(8,128)S(1)} %get-tuple-element.43), channel_id=1, source_target_pairs={{0,2},{2,0},{4,6},{6,4},{8,10},{10,8},{12,14},{14,12},{16,18},{18,... | collective-permute-start | bytes 135176 | tf_op jit(solution)/shard_map/ppermute | solution.py:28
  37.7 4.4 %collective-permute-start.7 = (f32[22,512]{1,0:T(8,128)S(1)}, f32[22,512]{1,0:T(8,128)S(1)}, u32[]{:S(2)}, u32[]{:S(2)}) collective-permute-start(f32[22,512]{1,0:T(8,128)S(1)} %get-tuple-element.44), channel_id=1, source_target_pairs={{0,4},{2,6},{4,0},{6,2},{8,12},{10,14},{12,8},{14,10},{16,20},{18,... | collective-permute-start | bytes 135176 | tf_op jit(solution)/shard_map/ppermute | solution.py:28
  39.2 5.0 %collective-permute-start.8 = (f32[22,512]{1,0:T(8,128)S(1)}, f32[22,512]{1,0:T(8,128)S(1)}, u32[]{:S(2)}, u32[]{:S(2)}) collective-permute-start(f32[22,512]{1,0:T(8,128)S(1)} %get-tuple-element.45), channel_id=1, source_target_pairs={{0,6},{2,4},{4,2},{6,0},{8,14},{10,12},{12,10},{14,8},{16,22},{18,... | collective-permute-start | bytes 135176 | tf_op jit(solution)/shard_map/ppermute | solution.py:28
  47.8 14.9 %collective-permute-start.11 = (bf16[256,1024]{1,0:T(8,128)(2,1)S(1)}, bf16[256,1024]{1,0:T(8,128)(2,1)S(1)}, u32[]{:S(2)}, u32[]{:S(2)}) collective-permute-start(bf16[256,1024]{1,0:T(8,128)(2,1)S(1)} %hidden_rows.2.refs_0_), channel_id=1, source_target_pairs={{0,4},{2,6},{4,0},{6,2},{8,12},{10,14},{12,8},{14,10},{16,20},{18,... | collective-permute-start | bytes 1572872 | tf_op jit(solution)/shard_map/ppermute | solution.py:28
  48.4 14.4 %collective-permute-start.9 = (bf16[256,1024]{1,0:T(8,128)(2,1)S(1)}, bf16[256,1024]{1,0:T(8,128)(2,1)S(1)}, u32[]{:S(2)}, u32[]{:S(2)}) collective-permute-start(bf16[256,1024]{1,0:T(8,128)(2,1)S(1)} %hidden_rows.2.refs_0_), channel_id=1, source_target_pairs={{0,2},{2,0},{4,6},{6,4},{8,10},{10,8},{12,14},{14,12},{16,18},{18,... | collective-permute-start | bytes 1572872 | tf_op jit(solution)/shard_map/ppermute | solution.py:28
  52.6 21.4 %collective-permute-start.12 = (bf16[256,1024]{1,0:T(8,128)(2,1)S(1)}, bf16[256,1024]{1,0:T(8,128)(2,1)S(1)}, u32[]{:S(2)}, u32[]{:S(2)}) collective-permute-start(bf16[256,1024]{1,0:T(8,128)(2,1)S(1)} %hidden_rows.3.refs_1_), channel_id=1, source_target_pairs={{0,4},{2,6},{4,0},{6,2},{8,12},{10,14},{12,8},{14,10},{16,20},{18,... | collective-permute-start | bytes 1572872 | tf_op jit(solution)/shard_map/ppermute | solution.py:28
  62.8 23.0 %collective-permute-start.19 = (bf16[2048,256]{1,0:T(8,128)(2,1)S(1)}, bf16[2048,256]{1,0:T(8,128)(2,1)S(1)}, u32[]{:S(2)}, u32[]{:S(2)}) collective-permute-start(bf16[2048,256]{1,0:T(8,128)(2,1)S(1)} %collective-permute-done.17.refs_8_.refs_10_), channel_id=1, source_target_pairs={{8,0},{10,2},{12,4},{14,6},{16,24},{18,26},{20,28},{22,30},{9,1},{... | collective-permute-start | bytes 3145736 | tf_op jit(solution)/shard_map/ppermute | solution.py:579
  64.1 14.3 %collective-permute-start.10 = (bf16[256,1024]{1,0:T(8,128)(2,1)S(1)}, bf16[256,1024]{1,0:T(8,128)(2,1)S(1)}, u32[]{:S(2)}, u32[]{:S(2)}) collective-permute-start(bf16[256,1024]{1,0:T(8,128)(2,1)S(1)} %hidden_rows.3.refs_1_), channel_id=1, source_target_pairs={{0,2},{2,0},{4,6},{6,4},{8,10},{10,8},{12,14},{14,12},{16,18},{18,... | collective-permute-start | bytes 1572872 | tf_op jit(solution)/shard_map/ppermute | solution.py:28
  65.0 17.3 %collective-permute-start.13 = (bf16[256,1024]{1,0:T(8,128)(2,1)S(1)}, bf16[256,1024]{1,0:T(8,128)(2,1)S(1)}, u32[]{:S(2)}, u32[]{:S(2)}) collective-permute-start(bf16[256,1024]{1,0:T(8,128)(2,1)S(1)} %collective-permute-done.9.refs_2_), channel_id=1, source_target_pairs={{0,4},{2,6},{4,0},{6,2},{8,12},{10,14},{12,8},{14,10},{16,20},{18,... | collective-permute-start | bytes 1572872 | tf_op jit(solution)/shard_map/ppermute | solution.py:28
  74.0 11.3 %collective-permute-start.14 = (bf16[256,1024]{1,0:T(8,128)(2,1)S(1)}, bf16[256,1024]{1,0:T(8,128)(2,1)S(1)}, u32[]{:S(2)}, u32[]{:S(2)}) collective-permute-start(bf16[256,1024]{1,0:T(8,128)(2,1)S(1)} %collective-permute-done.12.refs_5_), channel_id=1, source_target_pairs={{0,2},{2,0},{4,6},{6,4},{8,10},{10,8},{12,14},{14,12},{16,18},{18,... | collective-permute-start | bytes 1572872 | tf_op jit(solution)/shard_map/ppermute | solution.py:28
  89.8 2.7 %collective-permute-start.20 = (bf16[1024,512]{1,0:T(8,128)(2,1)S(1)}, bf16[1024,512]{1,0:T(8,128)(2,1)S(1)}, u32[]{:S(2)}, u32[]{:S(2)}) collective-permute-start(bf16[1024,512]{1,0:T(8,128)(2,1)S(1)} %get-tuple-element.52), channel_id=1, source_target_pairs={{0,1},{1,0},{2,3},{3,2},{4,5},{5,4},{6,7},{7,6},{8,9},{9,8},{10,11... | collective-permute-start | bytes 3145736 | tf_op jit(solution)/shard_map/ppermute | solution.py:632
  92.7 9.2 %collective-permute-start.21 = (bf16[256,512]{1,0:T(8,128)(2,1)S(1)}, bf16[256,512]{1,0:T(8,128)(2,1)S(1)}, u32[]{:S(2)}, u32[]{:S(2)}) collective-permute-start(bf16[256,512]{1,0:T(8,128)(2,1)S(1)} %get-tuple-element.54), channel_id=1, source_target_pairs={{0,2},{2,0},{4,6},{6,4},{8,10},{10,8},{12,14},{14,12},{16,18},{18,... | collective-permute-start | bytes 786440 | tf_op jit(solution)/shard_map/ppermute | solution.py:28
  94.3 13.7 %collective-permute-start.22 = (bf16[256,512]{1,0:T(8,128)(2,1)S(1)}, bf16[256,512]{1,0:T(8,128)(2,1)S(1)}, u32[]{:S(2)}, u32[]{:S(2)}) collective-permute-start(bf16[256,512]{1,0:T(8,128)(2,1)S(1)} %get-tuple-element.55), channel_id=1, source_target_pairs={{0,4},{2,6},{4,0},{6,2},{8,12},{10,14},{12,8},{14,10},{16,20},{18,... | collective-permute-start | bytes 786440 | tf_op jit(solution)/shard_map/ppermute | solution.py:28
  95.8 12.2 %collective-permute-start.23 = (bf16[256,512]{1,0:T(8,128)(2,1)S(1)}, bf16[256,512]{1,0:T(8,128)(2,1)S(1)}, u32[]{:S(2)}, u32[]{:S(2)}) collective-permute-start(bf16[256,512]{1,0:T(8,128)(2,1)S(1)} %get-tuple-element.56), channel_id=1, source_target_pairs={{0,6},{2,4},{4,2},{6,0},{8,14},{10,12},{12,10},{14,8},{16,22},{18,... | collective-permute-start | bytes 786440 | tf_op jit(solution)/shard_map/ppermute | solution.py:28
  (6 other events, 143.1 us)

commit v5 on v4

--- a/solution.py
+++ b/solution.py
@@ -512,7 +512,10 @@
         total = jnp.dot(joined, together, preferred_element_type=jnp.float32).astype(kept.dtype)
         outs[0][made:] = total[:, : 2 * width]
         outs[1][made:] = total[:, 2 * width :]
-        times_into(rows[:-1], columns[3], outs[1], width)
+        pieces = [jnp.concatenate([part[k][...] for part in rows[:-1]], axis=0) for k in range(rows_in[0])]
+        joined = jnp.concatenate(pieces, axis=1)
+        total = jnp.dot(joined, columns[3][...], preferred_element_type=jnp.float32)
+        outs[1][:made, width:] = total.astype(kept.dtype)
 
     for keeps in (0, 1):
         for middle in (0, 1):

time: 110 us -> 110 us (level)
  no operation moved by 1% of the time
where the time goes in v5:
time: 110 us
  waiting for transfers between devices  49.5 us (45%)
  starting transfers between devices  33.6 us (31%)
  Pallas kernels  24.4 us (22%)
  local copies, waits for them, and re-layouts  1.81 us (2%)
    ppermute x15, waiting for transfers between devices, send_xor(): return lax.ppermute(value, 'ctx', pairs)  43.6 us
    ppermute x15, starting transfers between devices, send_xor(): return lax.ppermute(value, 'ctx', pairs)  16.4 us
    ppermute x5, starting transfers between devices, send_planes(): return lax.ppermute(value, 'ctx', pairs)  10.1 us
    pallas_call x2, Pallas kernels, project(): pl.pallas_call(functools.partial(near_body if len(slots) == 3 else projec...  7.83 us
    pallas_call x2, Pallas kernels, hidden_rows(): pl.pallas_call(functools.partial(hidden_body, seg_len=seg_len, order=orde...  7.21 us
    ppermute x3, starting transfers between devices, send_along(): return lax.ppermute(value, 'ctx', pairs)  7.02 us
    pallas_call x1, Pallas kernels, local_scan(): pl.pallas_call(functools.partial(local_scan_body, seg_len=seg_len, order=...  6.12 us
    ppermute x1, waiting for transfers between devices, project_4x4(): mixed = add_up(kept, lax.ppermute(sent, 'tp', [(0, 1), (1, 0)]), group)  2.65 us
  transfers between devices with their start and end apart: 24, of which 17 were waited for; matrix products, arithmetic and copies ran while one was open for 0% of the time, Pallas kernels for 17%

profile of v5, /device:TPU:0, one launch (start us, length us, event | category | flops | bytes accessed | tf_op | source)
XLA Modules:
  0.0 109.6 jit_solution(5454151524659847304)
XLA Ops:
  0.0 1.8 %collective-permute-start.16 = (bf16[2048,256]{1,0:T(8,128)(2,1)}, bf16[2048,256]{1,0:T(8,128)(2,1)}, u32[]{:S(2)}, u32[]{:S(2)}) collective-permute-start(bf16[2048,256]{1,0:T(8,128)(2,1)} %refs_8_.1), channel_id=1, source_target_pairs={{8,16},{10,18},{12,20},{14,22},{16,8},{18,10},{20,12},{22,14},{9,1... | collective-permute-start | bytes 3145736 | tf_op jit(solution)/shard_map/ppermute | solution.py:582
  1.8 5.1 %collective-permute-start.15 = (bf16[2048,256]{1,0:T(8,128)(2,1)}, bf16[2048,256]{1,0:T(8,128)(2,1)}, u32[]{:S(2)}, u32[]{:S(2)}) collective-permute-start(bf16[2048,256]{1,0:T(8,128)(2,1)} %refs_8_.1), channel_id=1, source_target_pairs={{0,8},{2,10},{4,12},{6,14},{8,0},{10,2},{12,4},{14,6},{16,24},{18,... | collective-permute-start | bytes 3145736 | tf_op jit(solution)/shard_map/ppermute | solution.py:582
  8.7 6.1 %local_scan.1 = (f32[26,512]{1,0:T(8,128)S(1)}, f32[26,512]{1,0:T(8,128)S(1)}, f32[26,512]{1,0:T(8,128)S(1)}, f32[26,512]{1,0:T(8,128)S(1)}, f32[16,256,128]{2,1...) custom-call(s32[4]{0:T(128)S(1)} %pad_add_fusion.place, bf16[3,256,2048]{2,1,0:T(8,128)(2,1)} %bitcast.9, ...), custom_call_target="tpu_custom_call" | custom-call | flops 26214400 | bytes 5242880 | tf_op jit(solution)/shard_map/local_scan/pallas_call | solution.py:200
  14.8 1.6 %collective-permute-start = (f32[26,512]{1,0:T(8,128)S(1)}, f32[26,512]{1,0:T(8,128)S(1)}, u32[]{:S(2)}, u32[]{:S(2)}) collective-permute-start(f32[26,512]{1,0:T(8,128)S(1)} %get-tuple-element.34), channel_id=1, source_target_pairs={{0,2},{2,0},{4,6},{6,4},{8,10},{10,8},{12,14},{14,12},{16,18},{18,... | collective-permute-start | bytes 159752 | tf_op jit(solution)/shard_map/ppermute | solution.py:28
  19.2 2.2 %collective-permute-done.1.rest_2_ = f32[26,512]{1,0:T(8,128)S(1)} collective-permute-done((f32[26,512]{1,0:T(8,128)S(1)}, f32[26,512]{1,0:T(8,128)S(1)}, u32[]{:S(2)}, u32[]{:S(2)}) %collective-permute-start.1) | collective-permute-done | bytes 53280 | tf_op jit(solution)/shard_map/ppermute | solution.py:28
  21.4 1.7 %collective-permute-done.2.rest_3_ = f32[26,512]{1,0:T(8,128)S(1)} collective-permute-done((f32[26,512]{1,0:T(8,128)S(1)}, f32[26,512]{1,0:T(8,128)S(1)}, u32[]{:S(2)}, u32[]{:S(2)}) %collective-permute-start.2) | collective-permute-done | bytes 53280 | tf_op jit(solution)/shard_map/ppermute | solution.py:28
  23.7 3.3 %collective-permute-start.5 = (f32[26,512]{1,0:T(8,128)S(1)}, f32[26,512]{1,0:T(8,128)S(1)}, u32[]{:S(2)}, u32[]{:S(2)}) collective-permute-start(f32[26,512]{1,0:T(8,128)S(1)} %get-tuple-element.37.whole), channel_id=1, source_target_pairs={{0,24},{2,26},{4,28},{6,30},{1,25},{3,27},{5,29},{7,31}} | collective-permute-start | bytes 159752 | tf_op jit(solution)/shard_map/ppermute | solution.py:40
  28.3 2.5 %collective-permute-start.3 = (f32[26,512]{1,0:T(8,128)S(1)}, f32[26,512]{1,0:T(8,128)S(1)}, u32[]{:S(2)}, u32[]{:S(2)}) collective-permute-start(f32[26,512]{1,0:T(8,128)S(1)} %get-tuple-element.37.whole), channel_id=1, source_target_pairs={{0,8},{2,10},{4,12},{6,14},{8,16},{10,18},{12,20},{14,22},{16,24},... | collective-permute-start | bytes 159752 | tf_op jit(solution)/shard_map/ppermute | solution.py:40
  36.1 1.6 %collective-permute-start.6 = (f32[22,512]{1,0:T(8,128)S(1)}, f32[22,512]{1,0:T(8,128)S(1)}, u32[]{:S(2)}, u32[]{:S(2)}) collective-permute-start(f32[22,512]{1,0:T(8,128)S(1)} %get-tuple-element.43), channel_id=1, source_target_pairs={{0,2},{2,0},{4,6},{6,4},{8,10},{10,8},{12,14},{14,12},{16,18},{18,... | collective-permute-start | bytes 135176 | tf_op jit(solution)/shard_map/ppermute | solution.py:28
  42.1 2.1 %collective-permute-done.8.rest_3_ = f32[22,512]{1,0:T(8,128)S(1)} collective-permute-done((f32[22,512]{1,0:T(8,128)S(1)}, f32[22,512]{1,0:T(8,128)S(1)}, u32[]{:S(2)}, u32[]{:S(2)}) %collective-permute-start.8) | collective-permute-done | bytes 45088 | tf_op jit(solution)/shard_map/ppermute | solution.py:28
  44.2 3.6 %hidden_rows.2.refs_0_ = bf16[256,1024]{1,0:T(8,128)(2,1)S(1)} custom-call(s32[4]{0:T(128)S(1)} %pad_add_fusion.place, bf16[3,256,2048]{2,1,0:T(8,128)(2,1)S(1)} %bitcast.10, bf16[3,256,2048]{2,1,0:T(8,128)(2,1)S(1)} %bitcast.11, f32[3,3,2048]{2,1,0:T(4,128)S(1)} %copy-done.2, f32[16,2048]{1,0:T(8,128)S(1)} %bitcast.17, ...), custom_call_target="tpu_custom_call" | custom-call | flops 20971520 | bytes 2621440 | tf_op jit(solution)/shard_map/hidden_rows/pallas_call | solution.py:434
  48.9 3.6 %hidden_rows.3.refs_1_ = bf16[256,1024]{1,0:T(8,128)(2,1)S(1)} custom-call(s32[4]{0:T(128)S(1)} %pad_add_fusion.place, bf16[3,256,2048]{2,1,0:T(8,128)(2,1)S(1)} %bitcast.12, bf16[3,256,2048]{2,1,0:T(8,128)(2,1)S(1)} %bitcast.13, f32[3,3,2048]{2,1,0:T(4,128)S(1)} %copy-done.2, f32[16,2048]{1,0:T(8,128)S(1)} %bitcast.18, ...), custom_call_target="tpu_custom_call" | custom-call | flops 20971520 | bytes 2621440 | tf_op jit(solution)/shard_map/hidden_rows/pallas_call | solution.py:434
  52.6 1.6 %collective-permute-start.12 = (bf16[256,1024]{1,0:T(8,128)(2,1)S(1)}, bf16[256,1024]{1,0:T(8,128)(2,1)S(1)}, u32[]{:S(2)}, u32[]{:S(2)}) collective-permute-start(bf16[256,1024]{1,0:T(8,128)(2,1)S(1)} %hidden_rows.3.refs_1_), channel_id=1, source_target_pairs={{0,4},{2,6},{4,0},{6,2},{8,12},{10,14},{12,8},{14,10},{16,20},{18,... | collective-permute-start | bytes 1572872 | tf_op jit(solution)/shard_map/ppermute | solution.py:28
  54.1 8.6 %collective-permute-done.11.refs_4_ = bf16[256,1024]{1,0:T(8,128)(2,1)S(1)} collective-permute-done((bf16[256,1024]{1,0:T(8,128)(2,1)S(1)}, bf16[256,1024]{1,0:T(8,128)(2,1)S(1)}, u32[]{:S(2)}, u32[]{:S(2)}) %collective-permute-start.11) | collective-permute-done | bytes 524320 | tf_op jit(solution)/shard_map/ppermute | solution.py:28
  66.6 7.4 %collective-permute-done.12.refs_5_ = bf16[256,1024]{1,0:T(8,128)(2,1)S(1)} collective-permute-done((bf16[256,1024]{1,0:T(8,128)(2,1)S(1)}, bf16[256,1024]{1,0:T(8,128)(2,1)S(1)}, u32[]{:S(2)}, u32[]{:S(2)}) %collective-permute-start.12) | collective-permute-done | bytes 524320 | tf_op jit(solution)/shard_map/ppermute | solution.py:28
  74.5 3.9 %collective-permute-done.10.refs_3_ = bf16[256,1024]{1,0:T(8,128)(2,1)S(1)} collective-permute-done((bf16[256,1024]{1,0:T(8,128)(2,1)S(1)}, bf16[256,1024]{1,0:T(8,128)(2,1)S(1)}, u32[]{:S(2)}, u32[]{:S(2)}) %collective-permute-start.10) | collective-permute-done | bytes 524320 | tf_op jit(solution)/shard_map/ppermute | solution.py:28
  78.4 3.9 %project.2 = (bf16[768,512]{1,0:T(8,128)(2,1)S(1)}, bf16[768,256]{1,0:T(8,128)(2,1)S(1)}) custom-call(s32[4]{0:T(128)S(1)} %pad_add_fusion.place, bf16[256,1024]{1,0:T(8,128)(2,1)S(1)} %hidden_rows.2.refs_0_, bf16[256,1024]{1,0:T(8,128)(2,1)S(1)} %hidden_rows.3.refs_1_, bf16[256,1024]{1,0:T(8,128)(2,1)S(1)} %collective-permute-done.9.refs_2_, ...), custom_call_target="tpu_custom_call" | custom-call | flops 2415919104 | bytes 7471104 | tf_op jit(solution)/shard_map/project/pallas_call | solution.py:533
  82.3 3.0 %collective-permute-done.14.refs_7_ = bf16[256,1024]{1,0:T(8,128)(2,1)S(1)} collective-permute-done((bf16[256,1024]{1,0:T(8,128)(2,1)S(1)}, bf16[256,1024]{1,0:T(8,128)(2,1)S(1)}, u32[]{:S(2)}, u32[]{:S(2)}) %collective-permute-start.14) | collective-permute-done | bytes 524320 | tf_op jit(solution)/shard_map/ppermute | solution.py:28
  85.8 3.9 %project.3 = (bf16[1024,512]{1,0:T(8,128)(2,1)S(1)}, bf16[1024,512]{1,0:T(8,128)(2,1)S(1)}) custom-call(s32[4]{0:T(128)S(1)} %pad_add_fusion.place, bf16[256,1024]{1,0:T(8,128)(2,1)S(1)} %hidden_rows.2.refs_0_, bf16[256,1024]{1,0:T(8,128)(2,1)S(1)} %hidden_rows.3.refs_1_, bf16[256,1024]{1,0:T(8,128)(2,1)S(1)} %collective-permute-done.9.refs_2_, ...), custom_call_target="tpu_custom_call" | custom-call | flops 4294967296 | bytes 10485760 | tf_op jit(solution)/shard_map/project/pallas_call | solution.py:533
  89.8 2.6 %collective-permute-done.20.b = bf16[1024,512]{1,0:T(8,128)(2,1)S(1)} collective-permute-done((bf16[1024,512]{1,0:T(8,128)(2,1)S(1)}, bf16[1024,512]{1,0:T(8,128)(2,1)S(1)}, u32[]{:S(2)}, u32[]{:S(2)}) %collective-permute-start.20) | collective-permute-done | bytes 1048608 | tf_op jit(solution)/shard_map/ppermute | solution.py:635
  92.7 1.6 %collective-permute-start.21 = (bf16[256,512]{1,0:T(8,128)(2,1)S(1)}, bf16[256,512]{1,0:T(8,128)(2,1)S(1)}, u32[]{:S(2)}, u32[]{:S(2)}) collective-permute-start(bf16[256,512]{1,0:T(8,128)(2,1)S(1)} %get-tuple-element.54), channel_id=1, source_target_pairs={{0,2},{2,0},{4,6},{6,4},{8,10},{10,8},{12,14},{14,12},{16,18},{18,... | collective-permute-start | bytes 786440 | tf_op jit(solution)/shard_map/ppermute | solution.py:28
  96.3 5.7 %collective-permute-done.21.refs_1_ = bf16[256,512]{1,0:T(8,128)(2,1)S(1)} collective-permute-done((bf16[256,512]{1,0:T(8,128)(2,1)S(1)}, bf16[256,512]{1,0:T(8,128)(2,1)S(1)}, u32[]{:S(2)}, u32[]{:S(2)}) %collective-permute-start.21) | collective-permute-done | bytes 262176 | tf_op jit(solution)/shard_map/ppermute | solution.py:28
  101.9 6.0 %collective-permute-done.22.refs_2_ = bf16[256,512]{1,0:T(8,128)(2,1)S(1)} collective-permute-done((bf16[256,512]{1,0:T(8,128)(2,1)S(1)}, bf16[256,512]{1,0:T(8,128)(2,1)S(1)}, u32[]{:S(2)}, u32[]{:S(2)}) %collective-permute-start.22) | collective-permute-done | bytes 262176 | tf_op jit(solution)/shard_map/ppermute | solution.py:28
  108.0 1.7 %assemble.1 = bf16[256,2048]{1,0:T(8,128)(2,1)} custom-call(s32[4]{0:T(128)S(1)} %pad_add_fusion.place, bf16[256,512]{1,0:T(8,128)(2,1)S(1)} %get-tuple-element.53.refs_0_, bf16[256,512]{1,0:T(8,128)(2,1)S(1)} %collective-permute-done.21.refs_1_, bf16[256,512]{1,0:T(8,128)(2,1)S(1)} %collective-permute-done.22.refs_2_, ...), custom_call_target="tpu_custom_call" | custom-call | bytes 2097152 | tf_op jit(solution)/shard_map/assemble/pallas_call | solution.py:565
  (47 shorter events, 24.6 us)
Async XLA Ops:
  0.0 34.1 %collective-permute-start.16 = (bf16[2048,256]{1,0:T(8,128)(2,1)}, bf16[2048,256]{1,0:T(8,128)(2,1)}, u32[]{:S(2)}, u32[]{:S(2)}) collective-permute-start(bf16[2048,256]{1,0:T(8,128)(2,1)} %refs_8_.1), channel_id=1, source_target_pairs={{8,16},{10,18},{12,20},{14,22},{16,8},{18,10},{20,12},{22,14},{9,1... | collective-permute-start | bytes 3145736 | tf_op jit(solution)/shard_map/ppermute | solution.py:582
  1.8 32.3 %collective-permute-start.15 = (bf16[2048,256]{1,0:T(8,128)(2,1)}, bf16[2048,256]{1,0:T(8,128)(2,1)}, u32[]{:S(2)}, u32[]{:S(2)}) collective-permute-start(bf16[2048,256]{1,0:T(8,128)(2,1)} %refs_8_.1), channel_id=1, source_target_pairs={{0,8},{2,10},{4,12},{6,14},{8,0},{10,2},{12,4},{14,6},{16,24},{18,... | collective-permute-start | bytes 3145736 | tf_op jit(solution)/shard_map/ppermute | solution.py:582
  14.8 4.3 %collective-permute-start = (f32[26,512]{1,0:T(8,128)S(1)}, f32[26,512]{1,0:T(8,128)S(1)}, u32[]{:S(2)}, u32[]{:S(2)}) collective-permute-start(f32[26,512]{1,0:T(8,128)S(1)} %get-tuple-element.34), channel_id=1, source_target_pairs={{0,2},{2,0},{4,6},{6,4},{8,10},{10,8},{12,14},{14,12},{16,18},{18,... | collective-permute-start | bytes 159752 | tf_op jit(solution)/shard_map/ppermute | solution.py:28
  16.4 5.0 %collective-permute-start.1 = (f32[26,512]{1,0:T(8,128)S(1)}, f32[26,512]{1,0:T(8,128)S(1)}, u32[]{:S(2)}, u32[]{:S(2)}) collective-permute-start(f32[26,512]{1,0:T(8,128)S(1)} %get-tuple-element.35), channel_id=1, source_target_pairs={{0,4},{2,6},{4,0},{6,2},{8,12},{10,14},{12,8},{14,10},{16,20},{18,... | collective-permute-start | bytes 159752 | tf_op jit(solution)/shard_map/ppermute | solution.py:28
  17.9 5.2 %collective-permute-start.2 = (f32[26,512]{1,0:T(8,128)S(1)}, f32[26,512]{1,0:T(8,128)S(1)}, u32[]{:S(2)}, u32[]{:S(2)}) collective-permute-start(f32[26,512]{1,0:T(8,128)S(1)} %get-tuple-element.36), channel_id=1, source_target_pairs={{0,6},{2,4},{4,2},{6,0},{8,14},{10,12},{12,10},{14,8},{16,22},{18,... | collective-permute-start | bytes 159752 | tf_op jit(solution)/shard_map/ppermute | solution.py:28
  23.7 8.3 %collective-permute-start.5 = (f32[26,512]{1,0:T(8,128)S(1)}, f32[26,512]{1,0:T(8,128)S(1)}, u32[]{:S(2)}, u32[]{:S(2)}) collective-permute-start(f32[26,512]{1,0:T(8,128)S(1)} %get-tuple-element.37.whole), channel_id=1, source_target_pairs={{0,24},{2,26},{4,28},{6,30},{1,25},{3,27},{5,29},{7,31}} | collective-permute-start | bytes 159752 | tf_op jit(solution)/shard_map/ppermute | solution.py:40
  27.0 5.7 %collective-permute-start.4 = (f32[26,512]{1,0:T(8,128)S(1)}, f32[26,512]{1,0:T(8,128)S(1)}, u32[]{:S(2)}, u32[]{:S(2)}) collective-permute-start(f32[26,512]{1,0:T(8,128)S(1)} %get-tuple-element.37.whole), channel_id=1, source_target_pairs={{0,16},{2,18},{4,20},{6,22},{8,24},{10,26},{12,28},{14,30},{1,17},... | collective-permute-start | bytes 159752 | tf_op jit(solution)/shard_map/ppermute | solution.py:40
  28.3 5.1 %collective-permute-start.3 = (f32[26,512]{1,0:T(8,128)S(1)}, f32[26,512]{1,0:T(8,128)S(1)}, u32[]{:S(2)}, u32[]{:S(2)}) collective-permute-start(f32[26,512]{1,0:T(8,128)S(1)} %get-tuple-element.37.whole), channel_id=1, source_target_pairs={{0,8},{2,10},{4,12},{6,14},{8,16},{10,18},{12,20},{14,22},{16,24},... | collective-permute-start | bytes 159752 | tf_op jit(solution)/shard_map/ppermute | solution.py:40
  34.1 28.7 %collective-permute-start.17 = (bf16[2048,256]{1,0:T(8,128)(2,1)}, bf16[2048,256]{1,0:T(8,128)(2,1)S(1)}, u32[]{:S(2)}, u32[]{:S(2)}) collective-permute-start(bf16[2048,256]{1,0:T(8,128)(2,1)} %collective-permute-done.15.refs_7_.refs_9_), channel_id=1, source_target_pairs={{8,16},{10,18},{12,20},{14,22},{16,8},{18,10},{20,12},{22,14},{9,1... | collective-permute-start | bytes 3145736 | tf_op jit(solution)/shard_map/ppermute | solution.py:582
  34.8 27.9 %collective-permute-start.18 = (bf16[2048,256]{1,0:T(8,128)(2,1)}, bf16[2048,256]{1,0:T(8,128)(2,1)S(1)}, u32[]{:S(2)}, u32[]{:S(2)}) collective-permute-start(bf16[2048,256]{1,0:T(8,128)(2,1)} %collective-permute-done.16.refs_12_), channel_id=1, source_target_pairs={{8,0},{10,2},{12,4},{14,6},{16,24},{18,26},{20,28},{22,30},{9,1},{... | collective-permute-start | bytes 3145736 | tf_op jit(solution)/shard_map/ppermute | solution.py:582
  36.1 4.6 %collective-permute-start.6 = (f32[22,512]{1,0:T(8,128)S(1)}, f32[22,512]{1,0:T(8,128)S(1)}, u32[]{:S(2)}, u32[]{:S(2)}) collective-permute-start(f32[22,512]{1,0:T(8,128)S(1)} %get-tuple-element.43), channel_id=1, source_target_pairs={{0,2},{2,0},{4,6},{6,4},{8,10},{10,8},{12,14},{14,12},{16,18},{18,... | collective-permute-start | bytes 135176 | tf_op jit(solution)/shard_map/ppermute | solution.py:28
  37.7 4.4 %collective-permute-start.7 = (f32[22,512]{1,0:T(8,128)S(1)}, f32[22,512]{1,0:T(8,128)S(1)}, u32[]{:S(2)}, u32[]{:S(2)}) collective-permute-start(f32[22,512]{1,0:T(8,128)S(1)} %get-tuple-element.44), channel_id=1, source_target_pairs={{0,4},{2,6},{4,0},{6,2},{8,12},{10,14},{12,8},{14,10},{16,20},{18,... | collective-permute-start | bytes 135176 | tf_op jit(solution)/shard_map/ppermute | solution.py:28
  39.2 5.0 %collective-permute-start.8 = (f32[22,512]{1,0:T(8,128)S(1)}, f32[22,512]{1,0:T(8,128)S(1)}, u32[]{:S(2)}, u32[]{:S(2)}) collective-permute-start(f32[22,512]{1,0:T(8,128)S(1)} %get-tuple-element.45), channel_id=1, source_target_pairs={{0,6},{2,4},{4,2},{6,0},{8,14},{10,12},{12,10},{14,8},{16,22},{18,... | collective-permute-start | bytes 135176 | tf_op jit(solution)/shard_map/ppermute | solution.py:28
  47.8 14.9 %collective-permute-start.11 = (bf16[256,1024]{1,0:T(8,128)(2,1)S(1)}, bf16[256,1024]{1,0:T(8,128)(2,1)S(1)}, u32[]{:S(2)}, u32[]{:S(2)}) collective-permute-start(bf16[256,1024]{1,0:T(8,128)(2,1)S(1)} %hidden_rows.2.refs_0_), channel_id=1, source_target_pairs={{0,4},{2,6},{4,0},{6,2},{8,12},{10,14},{12,8},{14,10},{16,20},{18,... | collective-permute-start | bytes 1572872 | tf_op jit(solution)/shard_map/ppermute | solution.py:28
  48.4 14.4 %collective-permute-start.9 = (bf16[256,1024]{1,0:T(8,128)(2,1)S(1)}, bf16[256,1024]{1,0:T(8,128)(2,1)S(1)}, u32[]{:S(2)}, u32[]{:S(2)}) collective-permute-start(bf16[256,1024]{1,0:T(8,128)(2,1)S(1)} %hidden_rows.2.refs_0_), channel_id=1, source_target_pairs={{0,2},{2,0},{4,6},{6,4},{8,10},{10,8},{12,14},{14,12},{16,18},{18,... | collective-permute-start | bytes 1572872 | tf_op jit(solution)/shard_map/ppermute | solution.py:28
  52.6 21.4 %collective-permute-start.12 = (bf16[256,1024]{1,0:T(8,128)(2,1)S(1)}, bf16[256,1024]{1,0:T(8,128)(2,1)S(1)}, u32[]{:S(2)}, u32[]{:S(2)}) collective-permute-start(bf16[256,1024]{1,0:T(8,128)(2,1)S(1)} %hidden_rows.3.refs_1_), channel_id=1, source_target_pairs={{0,4},{2,6},{4,0},{6,2},{8,12},{10,14},{12,8},{14,10},{16,20},{18,... | collective-permute-start | bytes 1572872 | tf_op jit(solution)/shard_map/ppermute | solution.py:28
  62.8 23.0 %collective-permute-start.19 = (bf16[2048,256]{1,0:T(8,128)(2,1)S(1)}, bf16[2048,256]{1,0:T(8,128)(2,1)S(1)}, u32[]{:S(2)}, u32[]{:S(2)}) collective-permute-start(bf16[2048,256]{1,0:T(8,128)(2,1)S(1)} %collective-permute-done.17.refs_8_.refs_10_), channel_id=1, source_target_pairs={{8,0},{10,2},{12,4},{14,6},{16,24},{18,26},{20,28},{22,30},{9,1},{... | collective-permute-start | bytes 3145736 | tf_op jit(solution)/shard_map/ppermute | solution.py:582
  64.1 14.3 %collective-permute-start.10 = (bf16[256,1024]{1,0:T(8,128)(2,1)S(1)}, bf16[256,1024]{1,0:T(8,128)(2,1)S(1)}, u32[]{:S(2)}, u32[]{:S(2)}) collective-permute-start(bf16[256,1024]{1,0:T(8,128)(2,1)S(1)} %hidden_rows.3.refs_1_), channel_id=1, source_target_pairs={{0,2},{2,0},{4,6},{6,4},{8,10},{10,8},{12,14},{14,12},{16,18},{18,... | collective-permute-start | bytes 1572872 | tf_op jit(solution)/shard_map/ppermute | solution.py:28
  65.0 17.3 %collective-permute-start.13 = (bf16[256,1024]{1,0:T(8,128)(2,1)S(1)}, bf16[256,1024]{1,0:T(8,128)(2,1)S(1)}, u32[]{:S(2)}, u32[]{:S(2)}) collective-permute-start(bf16[256,1024]{1,0:T(8,128)(2,1)S(1)} %collective-permute-done.9.refs_2_), channel_id=1, source_target_pairs={{0,4},{2,6},{4,0},{6,2},{8,12},{10,14},{12,8},{14,10},{16,20},{18,... | collective-permute-start | bytes 1572872 | tf_op jit(solution)/shard_map/ppermute | solution.py:28
  74.0 11.3 %collective-permute-start.14 = (bf16[256,1024]{1,0:T(8,128)(2,1)S(1)}, bf16[256,1024]{1,0:T(8,128)(2,1)S(1)}, u32[]{:S(2)}, u32[]{:S(2)}) collective-permute-start(bf16[256,1024]{1,0:T(8,128)(2,1)S(1)} %collective-permute-done.12.refs_5_), channel_id=1, source_target_pairs={{0,2},{2,0},{4,6},{6,4},{8,10},{10,8},{12,14},{14,12},{16,18},{18,... | collective-permute-start | bytes 1572872 | tf_op jit(solution)/shard_map/ppermute | solution.py:28
  89.7 2.7 %collective-permute-start.20 = (bf16[1024,512]{1,0:T(8,128)(2,1)S(1)}, bf16[1024,512]{1,0:T(8,128)(2,1)S(1)}, u32[]{:S(2)}, u32[]{:S(2)}) collective-permute-start(bf16[1024,512]{1,0:T(8,128)(2,1)S(1)} %get-tuple-element.52), channel_id=1, source_target_pairs={{0,1},{1,0},{2,3},{3,2},{4,5},{5,4},{6,7},{7,6},{8,9},{9,8},{10,11... | collective-permute-start | bytes 3145736 | tf_op jit(solution)/shard_map/ppermute | solution.py:635
  92.7 9.2 %collective-permute-start.21 = (bf16[256,512]{1,0:T(8,128)(2,1)S(1)}, bf16[256,512]{1,0:T(8,128)(2,1)S(1)}, u32[]{:S(2)}, u32[]{:S(2)}) collective-permute-start(bf16[256,512]{1,0:T(8,128)(2,1)S(1)} %get-tuple-element.54), channel_id=1, source_target_pairs={{0,2},{2,0},{4,6},{6,4},{8,10},{10,8},{12,14},{14,12},{16,18},{18,... | collective-permute-start | bytes 786440 | tf_op jit(solution)/shard_map/ppermute | solution.py:28
  94.3 13.7 %collective-permute-start.22 = (bf16[256,512]{1,0:T(8,128)(2,1)S(1)}, bf16[256,512]{1,0:T(8,128)(2,1)S(1)}, u32[]{:S(2)}, u32[]{:S(2)}) collective-permute-start(bf16[256,512]{1,0:T(8,128)(2,1)S(1)} %get-tuple-element.55), channel_id=1, source_target_pairs={{0,4},{2,6},{4,0},{6,2},{8,12},{10,14},{12,8},{14,10},{16,20},{18,... | collective-permute-start | bytes 786440 | tf_op jit(solution)/shard_map/ppermute | solution.py:28
  95.8 12.2 %collective-permute-start.23 = (bf16[256,512]{1,0:T(8,128)(2,1)S(1)}, bf16[256,512]{1,0:T(8,128)(2,1)S(1)}, u32[]{:S(2)}, u32[]{:S(2)}) collective-permute-start(bf16[256,512]{1,0:T(8,128)(2,1)S(1)} %get-tuple-element.56), channel_id=1, source_target_pairs={{0,6},{2,4},{4,2},{6,0},{8,14},{10,12},{12,10},{14,8},{16,22},{18,... | collective-permute-start | bytes 786440 | tf_op jit(solution)/shard_map/ppermute | solution.py:28
  (6 other events, 143.1 us)
